TPU v7x, 128 devices: a whole 4x4x4 slice. The times are simulated.
128 devices in a mesh: dp: 8 (over y, core), ctx: 16 (over x, z).
Axes of the slice: x: 4, y: 4, z: 4, core: 2. Of those that a mesh axis runs over, the one named last changes fastest.
Arguments:
- queries: bfloat16 [8, 4096, 2048], P('dp', 'ctx'), may hold values from -6 to 6
- keys: bfloat16 [8, 4096, 2048], P('dp', 'ctx'), may hold values from -6 to 6
- values: bfloat16 [8, 4096, 2048], P('dp', 'ctx'), may hold values from -6 to 6
- out_weight: bfloat16 [2048, 2048], replicated, may hold values from -0.125 to 0.125
- grad_out: bfloat16 [8, 4096, 2048], P('dp', 'ctx'), may hold values from -6 to 6
- tile_docs: int32 [8, 32], P('dp', 'ctx'), may hold values from 0 to 9, never falling along the last dimension, each value on 1 to 8 neighbouring positions
Outputs:
- layer_out: bfloat16 [8, 4096, 2048], P('dp', 'ctx')
- grad_queries: bfloat16 [8, 4096, 2048], P('dp', 'ctx')
- grad_keys: bfloat16 [8, 4096, 2048], P('dp', 'ctx')
- grad_values: bfloat16 [8, 4096, 2048], P('dp', 'ctx')
- grad_weight: float32 [2048, 2048], P('dp', 'ctx')
Inputs may be any that keep to these rules, and one draw needn't show every extreme that they name: `tile_docs`: along each sequence the document number never falls from tile to tile; every document covers 1 to 8 tiles, and one document of every sequence covers exactly 8.
All inputs are finite; a program needn't handle non-finite values.
Results may differ from a plain program's by a relative error of at most 0.0058.
Values sent between devices are 32-bit elements; how exact they have to be, the bound alone decides.
No kernel may reach another device: no remote copies, remote signals or barrier semaphores. Data moves between devices by JAX's collectives and lax.ppermute only.
A program may use at most 128 MiB of HBM per device.

v0:
```python
import jax
import jax.numpy as jnp
from jax import lax
from jax.sharding import PartitionSpec as P

HEADS = 16
HDIM = 128
TILE = 128


def prefix(part, axis, combine, identity, reverse):
    count = lax.axis_size(axis)
    place = lax.axis_index(axis)
    ahead = count - 1 - place if reverse else place
    gathered = jax.tree.map(lambda a: lax.all_gather(a, axis), part)
    state = jax.tree.map(lambda a, e: jnp.zeros_like(a) + jnp.asarray(e, a.dtype), part, identity)

    def one(turn, state):
        source = count - 1 - turn if reverse else turn
        return combine(
            state, jax.tree.map(lambda a: lax.dynamic_index_in_dim(a, source, 0, False), gathered)
        )

    return lax.fori_loop(0, ahead, one, state)


def join_forward(earlier, later):
    a_state, a_ends = earlier
    b_state, b_ends = later
    a_empty = a_ends[0] < 0.0
    b_empty = b_ends[0] < 0.0
    first = jnp.where(a_empty, b_ends[0], a_ends[0])
    last = jnp.where(b_empty, a_ends[1], b_ends[1])
    linked = (b_ends[0] == b_ends[1]) & (b_ends[0] == a_ends[1])
    state = jnp.where(b_empty, a_state, b_state + jnp.where(linked, a_state, 0.0))
    return (state, jnp.stack([first, last]))


def join_backward(earlier, later):
    a_state, a_ends = earlier
    b_state, b_ends = later
    a_empty = a_ends[0] < 0.0
    b_empty = b_ends[0] < 0.0
    first = jnp.where(b_empty, a_ends[0], b_ends[0])
    last = jnp.where(a_empty, b_ends[1], a_ends[1])
    linked = (b_ends[0] == b_ends[1]) & (b_ends[1] == a_ends[0])
    state = jnp.where(b_empty, a_state, b_state + jnp.where(linked, a_state, 0.0))
    return (state, jnp.stack([first, last]))


def body(queries, keys, values, out_weight, grad_out, tile_docs):
    tokens = queries.shape[1]
    tiles = tokens // TILE
    scale = 1.0 / HDIM
    highest = lax.Precision.HIGHEST
    f32 = jnp.float32
    bf16 = jnp.bfloat16

    def split(x):
        return x.reshape(tiles, TILE, HEADS, HDIM)

    q = split(queries)
    k = split(keys)
    v = split(values)
    ids = tile_docs[0]
    id_float = ids.astype(f32)
    rows = lax.broadcasted_iota(jnp.int32, (TILE, TILE), 0)
    cols = lax.broadcasted_iota(jnp.int32, (TILE, TILE), 1)
    causal = rows >= cols
    scores = jnp.einsum("ntha,nsha->nhts", q, k, preferred_element_type=f32)
    attn_q = (scale * jnp.where(causal, scores, 0.0)).astype(bf16)
    kv = jnp.einsum("ntha,nthc->nhac", k, v, preferred_element_type=f32)
    order_tile = lax.broadcasted_iota(jnp.int32, (tiles,), 0)
    same_doc = ids[:, None] == ids[None, :]
    before = (same_doc & (order_tile[:, None] > order_tile[None, :])).astype(f32)
    after = (same_doc & (order_tile[:, None] < order_tile[None, :])).astype(f32)
    last_mask = (ids == ids[tiles - 1]).astype(f32)
    first_mask = (ids == ids[0]).astype(f32)
    ends = jnp.stack([id_float[0], id_float[tiles - 1]])
    trailing = jnp.einsum("i,ihac->hac", last_mask, kv, precision=highest)
    blank = (jnp.zeros_like(trailing), jnp.full((2,), -1.0, f32))
    prior_state, prior_ends = prefix((trailing, ends), "ctx", join_forward, blank, False)
    take_prior = (id_float == prior_ends[1]).astype(f32)
    state = jnp.einsum("ji,ihac->jhac", before, kv, precision=highest)
    state = state + take_prior[:, None, None, None] * prior_state[None]
    state_b = (scale * state).astype(bf16)
    out_tiles = jnp.einsum("nhts,nshc->nthc", attn_q, v, preferred_element_type=f32)
    out_tiles = out_tiles + jnp.einsum("ntha,nhac->nthc", q, state_b, preferred_element_type=f32)
    attended = out_tiles.astype(bf16).reshape(tokens, HEADS * HDIM)
    layer_out = jnp.dot(attended, out_weight, preferred_element_type=f32).astype(bf16)
    upstream = grad_out[0]
    grad_att = lax.dot_general(
        upstream, out_weight, (((1,), (1,)), ((), ())), preferred_element_type=f32
    ).astype(bf16)
    g = split(grad_att)
    qg = jnp.einsum("ntha,nthc->nhca", q, g, preferred_element_type=f32)
    leading = jnp.einsum("i,ihca->hca", first_mask, qg, precision=highest)
    later_state, later_ends = prefix((leading, ends), "ctx", join_backward, blank, True)
    take_later = (id_float == later_ends[0]).astype(f32)
    rev = jnp.einsum("ji,ihca->jhca", after, qg, precision=highest)
    rev = rev + take_later[:, None, None, None] * later_state[None]
    rev_b = (scale * rev).astype(bf16)
    attn_g = jnp.einsum("nthc,nshc->nhts", g, v, preferred_element_type=f32)
    attn_g = (scale * jnp.where(causal, attn_g, 0.0)).astype(bf16)
    grad_q = jnp.einsum("nhts,nsha->ntha", attn_g, k, preferred_element_type=f32)
    grad_q = grad_q + jnp.einsum("nthc,nhac->ntha", g, state_b, preferred_element_type=f32)
    grad_k = jnp.einsum("nhts,ntha->nsha", attn_g, q, preferred_element_type=f32)
    grad_k = grad_k + jnp.einsum("nshc,nhca->nsha", v, rev_b, preferred_element_type=f32)
    grad_v = jnp.einsum("nhts,nthc->nshc", attn_q, g, preferred_element_type=f32)
    grad_v = grad_v + jnp.einsum("nsha,nhca->nshc", k, rev_b, preferred_element_type=f32)

    def shaped(x):
        return x.astype(bf16).reshape(1, tokens, HEADS * HDIM)

    total_tokens = tokens * lax.axis_size("dp") * lax.axis_size("ctx")
    factor = 1.0 / float(total_tokens) ** 0.5
    by_feature = lax.psum_scatter(
        lax.dot_general(upstream, attended, (((0,), (0,)), ((), ())), preferred_element_type=f32),
        "ctx",
        scatter_dimension=0,
        tiled=True,
    )
    reduced = lax.psum_scatter(by_feature, "dp", scatter_dimension=1, tiled=True)
    grad_weight = jnp.transpose(reduced) * factor
    return (layer_out[None], shaped(grad_q), shaped(grad_k), shaped(grad_v), grad_weight)


def solution(mesh):
    in_specs = (
        P("dp", "ctx", None),
        P("dp", "ctx", None),
        P("dp", "ctx", None),
        P(),
        P("dp", "ctx", None),
        P("dp", "ctx"),
    )
    out_specs = (
        P("dp", "ctx", None),
        P("dp", "ctx", None),
        P("dp", "ctx", None),
        P("dp", "ctx", None),
        P("dp", "ctx"),
    )
    return jax.shard_map(body, mesh=mesh, in_specs=in_specs, out_specs=out_specs, check_vma=False)
```

profile of v0, /device:TPU:0, one launch (start us, length us, event | category | flops | bytes accessed | tf_op | source)
XLA Modules:
  0.0 560.4 jit_solution(14957972430727258968)
XLA Ops:
  7.2 1.2 copy-done
  8.4 5.7 %fusion.19 = bf16[32,8,16,128]{3,1,2,0:T(8,128)(2,1)S(1)} fusion(bf16[2048,2048]{1,0:T(8,128)(2,1)} %param.13, bf16[1,256,2048]{2,1,0:T(8,128)(2,1)S(1)} %copy-done), kind=kOutput, calls=%fused_computation.36 | convolution fusion | flops 2148007936 | bytes 10485760 | tf_op jit(solution)/shard_map/dot_general | solution.py:92
  14.4 1.0 copy.89
  15.4 1.8 copy.112
  17.3 0.7 fusion.65
  18.4 1.3 copy-done.16
  19.8 6.1 %fusion.10 = f32[1,16,128,128]{3,0,2,1:T(1,128)} fusion(f32[2,16,128,128]{3,2,1,0:T(8,128)S(1)} %fusion.37, s32[]{:T(128)} %bitcast.35, s32[1,2]{1,0:T(1,128)S(1)} %copy-done.27), kind=kOutput, calls=%fused_computation.27 | convolution fusion | flops 6291458 | bytes 3145740 | tf_op jit(solution)/shard_map/i,ihca->hca/dot_general | solution.py:97
  26.0 1.5 copy.113
  27.4 1.8 copy.114
  30.2 1.3 copy-done.18
  31.5 6.0 %fusion.14 = f32[1,16,128,128]{3,0,2,1:T(1,128)} fusion(f32[2,16,128,128]{3,2,1,0:T(8,128)S(1)} %fusion.28, s32[]{:T(128)} %bitcast.20, s32[1,2]{1,0:T(1,128)S(1)} %copy-done.27), kind=kOutput, calls=%fused_computation.31 | convolution fusion | flops 6291458 | bytes 3145740 | tf_op jit(solution)/shard_map/i,ihac->hac/dot_general | solution.py:80
  37.7 22.2 %all-gather.2 = f32[16,1,2]{2,1,0:T(1,128)S(1)} all-gather(f32[1,1,2]{2,1,0:T(1,128)S(1)} %convert_bitcast_fusion), channel_id=1, replica_groups=mesh['dp'=8,'ctx'=16] {'ctx'}, dimensions={0}, use_global_device_ids=true | all-gather | bytes 136 | tf_op jit(solution)/shard_map/all_gather | solution.py:15
  60.0 0.8 multiply_convert_fusion.1
  61.2 1.8 fusion.30
  63.0 0.9 copy-done.17
  63.9 5.7 %fusion.12 = f32[2,16,128,128]{3,0,2,1:T(2,128)} fusion(f32[2,16,128,128]{3,2,1,0:T(8,128)S(1)} %copy-done.17, s32[2]{0:T(128)S(1)} %bitcast.191), kind=kOutput, calls=%fused_computation.29 | convolution fusion | flops 12582924 | bytes 4194312 | tf_op jit(solution)/shard_map/ji,ihca->jhca/dot_general | solution.py:100
  69.6 5.7 %fusion.16 = f32[2,16,128,128]{3,0,2,1:T(2,128)} fusion(f32[2,16,128,128]{3,2,1,0:T(8,128)S(1)} %copy-done.19, s32[2]{0:T(128)S(1)} %bitcast.192), kind=kOutput, calls=%fused_computation.33 | convolution fusion | flops 12582924 | bytes 4194312 | tf_op jit(solution)/shard_map/ji,ihac->jhac/dot_general | solution.py:84
  75.3 64.7 %all-gather.8.cloned.1.call-done = f32[256,128,128]{2,1,0:T(8,128)} async-done(((f32[16,128,128]{2,1,0:T(8,128)}), f32[256,128,128]{2,1,0:T(8,128)}) %all-gather.8.cloned.1.call-update) | async-done | bytes 16777232 | tf_op jit(solution)/shard_map/all_gather | solution.py:15
  140.1 137.9 %while.27 = (s32[]{:T(128)}, f32[16,128,128]{2,1,0:T(8,128)S(1)}, f32[2]{0:T(128)S(1)}, s32[]{:T(128)}, f32[16,2]{0,1:T(2,128)S(1)}, /*index=5*/f32[16,16,128,12...) while((s32[]{:T(128)}, f32[16,128,128]{2,1,0:T(8,128)S(1)}, ...), condition=%wide.region_3.4_spmd, body=%wide.region_2.3_spmd.sunk | while | flops 786447 | bytes 3146022 | solution.py:24
  144.6 1.6 fusion.92
  149.4 0.6 fusion.90
  153.8 1.8 fusion.92
  163.2 1.6 fusion.92
  172.4 1.6 fusion.92
  177.1 0.6 fusion.90
  181.5 1.6 fusion.92
  186.3 0.6 fusion.90
  190.7 1.6 fusion.92
  195.5 0.6 fusion.90
  199.9 1.6 fusion.92
  204.7 0.6 fusion.90
  209.1 1.6 fusion.92
  218.3 1.6 fusion.92
  223.1 0.6 fusion.90
  227.5 1.6 fusion.92
  232.3 0.6 fusion.90
  236.7 1.6 fusion.92
  245.9 1.6 fusion.92
  250.6 0.6 fusion.90
  255.0 1.6 fusion.92
  264.2 1.6 fusion.92
  273.4 1.6 fusion.92
  278.7 0.7 compare_convert_fusion
  279.5 4.0 fusion.7
  284.4 0.7 copy.80
  285.1 1.0 copy-done.22
  286.1 8.2 %convolution_bitcast_fusion = f32[2048,2048]{0,1:T(8,128)} fusion(bf16[1,256,2048]{2,1,0:T(8,128)(2,1)S(1)} %copy-done, bf16[32,8,16,128]{3,2,1,0:T(8,128)(2,1)S(1)} %bitcast.179), kind=kOutput, calls=%fused_computation.8 | convolution fusion | flops 2147483648 | bytes 18874368 | tf_op jit(solution)/shard_map/dot_general | solution.py:118
  294.6 0.9 copy-done.3
  295.8 0.9 multiply_convert_fusion
  296.7 1.8 fusion.66
  298.7 1.9 fusion.39
  300.6 218.2 %reduce-scatter.3.cloned.1.call-done = f32[128,2048]{0,1:T(8,128)} async-done(((f32[2048,2048]{0,1:T(8,128)}), f32[128,2048]{0,1:T(8,128)}) %reduce-scatter.3.cloned.1.call-update) | async-done | bytes 1048592 | tf_op jit(solution)/shard_map/reduce_scatter | solution.py:117
  518.8 3.2 fusion.34
  522.5 1.6 copy.96
  524.2 2.3 reshape.67
  526.5 3.4 fusion.18
  529.9 2.0 copy.99
  531.9 1.3 reshape.68
  533.2 2.5 fusion.4
  535.7 0.7 copy.86
  536.4 1.3 reshape.66
  537.6 6.8 %fusion.2 = bf16[1,256,2048]{2,1,0:T(8,128)(2,1)} fusion(bf16[2048,2048]{1,0:T(8,128)(2,1)} %param.13, bf16[32,8,16,128]{3,2,1,0:T(8,128)(2,1)S(1)} %bitcast.180), kind=kOutput, calls=%fused_computation.11 | convolution fusion | flops 2148007936 | bytes 10485760 | tf_op jit(solution)/shard_map/dot_general | solution.py:90
  544.4 7.8 %reduce-scatter.5.cloned.1.call-done = f32[128,256]{0,1:T(8,128)} async-done(((f32[128,2048]{0,1:T(8,128)}), f32[128,256]{0,1:T(8,128)}) %reduce-scatter.5.cloned.1.call-update) | async-done | bytes 131088 | tf_op jit(solution)/shard_map/reduce_scatter | solution.py:123
  552.3 1.6 multiply_bitcast_fusion
  (125 shorter events, 20.7 us)
Async XLA Ops:
  7.2 1.2 copy-start
  7.2 132.8 %all-gather.8.cloned.1.call-start = ((), (), s32[]{:S(2)}) async-start(), calls=%async_computation.5 | async-start | bytes 17825792 | tf_op jit(solution)/shard_map/all_gather | solution.py:15
  14.4 2.9 copy-start.27
  15.4 3.0 copy-start.2
  17.2 42.7 %copy-start.6 = (bf16[32,8,16,128]{3,2,1,0:T(8,128)(2,1)}, bf16[32,8,16,128]{3,2,1,0:T(8,128)(2,1)S(1)}, u32[]{:S(2)}) copy-start(bf16[32,8,16,128]{3,2,1,0:T(8,128)(2,1)S(1)} %copy.112) | copy-start | bytes 3145732
  18.4 1.4 copy-start.16
  25.9 252.1 %all-gather.6.cloned.1.call-start = ((), (), s32[]{:S(2)}) async-start(), calls=%async_computation.4 | async-start | bytes 17825792 | tf_op jit(solution)/shard_map/all_gather | solution.py:15
  27.4 32.6 %copy-start.4 = (bf16[32,8,16,128]{3,2,1,0:T(8,128)(2,1)}, bf16[32,8,16,128]{3,2,1,0:T(8,128)(2,1)S(1)}, u32[]{:S(2)}) copy-start(bf16[32,8,16,128]{3,2,1,0:T(8,128)(2,1)S(1)} %copy.113) | copy-start | bytes 3145732
  29.3 1.0 copy-start.9
  30.2 1.3 copy-start.18
  37.6 481.1 %reduce-scatter.3.cloned.1.call-start = ((), (), s32[]{:S(2)}) async-start(), calls=%async_computation.2 | async-start | bytes 17825792 | tf_op jit(solution)/shard_map/reduce_scatter | solution.py:117
  60.0 1.2 copy-start.10
  61.2 1.8 copy-start.24
  61.2 2.7 copy-start.17
  63.9 5.7 %copy-start.19 = (f32[2,16,128,128]{3,2,1,0:T(8,128)S(1)}, f32[2,16,128,128]{3,2,1,0:T(8,128)}, u32[]{:S(2)}) copy-start(f32[2,16,128,128]{3,2,1,0:T(8,128)} %copy-done.18) | copy-start | bytes 6291460
  279.4 4.0 copy-start.7
  279.4 4.0 copy-start.20
  283.4 1.0 copy-start.12
  285.1 1.0 copy-start.22
  294.2 1.2 copy-start.3
  294.3 1.5 copy-start.11
  294.3 2.4 copy-start.25
  294.3 258.0 %reduce-scatter.5.cloned.1.call-start = ((), (), s32[]{:S(2)}) async-start(), calls=%async_computation.3 | async-start | bytes 1179648 | tf_op jit(solution)/shard_map/reduce_scatter | solution.py:123
  296.7 1.8 copy-start.26
  296.7 2.0 copy-start.8
  298.7 220.1 %copy-start.5 = (bf16[32,8,16,128]{3,2,1,0:T(8,128)(2,1)S(1)}, bf16[32,8,16,128]{3,2,1,0:T(8,128)(2,1)}, u32[]{:S(2)}) copy-start(bf16[32,8,16,128]{3,2,1,0:T(8,128)(2,1)} %copy-done.4) | copy-start | bytes 3145732
  518.8 3.2 copy-start.14
  518.8 3.2 copy-start.21
  522.5 4.0 copy-start.15
  529.9 3.3 copy-start.13
  535.7 2.0 copy-start.23
  537.6 16.2 %copy-start.1 = (bf16[1,256,2048]{2,1,0:T(8,128)(2,1)S(1)}, bf16[1,256,2048]{2,1,0:T(8,128)(2,1)}, u32[]{:S(2)}) copy-start(bf16[1,256,2048]{2,1,0:T(8,128)(2,1)} %param.14) | copy-start | bytes 3145732
Sparse Core Ops, SparseCore 0:
  26.0 113.9 all-gather.7
  142.7 111.0 all-gather.5
  294.4 224.2 reduce-scatter.2
  521.0 31.2 reduce-scatter.4
where the time goes:
time: 563 us; the launch traced here: 560 us
  waiting for transfers between devices  291 us (52%)
  loops' own time  93.8 us (17%)
  matrix products  62.5 us (11%)
  local copies, waits for them, and re-layouts  45.1 us (8%)
  other arithmetic  31.5 us (6%)
  blocking collectives  22.2 us (4%)
  between operations  14.1 us (3%)
    reduce_scatter x1, waiting for transfers between devices, body(): lax.psum_scatter(lax.dot_general(upstream, attended, (((0,), (0,)), ((),...  218 us
    another operation x2, loops' own time, prefix(): return lax.fori_loop(0, ahead, one, state)  93.8 us
    all_gather x2, waiting for transfers between devices, prefix(): gathered = jax.tree.map(lambda a: lax.all_gather(a, axis), part)  64.7 us
    select_n x15, other arithmetic, join_backward(): jnp.where(b_empty, a_state, b_state + jnp.where(linked, a_state, 0.0))  24.1 us
    all_gather x1, blocking collectives, prefix(): gathered = jax.tree.map(lambda a: lax.all_gather(a, axis), part)  22.2 us
    unnamed x60, local copies, waits for them, and re-layouts  13.9 us
  transfers between devices with their start and end apart: 4, of which 3 were waited for; matrix products, arithmetic and copies ran while one was open for 18% of the time, Pallas kernels for 0%

commit v1 on v0

v1 whole, which is shorter than its diff:
```python
import functools

import jax
import jax.numpy as jnp
from jax import lax
from jax.experimental import pallas as pl
from jax.experimental.pallas import tpu as pltpu
from jax.sharding import Mesh
from jax.sharding import PartitionSpec as P

HEADS = 16
HDIM = 128
TILE = 128
TOKENS = 2 * TILE
BLOCKS = 16
ROWS = HDIM + 8
SCALE = 1.0 / HDIM
F32 = jnp.float32
BF16 = jnp.bfloat16
VMEM = 60 * 1024 * 1024
WEIGH = 100


def mul(a, b, da, db):
    return lax.dot_general(a, b, (((da,), (db,)), ((), ())), preferred_element_type=F32)


def params():
    return pltpu.CompilerParams(vmem_limit_bytes=VMEM)


def cost(flops, moved):
    return pl.CostEstimate(flops=int(flops) // WEIGH, bytes_accessed=int(moved) // WEIGH, transcendentals=0)


def whole(shape):
    return pl.BlockSpec(shape, lambda *_: (0,) * len(shape))


SMEM = pl.BlockSpec(memory_space=pltpu.SMEM)


def put_ends(ref, head, docs):
    ref[head, HDIM : HDIM + 1, :] = jnp.full((1, HDIM), docs[0, 0], jnp.int32).astype(F32)
    ref[head, HDIM + 1 : HDIM + 2, :] = jnp.full((1, HDIM), docs[0, 1], jnp.int32).astype(F32)
    ref[head, HDIM + 2 :, :] = jnp.zeros((ROWS - HDIM - 2, HDIM), F32)


def joined(x, keep, first):
    rows = lax.broadcasted_iota(jnp.int32, x.shape, 0)
    return jnp.where(keep | ((rows >= TILE) if first else (rows < TILE)), x, jnp.zeros_like(x))


def trailing_kernel(docs, k, v, out):
    kv = mul(joined(k[...], docs[0, 0] == docs[0, 1], True), v[...], 0, 0)
    for head in range(2):
        part = slice(head * HDIM, (head + 1) * HDIM)
        out[head, :HDIM, :] = kv[part, part]
        put_ends(out, head, docs)


def leading_kernel(docs, grad_out, weight, q, g, out):
    grad = mul(grad_out[...], weight[...], 1, 1).astype(BF16)
    g[...] = grad
    qg = mul(joined(grad, docs[0, 0] == docs[0, 1], False), q[...], 0, 0)
    for head in range(2):
        part = slice(head * HDIM, (head + 1) * HDIM)
        out[head, :HDIM, :] = qg[part, part]
        put_ends(out, head, docs)


def scan_kernel(reverse, part, out):
    carried = jnp.zeros((HDIM, HDIM), F32)
    near = jnp.full((1, HDIM), -1.0, F32)
    order = range(BLOCKS - 1, -1, -1) if reverse else range(BLOCKS)
    for block in order:
        first = part[block, HDIM : HDIM + 1, :]
        last = part[block, HDIM + 1 : HDIM + 2, :]
        entry, leave = (last, first) if reverse else (first, last)
        state = jnp.where(near == entry, carried, 0.0)
        out[block] = state
        carried = part[block, :HDIM, :] + jnp.where(first == last, state, 0.0)
        near = leave


def causal(same):
    rows = lax.broadcasted_iota(jnp.int32, (TOKENS, TOKENS), 0)
    cols = lax.broadcasted_iota(jnp.int32, (TOKENS, TOKENS), 1)
    return (rows >= cols) & (same | (rows < TILE) | (cols >= TILE))


def attended_kernel(place, docs, q, k, v, state, low, high, out, far, up, own, down, turned):
    del place
    step = pl.program_id(0)
    width = low.shape[1]
    up[:, pl.ds(pl.multiple_of(step * width, width), width)] = low[...]
    down[:, pl.ds(pl.multiple_of(step * width, width), width)] = high[...]
    same = docs[0, 0] == docs[0, 1]
    mask = causal(same)
    for head in range(state.shape[0]):
        cols = slice(head * HDIM, (head + 1) * HDIM)
        query = q[:, cols]
        attn = jnp.where(mask, SCALE * mul(query, k[:, cols], 1, 1), 0.0).astype(BF16)
        got = mul(attn, v[:, cols], 1, 0)
        got = got + mul(joined(query, same, False), (SCALE * state[head]).astype(BF16), 1, 0)
        got = got.astype(BF16)
        out[:, cols] = got
        turned[cols, :] = got.astype(F32).T

    @pl.when(step == 0)
    def _():
        far[...] = turned[...]

    @pl.when(step == 2)
    def _():
        own[...] = turned[...].astype(BF16)

    for when, wide in ((1, up), (3, down)):

        @pl.when(step == when)
        def _(wide=wide):
            for head in range(4):
                start = 4 * width + head * TOKENS
                wide[:, start : start + TOKENS] = turned[head * HDIM : (head + 1) * HDIM, :]


def grads_kernel(docs, q, k, v, g, state, rev, gq, gk, gv):
    same = docs[0, 0] == docs[0, 1]
    mask = causal(same)
    for head in range(state.shape[0]):
        cols = slice(head * HDIM, (head + 1) * HDIM)
        qh, kh, vh, gh = q[:, cols], k[:, cols], v[:, cols], g[:, cols]
        attn_q = jnp.where(mask, SCALE * mul(qh, kh, 1, 1), 0.0).astype(BF16)
        attn_g = jnp.where(mask, SCALE * mul(gh, vh, 1, 1), 0.0).astype(BF16)
        state_b = (SCALE * state[head]).astype(BF16)
        rev_b = (SCALE * rev[head]).astype(BF16)
        gq[:, cols] = (mul(attn_g, kh, 1, 0) + mul(joined(gh, same, False), state_b, 1, 1)).astype(BF16)
        gk[:, cols] = (mul(attn_g, qh, 0, 0) + mul(joined(vh, same, True), rev_b, 1, 0)).astype(BF16)
        gv[:, cols] = (mul(attn_q, gh, 0, 0) + mul(joined(kh, same, True), rev_b, 1, 1)).astype(BF16)


def product_kernel(side, att_own, att_far, att_low, att_high, own, low_a, low_b, high_a, high_b, far_a, far_b, out, left, right):
    del side

    @pl.when(pl.program_id(0) == 0)
    def _():
        left[:, :TOKENS] = att_own[...]
        for i, att in enumerate((att_low, att_high)):
            cols = slice((i + 1) * TOKENS, (i + 2) * TOKENS)
            left[:HDIM, cols] = att[:, :TOKENS].astype(BF16)
            left[HDIM:, cols] = att[:, TOKENS:].astype(BF16)
        left[:, 3 * TOKENS :] = att_far[...].astype(BF16)

    right[:TOKENS] = own[...]
    for i, other in enumerate((low_a, low_b, high_a, high_b, far_a, far_b)):
        right[TOKENS + i * TILE : TOKENS + (i + 1) * TILE] = other[...].astype(BF16)
    total = mul(left[...], right[...], 1, 0)
    for block in range(out.shape[0]):
        out[block] = total[:, block * HDIM : (block + 1) * HDIM]


def product(att_own, att_far, own, low, high, up, down, side):
    width = own.shape[1]
    step = 4 * HDIM
    rows = pl.BlockSpec((TOKENS, TOKENS), lambda i, w: (w[0], 0))
    packed = pl.BlockSpec((TILE, 2 * TOKENS), lambda i, w: (0, width // (2 * TOKENS) + w[0]))

    def cols(count):
        return pl.BlockSpec((count, step), lambda i, w: (0, i))

    spec = pltpu.PrefetchScalarGridSpec(
        num_scalar_prefetch=1,
        grid=(width // step,),
        in_specs=[rows, rows, packed, packed, cols(TOKENS)] + [cols(TILE)] * 6,
        out_specs=pl.BlockSpec((step // HDIM, TOKENS, HDIM), lambda i, w: (i, 0, 0)),
        scratch_shapes=[pltpu.VMEM((TOKENS, 4 * TOKENS), BF16), pltpu.VMEM((4 * TOKENS, step), BF16)],
    )
    return pl.pallas_call(
        product_kernel,
        grid_spec=spec,
        out_shape=jax.ShapeDtypeStruct((width // HDIM, TOKENS, HDIM), F32),
        compiler_params=params(),
        cost_estimate=cost(2 * 256 * 1024 * width, 4 * width * 1024),
        name="product",
    )(side.astype(jnp.int32).reshape(1), att_own, att_far, up, down, own, *low, *high, up, down)


def ring(step):
    return [(i, (i + step) % 4) for i in range(4)]


def body(queries, keys, values, weight, grad_out, docs):
    ctx = ("x", "z")
    q, k, v, go = queries[0], keys[0], values[0], grad_out[0]
    width = q.shape[1]
    factor = 1.0 / float(TOKENS * 128) ** 0.5

    top, bottom = go[:TILE].astype(F32), go[TILE:].astype(F32)
    top, bottom, k, v = lax.optimization_barrier((top, bottom, k, v))
    low_top = lax.ppermute(top, "y", ring(1))
    high_bottom = lax.ppermute(bottom, "y", ring(-1))
    low_bottom = lax.ppermute(bottom, "y", ring(1))
    high_top = lax.ppermute(top, "y", ring(-1))

    per = 2
    block = pl.BlockSpec((TOKENS, per * HDIM), lambda i: (0, i))
    summed = pl.BlockSpec((per, ROWS, HDIM), lambda i: (i, 0, 0))
    matrix = pl.BlockSpec((per, HDIM, HDIM), lambda i: (i, 0, 0))
    tokens = jax.ShapeDtypeStruct((TOKENS, width), BF16)
    payload = jax.ShapeDtypeStruct((HEADS, ROWS, HDIM), F32)

    trailing = pl.pallas_call(
        trailing_kernel,
        grid=(HEADS // per,),
        in_specs=[SMEM, block, block],
        out_specs=summed,
        out_shape=payload,
        compiler_params=params(),
        cost_estimate=cost(2 * 32 * 128**3, 3 << 20),
        name="trailing",
    )(docs, k, v)
    by_head = lax.all_to_all(trailing, ctx, 0, 0, tiled=True)

    g, leading = pl.pallas_call(
        leading_kernel,
        grid=(HEADS // per,),
        in_specs=[
            SMEM,
            whole((TOKENS, width)),
            pl.BlockSpec((per * HDIM, width), lambda i: (i, 0)),
            block,
        ],
        out_specs=[block, summed],
        out_shape=[tokens, payload],
        compiler_params=params(),
        cost_estimate=cost(2 * 256 * 2048 * 2048, 12 << 20),
        name="leading",
    )(docs, go, weight, q)

    def scan(parts, reverse):
        return pl.pallas_call(
            functools.partial(scan_kernel, reverse),
            out_shape=jax.ShapeDtypeStruct((BLOCKS, HDIM, HDIM), F32),
            compiler_params=params(),
            cost_estimate=cost(1 << 20, 2 << 20),
            name="scan",
        )(parts)

    by_head, leading, low_top, high_bottom = lax.optimization_barrier((by_head, leading, low_top, high_bottom))
    state = lax.all_to_all(scan(by_head, False), ctx, 0, 0, tiled=True)
    state, low_bottom, high_top = lax.optimization_barrier((state, low_bottom, high_top))

    def group(i, w):
        return (w[0] + 6 - i) % 4

    place = lax.axis_index("y").astype(jnp.int32).reshape(1)
    four = pl.BlockSpec((TOKENS, 4 * HDIM), lambda i, w: (0, group(i, w)))
    passed = pl.BlockSpec((TILE, 4 * HDIM), lambda i, w: (0, i))
    turned = jax.ShapeDtypeStruct((4 * HDIM, TOKENS), F32)
    packed = jax.ShapeDtypeStruct((TILE, width + 4 * TOKENS), F32)
    attended, far, up, att_own, down = pl.pallas_call(
        attended_kernel,
        grid_spec=pltpu.PrefetchScalarGridSpec(
            num_scalar_prefetch=1,
            grid=(HEADS // 4,),
            in_specs=[SMEM, four, four, four, pl.BlockSpec((4, HDIM, HDIM), lambda i, w: (group(i, w), 0, 0))]
            + [passed, passed],
            out_specs=[four] + [pl.BlockSpec(part.shape, lambda i, w: (0, 0)) for part in (turned, packed, turned, packed)],
            scratch_shapes=[pltpu.VMEM((4 * HDIM, TOKENS), F32)],
        ),
        out_shape=[tokens, turned, packed, jax.ShapeDtypeStruct(turned.shape, BF16), packed],
        compiler_params=params(),
        cost_estimate=cost(2 * 32 * 4 * 128**3, 7 << 20),
        name="attended",
    )(place, docs, q, k, v, state, low_top, high_bottom)
    leading, attended = lax.optimization_barrier((leading, attended))
    rev_by_head = lax.all_to_all(leading, ctx, 0, 0, tiled=True)
    up = lax.ppermute(up, "y", ring(1))
    down = lax.ppermute(down, "y", ring(-1))
    far = lax.ppermute(far, "y", ring(2))
    rev_by_head, far = lax.optimization_barrier((rev_by_head, far))
    rev_scan = scan(rev_by_head, True)

    layer_out = jnp.dot(attended, weight, preferred_element_type=F32).astype(BF16)

    core = lax.axis_index("core")
    rev = lax.all_to_all(rev_scan, ctx, 0, 0, tiled=True)
    far, rev = lax.optimization_barrier((far, rev))
    pieces = (att_own, far, go, (low_top, low_bottom), (high_top, high_bottom), up, down)
    given = product(*pieces, 1 - core)
    kept = product(*pieces, core)
    taken = lax.ppermute(given, "core", [(0, 1), (1, 0)])
    spread = lax.all_to_all((kept + taken) * factor, ctx, 0, 0, tiled=True)
    grad_weight = jnp.sum(spread, axis=0)

    grad_q, grad_k, grad_v = pl.pallas_call(
        grads_kernel,
        grid=(HEADS // per,),
        in_specs=[SMEM, block, block, block, block, matrix, matrix],
        out_specs=[block, block, block],
        out_shape=[tokens, tokens, tokens],
        compiler_params=params(),
        cost_estimate=cost(2 * 32 * 10 * 128**3, 9 << 20),
        name="grads",
    )(docs, q, k, v, g, state, rev)
    return layer_out[None], grad_q[None], grad_k[None], grad_v[None], grad_weight


def solution(mesh):
    fine = Mesh(mesh.devices.reshape(4, 2, 4, 4), ("y", "core", "x", "z"))
    dp, ctx = ("y", "core"), ("x", "z")
    tokens = P(dp, ctx, None)
    return jax.shard_map(
        body,
        mesh=fine,
        in_specs=(tokens, tokens, tokens, P(), tokens, P(dp, ctx)),
        out_specs=(tokens, tokens, tokens, tokens, P(dp, ctx)),
        check_vma=False,
    )
```

time: 563 us -> 198 us (0.35)
  waiting for transfers between devices: 291 us -> 90.9 us
  loops' own time: 93.8 us -> 0 us
  matrix products: 62.5 us -> 6.68 us
  Pallas kernels: 0 us -> 51.4 us
  local copies, waits for them, and re-layouts: 45.1 us -> 3.74 us
  starting transfers between devices: 0.38 us -> 36 us
  other arithmetic: 31.5 us -> 6.69 us
  blocking collectives: 22.2 us -> 0 us
  between operations: 14.1 us -> 0.74 us
    reduce_scatter x2 -> x0, waiting for transfers between devices: 226 us -> none  [the longest x1 218 us: body(): lax.psum_scatter(lax.dot_general(upstream, attended, (((0,), (0,)), ((),...]
    another operation x2 -> x0, loops' own time: 93.8 us -> none  [prefix(): return lax.fori_loop(0, ahead, one, state)]
    all_gather x2 -> x0, waiting for transfers between devices: 64.7 us -> none  [prefix(): gathered = jax.tree.map(lambda a: lax.all_gather(a, axis), part)]
    dot_general x19 -> x1, matrix products: 62.5 us -> 6.68 us  [body(): jnp.dot(attended, weight, preferred_element_type=F32).astype(BF16)]
    pallas_call x0 -> x8, Pallas kernels: none -> 51.4 us  [the longest x2 12.4 us: product(): pl.pallas_call(product_kernel, grid_spec=spec, out_shape=jax.ShapeDtypeSt...]
    ppermute x0 -> x8, waiting for transfers between devices: none -> 49.3 us  [the longest x1 42.6 us: body(): far = lax.ppermute(far, 'y', ring(2))]
    all_to_all x0 -> x5, waiting for transfers between devices: none -> 41.7 us  [the longest x1 14.1 us: body(): spread = lax.all_to_all((kept + taken) * factor, ctx, 0, 0, tiled=True)]
    all_to_all x0 -> x5, starting transfers between devices: none -> 26.7 us  [the longest x1 7.96 us: body(): by_head = lax.all_to_all(trailing, ctx, 0, 0, tiled=True)]
  transfers between devices with their start and end apart: 4 -> 13, of which waited for: 3 -> 6; matrix products, arithmetic and copies ran while one was open for 18% -> 3% of each run, Pallas kernels for 0% -> 19%
where the time goes in v1:
time: 198 us; the launch traced here: 196 us
  waiting for transfers between devices  90.9 us (46%)
  Pallas kernels  51.4 us (26%)
  starting transfers between devices  36 us (18%)
  other arithmetic  6.69 us (3%)
  matrix products  6.68 us (3%)
  local copies, waits for them, and re-layouts  3.74 us (2%)
    ppermute x1, waiting for transfers between devices, body(): far = lax.ppermute(far, 'y', ring(2))  42.6 us
    all_to_all x1, waiting for transfers between devices, body(): spread = lax.all_to_all((kept + taken) * factor, ctx, 0, 0, tiled=True)  14.1 us
    all_to_all x1, waiting for transfers between devices, body(): rev = lax.all_to_all(rev_scan, ctx, 0, 0, tiled=True)  13.8 us
    pallas_call x2, Pallas kernels, product(): pl.pallas_call(product_kernel, grid_spec=spec, out_shape=jax.ShapeDtypeSt...  12.4 us
    pallas_call x1, Pallas kernels, body(): pl.pallas_call(leading_kernel, grid=(HEADS // per,), in_specs=[SMEM, whol...  10.4 us
    pallas_call x1, Pallas kernels, body(): pl.pallas_call(grads_kernel, grid=(HEADS // per,), in_specs=[SMEM, block,...  9.93 us
    all_to_all x1, waiting for transfers between devices, body(): state = lax.all_to_all(scan(by_head, False), ctx, 0, 0, tiled=True)  8.46 us
    all_to_all x1, starting transfers between devices, body(): by_head = lax.all_to_all(trailing, ctx, 0, 0, tiled=True)  7.96 us
  transfers between devices with their start and end apart: 13, of which 6 were waited for; matrix products, arithmetic and copies ran while one was open for 3% of the time, Pallas kernels for 19%

profile of v1, /device:TPU:0, one launch (start us, length us, event | category | flops | bytes accessed | tf_op | source)
XLA Modules:
  0.0 196.2 jit_solution(16507866922163590205)
XLA Ops:
  0.6 2.8 %bitcast_convert_fusion = (f32[128,2048]{1,0:T(8,128)}, f32[128,2048]{1,0:T(8,128)}) fusion(bf16[1,256,2048]{2,1,0:T(8,128)(2,1)} %param.10), kind=kLoop, calls=%fused_computation.3 | loop fusion | flops 524288 | bytes 3145728 | tf_op jit(solution)/shard_map/convert_element_type | solution.py:198
  3.4 1.7 collective-permute-start
  5.1 1.6 collective-permute-start.1
  6.6 6.4 %trailing.1 = f32[16,136,128]{2,1,0:T(8,128)} custom-call(s32[1,2]{1,0:T(1,128)} %docs.7, bf16[256,2048]{1,0:T(8,128)(2,1)} %bitcast.23, bf16[256,2048]{1,0:T(8,128)(2,1)} %bitcast.26), custom_call_target="tpu_custom_call" | custom-call | flops 1342177 | bytes 31457 | tf_op jit(solution)/shard_map/trailing/pallas_call | solution.py:212
  13.0 8.0 %all-to-all-start = ((f32[16,136,128]{2,1,0:T(8,128)}), f32[16,136,128]{2,1,0:T(8,128)S(1)}, u32[]{:S(2)}, u32[]{:S(2)}) async-start(f32[16,136,128]{2,1,0:T(8,128)} %trailing.1), calls=%async_computation | async-start | bytes 2228224 | tf_op jit(solution)/shard_map/all_to_all | solution.py:222
  21.0 1.9 collective-permute-start.3
  22.9 0.2 collective-permute-start.2
  23.1 10.4 %leading.1 = (bf16[256,2048]{1,0:T(8,128)(2,1)}, f32[16,136,128]{2,1,0:T(8,128)}) custom-call(s32[1,2]{1,0:T(1,128)} %docs.7, bf16[256,2048]{1,0:T(8,128)(2,1)} %bitcast.20, bf16[2048,2048]{1,0:T(8,128)(2,1)} %weight.1, bf16[256,2048]{1,0:T(8,128)(2,1)} %bitcast.29), custom_call_target="tpu_custom_call" | custom-call | flops 21474836 | bytes 125829 | tf_op jit(solution)/shard_map/leading/pallas_call | solution.py:224
  33.5 5.3 %all-to-all-done.part = f32[16,136,128]{2,1,0:T(8,128)S(1)} async-done(((f32[16,136,128]{2,1,0:T(8,128)}), f32[16,136,128]{2,1,0:T(8,128)S(1)}, u32[]{:S(2)}, u32[]{:S(2)}) %all-to-all-start) | async-done | bytes 1114144 | tf_op jit(solution)/shard_map/all_to_all | solution.py:222
  38.8 0.0 copy-start.5
  38.8 0.0 collective-permute-done.low.low_a
  38.8 0.0 copy-start.2
  38.8 0.0 collective-permute-done.1.high.high_b
  38.8 0.0 copy-start.3
  38.8 1.0 copy-done.5
  39.8 2.4 %scan.2 = f32[16,128,128]{2,1,0:T(8,128)} custom-call(f32[16,136,128]{2,1,0:T(8,128)} %copy-done.5), custom_call_target="tpu_custom_call" | custom-call | flops 10485 | bytes 20971 | tf_op jit(solution)/shard_map/scan/pallas_call | solution.py:241
  42.2 0.0 copy-done.2
  42.2 0.0 copy-done.3
  42.2 3.7 %all-to-all-start.1 = ((f32[16,128,128]{2,1,0:T(8,128)}), f32[16,128,128]{2,1,0:T(8,128)S(1)}, u32[]{:S(2)}, u32[]{:S(2)}) async-start(f32[16,128,128]{2,1,0:T(8,128)} %scan.2), calls=%async_computation.1 | async-start | bytes 2097152 | tf_op jit(solution)/shard_map/all_to_all | solution.py:250
  45.8 6.6 %collective-permute-done.3.high_a = f32[128,2048]{1,0:T(8,128)} collective-permute-done((f32[128,2048]{1,0:T(8,128)}, f32[128,2048]{1,0:T(8,128)}, u32[]{:S(2)}, u32[]{:S(2)}) %collective-permute-start.3) | collective-permute-done | bytes 1048608 | tf_op jit(solution)/shard_map/ppermute | solution.py:203
  52.5 0.0 collective-permute-done.2.low_b
  52.5 8.5 %all-to-all-done.1.state = f32[16,128,128]{2,1,0:T(8,128)S(1)} async-done(((f32[16,128,128]{2,1,0:T(8,128)}), f32[16,128,128]{2,1,0:T(8,128)S(1)}, u32[]{:S(2)}, u32[]{:S(2)}) %all-to-all-start.1) | async-done | bytes 1048608 | tf_op jit(solution)/shard_map/all_to_all | solution.py:250
  60.9 0.0 copy-start.4
  60.9 1.1 copy-done.4
  62.0 7.5 %attended.1 = (bf16[256,2048]{1,0:T(8,128)(2,1)}, f32[512,256]{1,0:T(8,128)}, f32[128,3072]{1,0:T(8,128)}, bf16[512,256]{1,0:T(8,128)(2,1)}, f32[128,3072]{1,0:T(8,128)}) custom-call(s32[1]{0:T(128)} %bitcast.6.place, s32[1,2]{1,0:T(1,128)} %docs.7, bf16[256,2048]{1,0:T(8,128)(2,1)} %bitcast.30, bf16[256,2048]{1,0:T(8,128)(2,1)} %bitcast.24, ...), custom_call_target="tpu_custom_call" | custom-call | flops 5368709 | bytes 73400 | tf_op jit(solution)/shard_map/attended/pallas_call | solution.py:261
  69.5 4.4 %all-to-all-start.2 = ((f32[16,136,128]{2,1,0:T(8,128)}), f32[16,136,128]{2,1,0:T(8,128)}, u32[]{:S(2)}, u32[]{:S(2)}) async-start(f32[16,136,128]{2,1,0:T(8,128)} %get-tuple-element.45), calls=%async_computation.2 | async-start | bytes 2228224 | tf_op jit(solution)/shard_map/all_to_all | solution.py:277
  73.9 0.3 collective-permute-start.5
  74.3 3.0 %collective-permute-start.6 = (f32[128,3072]{1,0:T(8,128)}, f32[128,3072]{1,0:T(8,128)S(1)}, u32[]{:S(2)}, u32[]{:S(2)}) collective-permute-start(f32[128,3072]{1,0:T(8,128)} %get-tuple-element.56), channel_id=1, source_target_pairs={{0,96},{32,0},{64,32},{96,64},{1,97},{33,1},{65,33},{97,65},{2,98}... | collective-permute-start | bytes 4718600 | tf_op jit(solution)/shard_map/ppermute | solution.py:279
  77.2 0.7 collective-permute-start.4
  77.9 42.6 %collective-permute-done.4.att_far = f32[512,256]{1,0:T(8,128)} collective-permute-done((f32[512,256]{1,0:T(8,128)}, f32[512,256]{1,0:T(8,128)}, u32[]{:S(2)}, u32[]{:S(2)}) %collective-permute-start.4) | collective-permute-done | bytes 524320 | tf_op jit(solution)/shard_map/ppermute | solution.py:280
  120.5 0.0 all-to-all-done.2.part
  120.5 2.3 %scan.3 = f32[16,128,128]{2,1,0:T(8,128)} custom-call(f32[16,136,128]{2,1,0:T(8,128)} %all-to-all-done.2.part), custom_call_target="tpu_custom_call" | custom-call | flops 10485 | bytes 20971 | tf_op jit(solution)/shard_map/scan/pallas_call | solution.py:241
  122.9 6.9 %all-to-all-start.3 = ((f32[16,128,128]{2,1,0:T(8,128)}), f32[16,128,128]{2,1,0:T(8,128)}, u32[]{:S(2)}, u32[]{:S(2)}) async-start(f32[16,128,128]{2,1,0:T(8,128)} %scan.3), calls=%async_computation.3 | async-start | bytes 2097152 | tf_op jit(solution)/shard_map/all_to_all | solution.py:287
  129.7 13.8 %all-to-all-done.3.rev = f32[16,128,128]{2,1,0:T(8,128)} async-done(((f32[16,128,128]{2,1,0:T(8,128)}), f32[16,128,128]{2,1,0:T(8,128)}, u32[]{:S(2)}, u32[]{:S(2)}) %all-to-all-start.3) | async-done | bytes 1048608 | tf_op jit(solution)/shard_map/all_to_all | solution.py:287
  143.6 0.0 collective-permute-done.5.att_low.far_a
  143.6 0.0 copy-start
  143.6 0.0 collective-permute-done.6.att_high.far_b
  143.6 0.0 copy-start.1
  143.6 1.2 copy-done
  144.8 0.5 copy-done.1
  145.3 6.2 %product.3 = f32[16,256,128]{2,1,0:T(8,128)} custom-call(s32[1]{0:T(128)} %bitcast.12.side, bf16[512,256]{1,0:T(8,128)(2,1)} %get-tuple-element.53.att_own, f32[512,256]{1,0:T(8,128)} %collective-permute-done.4.att_far, f32[128,3072]{1,0:T(8,128)} %copy-done, f32[128,3072]{1,0:T(8,128)} %copy-done.1, bf16[256,2048]{1,0:T(8,128)(2,1)} %bitcast.21, ...), custom_call_target="tpu_custom_call" | custom-call | flops 10737418 | bytes 83886 | tf_op jit(solution)/shard_map/product/pallas_call | solution.py:178
  151.5 0.0 collective-permute-start.7
  151.5 6.2 %product.2 = f32[16,256,128]{2,1,0:T(8,128)} custom-call(s32[1]{0:T(128)} %bitcast.11.side, bf16[512,256]{1,0:T(8,128)(2,1)} %get-tuple-element.53.att_own, f32[512,256]{1,0:T(8,128)} %collective-permute-done.4.att_far, f32[128,3072]{1,0:T(8,128)} %copy-done, f32[128,3072]{1,0:T(8,128)} %copy-done.1, bf16[256,2048]{1,0:T(8,128)(2,1)} %bitcast.22, ...), custom_call_target="tpu_custom_call" | custom-call | flops 10737418 | bytes 83886 | tf_op jit(solution)/shard_map/product/pallas_call | solution.py:178
  157.7 0.0 collective-permute-done.7
  157.7 3.2 %add_multiply_fusion = f32[16,256,128]{2,1,0:T(8,128)} fusion(f32[16,256,128]{2,1,0:T(8,128)} %product.2, f32[16,256,128]{2,1,0:T(8,128)S(1)} %collective-permute-done.7), kind=kLoop, calls=%fused_computation.2 | loop fusion | flops 1048576 | bytes 6291456 | tf_op jit(solution)/shard_map/mul | solution.py:293
  160.9 0.0 copy-start.6
  160.9 3.8 %all-to-all-start.4 = ((f32[16,256,128]{2,1,0:T(8,128)}), f32[16,256,128]{2,1,0:T(8,128)S(1)}, u32[]{:S(2)}, u32[]{:S(2)}) async-start(f32[16,256,128]{2,1,0:T(8,128)} %add_multiply_fusion), calls=%async_computation.4 | async-start | bytes 4194304 | tf_op jit(solution)/shard_map/all_to_all | solution.py:293
  164.7 0.0 copy-done.6
  164.7 6.7 %fusion = bf16[1,256,2048]{2,1,0:T(8,128)(2,1)} fusion(bf16[256,2048]{1,0:T(8,128)(2,1)S(1)} %copy-done.6, bf16[2048,2048]{1,0:T(8,128)(2,1)} %weight.1), kind=kOutput, calls=%fused_computation.1 | convolution fusion | flops 2148007936 | bytes 10485760 | tf_op jit(solution)/shard_map/dot_general | solution.py:284
  171.4 9.9 %grads.1 = (bf16[256,2048]{1,0:T(8,128)(2,1)}, bf16[256,2048]{1,0:T(8,128)(2,1)}, bf16[256,2048]{1,0:T(8,128)(2,1)}) custom-call(s32[1,2]{1,0:T(1,128)} %docs.7, bf16[256,2048]{1,0:T(8,128)(2,1)} %bitcast.31, bf16[256,2048]{1,0:T(8,128)(2,1)} %bitcast.25, bf16[256,2048]{1,0:T(8,128)(2,1)} %bitcast.28, bf16[256,2048]{1,0:T(8,128)(2,1)} %get-tuple-element.44.g, ...), custom_call_target="tpu_custom_call" | custom-call | flops 13421772 | bytes 94371 | tf_op jit(solution)/shard_map/grads/pallas_call | solution.py:296
  181.4 14.1 %all-to-all-done.4 = f32[16,256,128]{2,1,0:T(8,128)S(1)} async-done(((f32[16,256,128]{2,1,0:T(8,128)}), f32[16,256,128]{2,1,0:T(8,128)S(1)}, u32[]{:S(2)}, u32[]{:S(2)}) %all-to-all-start.4) | async-done | bytes 2097184 | tf_op jit(solution)/shard_map/all_to_all | solution.py:293
  195.4 0.8 reduce_sum.9
Async XLA Ops:
  3.4 35.4 %collective-permute-start = (f32[128,2048]{1,0:T(8,128)}, f32[128,2048]{1,0:T(8,128)S(1)}, u32[]{:S(2)}, u32[]{:S(2)}) collective-permute-start(f32[128,2048]{1,0:T(8,128)} %get-tuple-element.35), channel_id=1, source_target_pairs={{0,32},{32,64},{64,96},{96,0},{1,33},{33,65},{65,97},{97,1},{2,34}... | collective-permute-start | bytes 3145736 | tf_op jit(solution)/shard_map/ppermute | solution.py:200
  5.1 33.7 %collective-permute-start.1 = (f32[128,2048]{1,0:T(8,128)}, f32[128,2048]{1,0:T(8,128)S(1)}, u32[]{:S(2)}, u32[]{:S(2)}) collective-permute-start(f32[128,2048]{1,0:T(8,128)} %get-tuple-element.36), channel_id=1, source_target_pairs={{0,96},{32,0},{64,32},{96,64},{1,97},{33,1},{65,33},{97,65},{2,98}... | collective-permute-start | bytes 3145736 | tf_op jit(solution)/shard_map/ppermute | solution.py:201
  13.0 25.7 %all-to-all-start = ((f32[16,136,128]{2,1,0:T(8,128)}), f32[16,136,128]{2,1,0:T(8,128)S(1)}, u32[]{:S(2)}, u32[]{:S(2)}) async-start(f32[16,136,128]{2,1,0:T(8,128)} %trailing.1), calls=%async_computation | async-start | bytes 2228224 | tf_op jit(solution)/shard_map/all_to_all | solution.py:222
  21.0 31.5 %collective-permute-start.3 = (f32[128,2048]{1,0:T(8,128)}, f32[128,2048]{1,0:T(8,128)}, u32[]{:S(2)}, u32[]{:S(2)}) collective-permute-start(f32[128,2048]{1,0:T(8,128)} %get-tuple-element.35), channel_id=1, source_target_pairs={{0,96},{32,0},{64,32},{96,64},{1,97},{33,1},{65,33},{97,65},{2,98}... | collective-permute-start | bytes 3145736 | tf_op jit(solution)/shard_map/ppermute | solution.py:203
  22.9 29.6 %collective-permute-start.2 = (f32[128,2048]{1,0:T(8,128)}, f32[128,2048]{1,0:T(8,128)}, u32[]{:S(2)}, u32[]{:S(2)}) collective-permute-start(f32[128,2048]{1,0:T(8,128)} %get-tuple-element.36), channel_id=1, source_target_pairs={{0,32},{32,64},{64,96},{96,0},{1,33},{33,65},{65,97},{97,1},{2,34}... | collective-permute-start | bytes 3145736 | tf_op jit(solution)/shard_map/ppermute | solution.py:202
  38.8 1.0 copy-start.5
  38.8 3.4 %copy-start.2 = (f32[128,2048]{1,0:T(8,128)}, f32[128,2048]{1,0:T(8,128)S(1)}, u32[]{:S(2)}) copy-start(f32[128,2048]{1,0:T(8,128)S(1)} %collective-permute-done.low.low_a) | copy-start | bytes 3145732
  38.8 3.4 %copy-start.3 = (f32[128,2048]{1,0:T(8,128)}, f32[128,2048]{1,0:T(8,128)S(1)}, u32[]{:S(2)}) copy-start(f32[128,2048]{1,0:T(8,128)S(1)} %collective-permute-done.1.high.high_b) | copy-start | bytes 3145732
  42.2 18.8 %all-to-all-start.1 = ((f32[16,128,128]{2,1,0:T(8,128)}), f32[16,128,128]{2,1,0:T(8,128)S(1)}, u32[]{:S(2)}, u32[]{:S(2)}) async-start(f32[16,128,128]{2,1,0:T(8,128)} %scan.2), calls=%async_computation.1 | async-start | bytes 2097152 | tf_op jit(solution)/shard_map/all_to_all | solution.py:250
  60.9 1.1 copy-start.4
  69.5 51.0 %all-to-all-start.2 = ((f32[16,136,128]{2,1,0:T(8,128)}), f32[16,136,128]{2,1,0:T(8,128)}, u32[]{:S(2)}, u32[]{:S(2)}) async-start(f32[16,136,128]{2,1,0:T(8,128)} %get-tuple-element.45), calls=%async_computation.2 | async-start | bytes 2228224 | tf_op jit(solution)/shard_map/all_to_all | solution.py:277
  73.9 69.7 %collective-permute-start.5 = (f32[128,3072]{1,0:T(8,128)}, f32[128,3072]{1,0:T(8,128)S(1)}, u32[]{:S(2)}, u32[]{:S(2)}) collective-permute-start(f32[128,3072]{1,0:T(8,128)} %get-tuple-element.55), channel_id=1, source_target_pairs={{0,32},{32,64},{64,96},{96,0},{1,33},{33,65},{65,97},{97,1},{2,34}... | collective-permute-start | bytes 4718600 | tf_op jit(solution)/shard_map/ppermute | solution.py:278
  74.3 69.3 %collective-permute-start.6 = (f32[128,3072]{1,0:T(8,128)}, f32[128,3072]{1,0:T(8,128)S(1)}, u32[]{:S(2)}, u32[]{:S(2)}) collective-permute-start(f32[128,3072]{1,0:T(8,128)} %get-tuple-element.56), channel_id=1, source_target_pairs={{0,96},{32,0},{64,32},{96,64},{1,97},{33,1},{65,33},{97,65},{2,98}... | collective-permute-start | bytes 4718600 | tf_op jit(solution)/shard_map/ppermute | solution.py:279
  77.2 43.3 %collective-permute-start.4 = (f32[512,256]{1,0:T(8,128)}, f32[512,256]{1,0:T(8,128)}, u32[]{:S(2)}, u32[]{:S(2)}) collective-permute-start(f32[512,256]{1,0:T(8,128)} %get-tuple-element.46), channel_id=1, source_target_pairs={{0,64},{32,96},{64,0},{96,32},{1,65},{33,97},{65,1},{97,33},{2,66}... | collective-permute-start | bytes 1572872 | tf_op jit(solution)/shard_map/ppermute | solution.py:280
  122.9 20.7 %all-to-all-start.3 = ((f32[16,128,128]{2,1,0:T(8,128)}), f32[16,128,128]{2,1,0:T(8,128)}, u32[]{:S(2)}, u32[]{:S(2)}) async-start(f32[16,128,128]{2,1,0:T(8,128)} %scan.3), calls=%async_computation.3 | async-start | bytes 2097152 | tf_op jit(solution)/shard_map/all_to_all | solution.py:287
  143.6 1.2 copy-start
  143.6 1.7 copy-start.1
  151.5 6.2 %collective-permute-start.7 = (f32[16,256,128]{2,1,0:T(8,128)}, f32[16,256,128]{2,1,0:T(8,128)S(1)}, u32[]{:S(2)}, u32[]{:S(2)}) collective-permute-start(f32[16,256,128]{2,1,0:T(8,128)} %product.3), channel_id=1, source_target_pairs={{0,16},{16,0},{1,17},{17,1},{2,18},{18,2},{3,19},{19,3},{4,20},{20... | collective-permute-start | bytes 6291464 | tf_op jit(solution)/shard_map/ppermute | solution.py:292
  160.9 3.9 %copy-start.6 = (bf16[256,2048]{1,0:T(8,128)(2,1)S(1)}, bf16[256,2048]{1,0:T(8,128)(2,1)}, u32[]{:S(2)}) copy-start(bf16[256,2048]{1,0:T(8,128)(2,1)} %get-tuple-element.43) | copy-start | bytes 3145732
  160.9 34.6 %all-to-all-start.4 = ((f32[16,256,128]{2,1,0:T(8,128)}), f32[16,256,128]{2,1,0:T(8,128)S(1)}, u32[]{:S(2)}, u32[]{:S(2)}) async-start(f32[16,256,128]{2,1,0:T(8,128)} %add_multiply_fusion), calls=%async_computation.4 | async-start | bytes 4194304 | tf_op jit(solution)/shard_map/all_to_all | solution.py:293

commit v2 on v1

v2 whole, which is shorter than its diff:
```python
import functools

import jax
import jax.numpy as jnp
from jax import lax
from jax.experimental import pallas as pl
from jax.experimental.pallas import tpu as pltpu
from jax.sharding import Mesh
from jax.sharding import PartitionSpec as P

HEADS = 16
HDIM = 128
TILE = 128
TOKENS = 2 * TILE
BLOCKS = 16
ROWS = HDIM + 8
SCALE = 1.0 / HDIM
F32 = jnp.float32
BF16 = jnp.bfloat16
VMEM = 60 * 1024 * 1024
SMALL = 24 * 1024 * 1024
WEIGH = 100


def mul(a, b, da, db):
    return lax.dot_general(a, b, (((da,), (db,)), ((), ())), preferred_element_type=F32)


def params(limit=VMEM):
    return pltpu.CompilerParams(vmem_limit_bytes=limit)


def cost(flops, moved):
    return pl.CostEstimate(flops=int(flops) // WEIGH, bytes_accessed=int(moved) // WEIGH, transcendentals=0)


def whole(shape):
    return pl.BlockSpec(shape, lambda *_: (0,) * len(shape))


SMEM = pl.BlockSpec(memory_space=pltpu.SMEM)


def put_ends(ref, head, docs):
    ref[head, HDIM : HDIM + 1, :] = jnp.full((1, HDIM), docs[0, 0], jnp.int32).astype(F32)
    ref[head, HDIM + 1 : HDIM + 2, :] = jnp.full((1, HDIM), docs[0, 1], jnp.int32).astype(F32)
    ref[head, HDIM + 2 :, :] = jnp.zeros((ROWS - HDIM - 2, HDIM), F32)


def joined(x, keep, first):
    rows = lax.broadcasted_iota(jnp.int32, x.shape, 0)
    return jnp.where(keep | ((rows >= TILE) if first else (rows < TILE)), x, jnp.zeros_like(x))


def trailing_kernel(docs, k, v, out):
    same = docs[0, 0] == docs[0, 1]
    for pair in range(out.shape[0] // 2):
        cols = slice(2 * pair * HDIM, 2 * (pair + 1) * HDIM)
        kv = mul(joined(k[:, cols], same, True), v[:, cols], 0, 0)
        for head in range(2):
            part = slice(head * HDIM, (head + 1) * HDIM)
            out[2 * pair + head, :HDIM, :] = kv[part, part]
            put_ends(out, 2 * pair + head, docs)


def leading_kernel(docs, grad_out, weight, q, g, out):
    grad = mul(grad_out[...], weight[...], 1, 1).astype(BF16)
    g[...] = grad
    qg = mul(joined(grad, docs[0, 0] == docs[0, 1], False), q[...], 0, 0)
    for head in range(2):
        part = slice(head * HDIM, (head + 1) * HDIM)
        out[head, :HDIM, :] = qg[part, part]
        put_ends(out, head, docs)


def scan_kernel(reverse, part, *rest):
    out = rest[-1]
    base = part.shape[1] - ROWS
    carried = jnp.zeros((HDIM, HDIM), F32)
    near = jnp.full((1, HDIM), -1.0, F32)
    order = range(BLOCKS - 1, -1, -1) if reverse else range(BLOCKS)
    for block in order:
        first = part[block, base + HDIM : base + HDIM + 1, :]
        last = part[block, base + HDIM + 1 : base + HDIM + 2, :]
        entry, leave = (last, first) if reverse else (first, last)
        state = jnp.where(near == entry, carried, 0.0)
        out[block, :HDIM, :] = state
        carried = part[block, base : base + HDIM, :] + jnp.where(first == last, state, 0.0)
        near = leave
    for along in rest[:-1]:
        out[:, HDIM:, :] = along[...]


def causal(same):
    rows = lax.broadcasted_iota(jnp.int32, (TOKENS, TOKENS), 0)
    cols = lax.broadcasted_iota(jnp.int32, (TOKENS, TOKENS), 1)
    return (rows >= cols) & (same | (rows < TILE) | (cols >= TILE))


def attended_kernel(place, docs, q, k, v, state, out, far, up, own, down, turned):
    del place
    step = pl.program_id(0)
    same = docs[0, 0] == docs[0, 1]
    mask = causal(same)
    for head in range(state.shape[0]):
        cols = slice(head * HDIM, (head + 1) * HDIM)
        query = q[:, cols]
        attn = jnp.where(mask, SCALE * mul(query, k[:, cols], 1, 1), 0.0).astype(BF16)
        got = mul(attn, v[:, cols], 1, 0)
        got = got + mul(joined(query, same, False), (SCALE * state[head]).astype(BF16), 1, 0)
        got = got.astype(BF16)
        out[:, cols] = got
        turned[cols, :] = got.astype(F32).T

    for when, wide in enumerate((far, up, own, down)):

        @pl.when(step == when)
        def _(wide=wide):
            wide[...] = turned[...].astype(wide.dtype)


def grads_kernel(docs, q, k, v, g, state, rev, gq, gk, gv):
    same = docs[0, 0] == docs[0, 1]
    mask = causal(same)
    for head in range(state.shape[0]):
        cols = slice(head * HDIM, (head + 1) * HDIM)
        qh, kh, vh, gh = q[:, cols], k[:, cols], v[:, cols], g[:, cols]
        attn_q = jnp.where(mask, SCALE * mul(qh, kh, 1, 1), 0.0).astype(BF16)
        attn_g = jnp.where(mask, SCALE * mul(gh, vh, 1, 1), 0.0).astype(BF16)
        state_b = (SCALE * state[head]).astype(BF16)
        rev_b = (SCALE * rev[head]).astype(BF16)
        gq[:, cols] = (mul(attn_g, kh, 1, 0) + mul(joined(gh, same, False), state_b, 1, 1)).astype(BF16)
        gk[:, cols] = (mul(attn_g, qh, 0, 0) + mul(joined(vh, same, True), rev_b, 1, 0)).astype(BF16)
        gv[:, cols] = (mul(attn_q, gh, 0, 0) + mul(joined(kh, same, True), rev_b, 1, 1)).astype(BF16)


def pack_kernel(own, *rest):
    others, out = rest[:-1], rest[-1]
    out[:TOKENS] = own[...]
    start = TOKENS
    for other in others:
        out[start : start + other.shape[0]] = other[...].astype(BF16)
        start += other.shape[0]


def pack(own, others):
    width = own.shape[1]
    step = 4 * HDIM

    def cols(count):
        return pl.BlockSpec((count, step), lambda i: (0, i))

    return pl.pallas_call(
        pack_kernel,
        grid=(width // step,),
        in_specs=[cols(TOKENS)] + [cols(other.shape[0]) for other in others],
        out_specs=cols(4 * TOKENS),
        out_shape=jax.ShapeDtypeStruct((4 * TOKENS, width), BF16),
        compiler_params=params(SMALL),
        cost_estimate=cost(1 << 20, 12 << 20),
        name="pack",
    )(own, *others)


def product_kernel(side, att_own, att_low, att_high, att_far, gathered, out, left):
    del side

    @pl.when(pl.program_id(0) == 0)
    def _():
        for i, att in enumerate((att_own, att_low, att_high, att_far)):
            left[:, i * TOKENS : (i + 1) * TOKENS] = att[...].astype(BF16)

    total = mul(left[...], gathered[...], 1, 0)
    for block in range(out.shape[0]):
        out[block] = total[:, block * HDIM : (block + 1) * HDIM]


def product(atts, gathered, side):
    width = gathered.shape[1]
    step = 4 * HDIM
    rows = pl.BlockSpec((TOKENS, TOKENS), lambda i, w: (w[0], 0))
    spec = pltpu.PrefetchScalarGridSpec(
        num_scalar_prefetch=1,
        grid=(width // step,),
        in_specs=[rows] * 4 + [pl.BlockSpec((4 * TOKENS, step), lambda i, w: (0, i))],
        out_specs=pl.BlockSpec((step // HDIM, TOKENS, HDIM), lambda i, w: (i, 0, 0)),
        scratch_shapes=[pltpu.VMEM((TOKENS, 4 * TOKENS), BF16)],
    )
    return pl.pallas_call(
        product_kernel,
        grid_spec=spec,
        out_shape=jax.ShapeDtypeStruct((width // HDIM, TOKENS, HDIM), F32),
        compiler_params=params(SMALL),
        cost_estimate=cost(2 * 256 * 1024 * width, 4 * width * 1024),
        name="product",
    )(side.astype(jnp.int32).reshape(1), *atts, gathered)


def ring(step):
    return [(i, (i + step) % 4) for i in range(4)]


def body(queries, keys, values, weight, grad_out, docs):
    ctx = ("x", "z")
    q, k, v, go = queries[0], keys[0], values[0], grad_out[0]
    width = q.shape[1]
    factor = 1.0 / float(TOKENS * 128) ** 0.5

    half = TILE // 2
    cuts = [go[half * i : half * (i + 1)].astype(F32) for i in range(4)]
    top, bottom = go[:TILE].astype(F32), go[TILE:].astype(F32)
    top, bottom, cuts, k, v = lax.optimization_barrier((top, bottom, cuts, k, v))
    low_top = lax.ppermute(top, "y", ring(1))
    high_bottom = lax.ppermute(bottom, "y", ring(-1))
    low_middle = lax.ppermute(cuts[2], "y", ring(1))
    high_middle = lax.ppermute(cuts[1], "y", ring(-1))
    low_rest = lax.ppermute(cuts[3], "y", ring(1))
    high_rest = lax.ppermute(cuts[0], "y", ring(-1))

    per = 2
    block = pl.BlockSpec((TOKENS, per * HDIM), lambda i: (0, i))
    summed = pl.BlockSpec((per, ROWS, HDIM), lambda i: (i, 0, 0))
    matrix = pl.BlockSpec((per, HDIM, HDIM), lambda i: (i, 0, 0))
    tokens = jax.ShapeDtypeStruct((TOKENS, width), BF16)
    payload = jax.ShapeDtypeStruct((HEADS, ROWS, HDIM), F32)

    trailing = pl.pallas_call(
        trailing_kernel,
        grid=(HEADS // 4,),
        in_specs=[SMEM] + [pl.BlockSpec((TOKENS, 4 * HDIM), lambda i: (0, i))] * 2,
        out_specs=pl.BlockSpec((4, ROWS, HDIM), lambda i: (i, 0, 0)),
        out_shape=payload,
        compiler_params=params(),
        cost_estimate=cost(2 * 32 * 128**3, 3 << 20),
        name="trailing",
    )(docs, k, v)
    by_head = lax.all_to_all(trailing, ctx, 0, 0, tiled=True)

    g, leading = pl.pallas_call(
        leading_kernel,
        grid=(HEADS // per,),
        in_specs=[
            SMEM,
            whole((TOKENS, width)),
            pl.BlockSpec((per * HDIM, width), lambda i: (i, 0)),
            block,
        ],
        out_specs=[block, summed],
        out_shape=[tokens, payload],
        compiler_params=params(),
        cost_estimate=cost(2 * 256 * 2048 * 2048, 12 << 20),
        name="leading",
    )(docs, go, weight, q)

    def scan(reverse, *parts):
        return pl.pallas_call(
            functools.partial(scan_kernel, reverse),
            out_shape=jax.ShapeDtypeStruct((BLOCKS, HDIM + ROWS * (len(parts) - 1), HDIM), F32),
            compiler_params=params(SMALL),
            cost_estimate=cost(1 << 20, 2 << 20),
            name="scan",
        )(*parts)

    by_head, leading, low_top, high_bottom, low_middle, high_middle = lax.optimization_barrier(
        (by_head, leading, low_top, high_bottom, low_middle, high_middle)
    )
    far_top = lax.ppermute(low_top, "y", ring(1))
    far_bottom = lax.ppermute(high_bottom, "y", ring(-1))
    both = lax.all_to_all(scan(False, by_head, leading), ctx, 0, 0, tiled=True)
    both, low_rest, high_rest = lax.optimization_barrier((both, low_rest, high_rest))

    def group(i, w):
        return (w[0] + 6 - i) % 4

    place = lax.axis_index("y").astype(jnp.int32).reshape(1)
    four = pl.BlockSpec((TOKENS, 4 * HDIM), lambda i, w: (0, group(i, w)))
    turned = jax.ShapeDtypeStruct((4 * HDIM, TOKENS), F32)
    attended, far, up, att_own, down = pl.pallas_call(
        attended_kernel,
        grid_spec=pltpu.PrefetchScalarGridSpec(
            num_scalar_prefetch=1,
            grid=(HEADS // 4,),
            in_specs=[SMEM, four, four, four, pl.BlockSpec((4, HDIM, HDIM), lambda i, w: (group(i, w), 0, 0))],
            out_specs=[four] + [pl.BlockSpec(part.shape, lambda i, w: (0, 0)) for part in (turned,) * 4],
            scratch_shapes=[pltpu.VMEM((4 * HDIM, TOKENS), F32)],
        ),
        out_shape=[tokens, turned, turned, jax.ShapeDtypeStruct(turned.shape, BF16), turned],
        compiler_params=params(),
        cost_estimate=cost(2 * 32 * 4 * 128**3, 7 << 20),
        name="attended",
    )(place, docs, q, k, v, both)
    behind, attended = lax.optimization_barrier((both, attended))
    rev_scan = scan(True, behind)
    rev = lax.all_to_all(rev_scan, ctx, 0, 0, tiled=True)
    far, up, down, far_top, far_bottom = lax.optimization_barrier((far, up, down, far_top, far_bottom))
    far = lax.ppermute(far, "y", ring(2))
    up = lax.ppermute(up, "y", ring(1))
    down = lax.ppermute(down, "y", ring(-1))
    gathered = pack(
        go, (low_top, low_middle, low_rest, high_rest, high_middle, high_bottom, far_top, far_bottom)
    )

    layer_out = jnp.dot(attended, weight, preferred_element_type=F32).astype(BF16)

    core = lax.axis_index("core")
    gathered, rev = lax.optimization_barrier((gathered, rev))
    atts = (att_own, up, down, far)
    given = product(atts, gathered, 1 - core)
    kept = product(atts, gathered, core)
    taken = lax.ppermute(given, "core", [(0, 1), (1, 0)])
    spread = lax.all_to_all((kept + taken) * factor, ctx, 0, 0, tiled=True)
    grad_weight = jnp.sum(spread, axis=0)

    grad_q, grad_k, grad_v = pl.pallas_call(
        grads_kernel,
        grid=(HEADS // per,),
        in_specs=[SMEM, block, block, block, block, matrix, matrix],
        out_specs=[block, block, block],
        out_shape=[tokens, tokens, tokens],
        compiler_params=params(),
        cost_estimate=cost(2 * 32 * 10 * 128**3, 9 << 20),
        name="grads",
    )(docs, q, k, v, g, both, rev)
    return layer_out[None], grad_q[None], grad_k[None], grad_v[None], grad_weight


def solution(mesh):
    fine = Mesh(mesh.devices.reshape(4, 2, 4, 4), ("y", "core", "x", "z"))
    dp, ctx = ("y", "core"), ("x", "z")
    tokens = P(dp, ctx, None)
    return jax.shard_map(
        body,
        mesh=fine,
        in_specs=(tokens, tokens, tokens, P(), tokens, P(dp, ctx)),
        out_specs=(tokens, tokens, tokens, tokens, P(dp, ctx)),
        check_vma=False,
    )
```

time: 198 us -> 184 us (0.929)
  waiting for transfers between devices: 90.9 us -> 66.3 us
  starting transfers between devices: 36 us -> 48.4 us
  Pallas kernels: 51.4 us -> 39.8 us
  local copies, waits for them, and re-layouts: 3.74 us -> 13.8 us
    ppermute x1, waiting for transfers between devices: 42.6 us -> 1.66 us  [body(): far = lax.ppermute(far, 'y', ring(2))]
    ppermute x2 -> x6, waiting for transfers between devices: 6.62 us -> 38.6 us  [the longest x1 29.9 us: body(): low_rest = lax.ppermute(cuts[3], 'y', ring(1))]
    all_to_all x1, waiting for transfers between devices: 13.8 us -> 1.83 us  [body(): rev = lax.all_to_all(rev_scan, ctx, 0, 0, tiled=True)]
    unnamed x14 -> x32, local copies, waits for them, and re-layouts: 3.74 us -> 13.8 us
    all_to_all x2 -> x1, waiting for transfers between devices: 8.47 us -> 0.01 us  [body(): both = lax.all_to_all(scan(False, by_head, leading), ctx, 0, 0, tiled=True)]
    pallas_call x2, Pallas kernels: 12.4 us -> 4.4 us  [product(): pl.pallas_call(product_kernel, grid_spec=spec, out_shape=jax.ShapeDtypeSt...]
    ppermute x2 -> x6, starting transfers between devices: 2.09 us -> 9.85 us  [the longest x1 3.23 us: body(): high_rest = lax.ppermute(cuts[0], 'y', ring(-1))]
    ppermute x1, waiting for transfers between devices: 0.01 us -> 7.47 us  [body(): up = lax.ppermute(up, 'y', ring(1))]
  transfers between devices with their start and end apart: 13 -> 16, of which waited for: 6 -> 8; matrix products, arithmetic and copies ran while one was open for 3% -> 4% of each run, Pallas kernels for 19% -> 21%
where the time goes in v2:
time: 184 us; the launch traced here: 182 us
  waiting for transfers between devices  66.3 us (36%)
  starting transfers between devices  48.4 us (26%)
  Pallas kernels  39.8 us (22%)
  local copies, waits for them, and re-layouts  13.8 us (8%)
  matrix products  6.68 us (4%)
  other arithmetic  6.63 us (4%)
    ppermute x1, waiting for transfers between devices, body(): low_rest = lax.ppermute(cuts[3], 'y', ring(1))  29.9 us
    all_to_all x1, waiting for transfers between devices, body(): spread = lax.all_to_all((kept + taken) * factor, ctx, 0, 0, tiled=True)  14.5 us
    unnamed x32, local copies, waits for them, and re-layouts  13.8 us
    pallas_call x1, Pallas kernels, body(): pl.pallas_call(leading_kernel, grid=(HEADS // per,), in_specs=[SMEM, whol...  10.4 us
    pallas_call x1, Pallas kernels, body(): pl.pallas_call(grads_kernel, grid=(HEADS // per,), in_specs=[SMEM, block,...  9.93 us
    ppermute x1, waiting for transfers between devices, body(): low_middle = lax.ppermute(cuts[2], 'y', ring(1))  8.71 us
    all_to_all x1, starting transfers between devices, body(): by_head = lax.all_to_all(trailing, ctx, 0, 0, tiled=True)  7.96 us
    all_to_all x1, starting transfers between devices, body(): both = lax.all_to_all(scan(False, by_head, leading), ctx, 0, 0, tiled=True)  7.88 us
  transfers between devices with their start and end apart: 16, of which 8 were waited for; matrix products, arithmetic and copies ran while one was open for 4% of the time, Pallas kernels for 21%

profile of v2, /device:TPU:0, one launch (start us, length us, event | category | flops | bytes accessed | tf_op | source)
XLA Modules:
  0.0 182.4 jit_solution(15086140003158218374)
XLA Ops:
  0.6 0.0 copy-start.4
  0.6 2.7 %bitcast_convert_fusion.2 = (f32[64,2048]{1,0:T(8,128)}, f32[64,2048]{1,0:T(8,128)}, f32[64,2048]{1,0:T(8,128)}, f32[64,2048]{1,0:T(8,128)}) fusion(bf16[1,256,2048]{2,1,0:T(8,128)(2,1)} %param.10), kind=kLoop, calls=%fused_computation.5 | loop fusion | flops 524288 | bytes 3145728 | tf_op jit(solution)/shard_map/convert_element_type | solution.py:210
  3.3 0.0 copy-done.4
  3.3 1.6 bitcast_convert_fusion
  4.9 1.7 collective-permute-start
  6.5 1.6 collective-permute-start.1
  8.1 4.1 %trailing.1 = f32[16,136,128]{2,1,0:T(8,128)} custom-call(s32[1,2]{1,0:T(1,128)} %docs.7, bf16[256,2048]{1,0:T(8,128)(2,1)} %bitcast.34, bf16[256,2048]{1,0:T(8,128)(2,1)} %bitcast.37), custom_call_target="tpu_custom_call" | custom-call | flops 1342177 | bytes 31457 | tf_op jit(solution)/shard_map/trailing/pallas_call | solution.py:227
  12.2 8.0 %all-to-all-start = ((f32[16,136,128]{2,1,0:T(8,128)}), f32[16,136,128]{2,1,0:T(8,128)S(1)}, u32[]{:S(2)}, u32[]{:S(2)}) async-start(f32[16,136,128]{2,1,0:T(8,128)} %trailing.1), calls=%async_computation | async-start | bytes 2228224 | tf_op jit(solution)/shard_map/all_to_all | solution.py:237
  20.2 0.4 collective-permute-start.2
  20.6 2.9 %collective-permute-start.3 = (f32[64,2048]{1,0:T(8,128)}, f32[64,2048]{1,0:T(8,128)}, u32[]{:S(2)}, u32[]{:S(2)}) collective-permute-start(f32[64,2048]{1,0:T(8,128)} %get-tuple-element.47), channel_id=1, source_target_pairs={{0,96},{32,0},{64,32},{96,64},{1,97},{33,1},{65,33},{97,65},{2,98}... | collective-permute-start | bytes 1572872 | tf_op jit(solution)/shard_map/ppermute | solution.py:216
  23.5 10.4 %leading.1 = (bf16[256,2048]{1,0:T(8,128)(2,1)}, f32[16,136,128]{2,1,0:T(8,128)}) custom-call(s32[1,2]{1,0:T(1,128)} %docs.7, bf16[256,2048]{1,0:T(8,128)(2,1)} %bitcast.32, bf16[2048,2048]{1,0:T(8,128)(2,1)} %weight.1, bf16[256,2048]{1,0:T(8,128)(2,1)} %bitcast.40), custom_call_target="tpu_custom_call" | custom-call | flops 21474836 | bytes 125829 | tf_op jit(solution)/shard_map/leading/pallas_call | solution.py:239
  33.9 8.7 %collective-permute-done.2.rest_1_ = f32[64,2048]{1,0:T(8,128)S(1)} collective-permute-done((f32[64,2048]{1,0:T(8,128)}, f32[64,2048]{1,0:T(8,128)S(1)}, u32[]{:S(2)}, u32[]{:S(2)}) %collective-permute-start.2) | collective-permute-done | bytes 524320 | tf_op jit(solution)/shard_map/ppermute | solution.py:215
  42.6 0.8 copy-done.13
  43.4 0.0 collective-permute-done.3.rest_4_
  43.4 0.0 all-to-all-done.part
  43.4 0.0 collective-permute-done.rest_0_
  43.4 0.0 copy-start.9
  43.4 0.0 collective-permute-done.1.rest_5_
  43.4 0.0 copy-start.11
  43.4 0.0 copy-start.7
  43.4 2.0 %copy-done.7 = f32[16,136,128]{2,1,0:T(8,128)S(1)} copy-done((f32[16,136,128]{2,1,0:T(8,128)S(1)}, f32[16,136,128]{2,1,0:T(8,128)}, u32[]{:S(2)}) %copy-start.7) | copy-done | bytes 1114136
  45.4 0.2 scan.2
  45.6 0.0 copy-done.11
  45.6 1.4 copy-done.6
  47.0 7.9 %all-to-all-start.1 = ((f32[16,264,128]{2,1,0:T(8,128)}), f32[16,264,128]{2,1,0:T(8,128)S(1)}, u32[]{:S(2)}, u32[]{:S(2)}) async-start(f32[16,264,128]{2,1,0:T(8,128)} %copy-done.6), calls=%async_computation.1 | async-start | bytes 4325376 | tf_op jit(solution)/shard_map/all_to_all | solution.py:269
  54.9 1.0 collective-permute-start.6
  55.9 2.3 %collective-permute-start.7 = (f32[128,2048]{1,0:T(8,128)}, f32[128,2048]{1,0:T(8,128)}, u32[]{:S(2)}, u32[]{:S(2)}) collective-permute-start(f32[128,2048]{1,0:T(8,128)} %copy-done.11), channel_id=1, source_target_pairs={{0,96},{32,0},{64,32},{96,64},{1,97},{33,1},{65,33},{97,65},{2,98}... | collective-permute-start | bytes 3145736 | tf_op jit(solution)/shard_map/ppermute | solution.py:268
  58.2 0.0 collective-permute-start.4
  58.2 3.2 %collective-permute-start.5 = (f32[64,2048]{1,0:T(8,128)}, f32[64,2048]{1,0:T(8,128)}, u32[]{:S(2)}, u32[]{:S(2)}) collective-permute-start(f32[64,2048]{1,0:T(8,128)} %get-tuple-element.51), channel_id=1, source_target_pairs={{0,96},{32,0},{64,32},{96,64},{1,97},{33,1},{65,33},{97,65},{2,98}... | collective-permute-start | bytes 1572872 | tf_op jit(solution)/shard_map/ppermute | solution.py:218
  61.4 29.9 %collective-permute-done.4.rest_2_ = f32[64,2048]{1,0:T(8,128)} collective-permute-done((f32[64,2048]{1,0:T(8,128)}, f32[64,2048]{1,0:T(8,128)}, u32[]{:S(2)}, u32[]{:S(2)}) %collective-permute-start.4) | collective-permute-done | bytes 524320 | tf_op jit(solution)/shard_map/ppermute | solution.py:217
  91.3 0.0 collective-permute-done.5.rest_3_
  91.3 0.0 all-to-all-done.1.state.part
  91.3 1.4 copy-done.2
  92.7 6.4 %attended.1 = (bf16[256,2048]{1,0:T(8,128)(2,1)}, f32[512,256]{1,0:T(8,128)}, f32[512,256]{1,0:T(8,128)}, bf16[512,256]{1,0:T(8,128)(2,1)}, f32[512,256]{1,0:T(8,128)}) custom-call(s32[1]{0:T(128)} %bitcast.10.place, s32[1,2]{1,0:T(1,128)} %docs.7, bf16[256,2048]{1,0:T(8,128)(2,1)} %bitcast.41, bf16[256,2048]{1,0:T(8,128)(2,1)} %bitcast.35, ...), custom_call_target="tpu_custom_call" | custom-call | flops 5368709 | bytes 73400 | tf_op jit(solution)/shard_map/attended/pallas_call | solution.py:278
  99.1 1.6 copy-done.3
  100.7 1.1 scan.3
  101.8 7.0 %all-to-all-start.2 = ((f32[16,128,128]{2,1,0:T(8,128)}), f32[16,128,128]{2,1,0:T(8,128)}, u32[]{:S(2)}, u32[]{:S(2)}) async-start(f32[16,128,128]{2,1,0:T(8,128)} %scan.3), calls=%async_computation.2 | async-start | bytes 2097152 | tf_op jit(solution)/shard_map/all_to_all | solution.py:294
  108.8 0.0 collective-permute-done.6.rest_6_
  108.8 0.0 collective-permute-done.7.rest_7_
  108.8 2.2 %collective-permute-start.10 = (f32[512,256]{1,0:T(8,128)}, f32[512,256]{1,0:T(8,128)S(1)}, u32[]{:S(2)}, u32[]{:S(2)}) collective-permute-start(f32[512,256]{1,0:T(8,128)} %get-tuple-element.75), channel_id=1, source_target_pairs={{0,64},{32,96},{64,0},{96,32},{1,65},{33,97},{65,1},{97,33},{2,66}... | collective-permute-start | bytes 1572872 | tf_op jit(solution)/shard_map/ppermute | solution.py:296
  111.0 1.9 %collective-permute-start.8 = (f32[512,256]{1,0:T(8,128)}, f32[512,256]{1,0:T(8,128)S(1)}, u32[]{:S(2)}, u32[]{:S(2)}) collective-permute-start(f32[512,256]{1,0:T(8,128)} %get-tuple-element.73), channel_id=1, source_target_pairs={{0,32},{32,64},{64,96},{96,0},{1,33},{33,65},{65,97},{97,1},{2,34}... | collective-permute-start | bytes 1572872 | tf_op jit(solution)/shard_map/ppermute | solution.py:297
  112.9 1.3 collective-permute-start.9
  114.3 0.0 copy-done.14
  114.3 1.2 copy-done.10
  115.5 1.2 copy-done.12
  116.7 3.3 %pack.1.gathered = bf16[1024,2048]{1,0:T(8,128)(2,1)S(1)} custom-call(bf16[256,2048]{1,0:T(8,128)(2,1)S(1)} %bitcast.33, f32[128,2048]{1,0:T(8,128)S(1)} %copy-done.10, f32[64,2048]{1,0:T(8,128)S(1)} %copy-done.14, f32[64,2048]{1,0:T(8,128)} %collective-permute-done.4.rest_2_, f32[64,2048]{1,0:T(8,128)} %collective-permute-done.5.rest_3_, ...), custom_call_target="tpu_custom_call" | custom-call | flops 10485 | bytes 125829 | tf_op jit(solution)/shard_map/pack/pallas_call | solution.py:153
  120.1 2.0 %copy-done = bf16[1024,2048]{1,0:T(8,128)(2,1)} copy-done((bf16[1024,2048]{1,0:T(8,128)(2,1)}, bf16[1024,2048]{1,0:T(8,128)(2,1)S(1)}, u32[]{:S(2)}) %copy-start) | copy-done | bytes 4194328
  122.0 1.8 %all-to-all-done.2.rev = f32[16,128,128]{2,1,0:T(8,128)} async-done(((f32[16,128,128]{2,1,0:T(8,128)}), f32[16,128,128]{2,1,0:T(8,128)}, u32[]{:S(2)}, u32[]{:S(2)}) %all-to-all-start.2) | async-done | bytes 1048608 | tf_op jit(solution)/shard_map/all_to_all | solution.py:294
  123.8 1.7 collective-permute-done.10.att_far
  125.5 7.5 %collective-permute-done.8.att_low = f32[512,256]{1,0:T(8,128)S(1)} collective-permute-done((f32[512,256]{1,0:T(8,128)}, f32[512,256]{1,0:T(8,128)S(1)}, u32[]{:S(2)}, u32[]{:S(2)}) %collective-permute-start.8) | collective-permute-done | bytes 524320 | tf_op jit(solution)/shard_map/ppermute | solution.py:297
  133.0 0.3 collective-permute-done.9.att_high
  133.2 0.0 copy-done.8
  133.2 2.2 %copy-done.1 = bf16[1024,2048]{1,0:T(8,128)(2,1)S(1)} copy-done((bf16[1024,2048]{1,0:T(8,128)(2,1)S(1)}, bf16[1024,2048]{1,0:T(8,128)(2,1)}, u32[]{:S(2)}) %copy-start.1) | copy-done | bytes 4194328
  135.4 2.2 %product.3 = f32[16,256,128]{2,1,0:T(8,128)S(1)} custom-call(s32[1]{0:T(128)} %bitcast.16.side, bf16[512,256]{1,0:T(8,128)(2,1)S(1)} %copy-done.8, f32[512,256]{1,0:T(8,128)S(1)} %collective-permute-done.8.att_low, f32[512,256]{1,0:T(8,128)S(1)} %collective-permute-done.9.att_high, f32[512,256]{1,0:T(8,128)S(1)} %collective-permute-done.10.att_far, ...), custom_call_target="tpu_custom_call" | custom-call | flops 10737418 | bytes 83886 | tf_op jit(solution)/shard_map/product/pallas_call | solution.py:189
  137.6 0.1 collective-permute-start.11
  137.7 2.2 %product.2 = f32[16,256,128]{2,1,0:T(8,128)S(1)} custom-call(s32[1]{0:T(128)} %bitcast.15.side, bf16[512,256]{1,0:T(8,128)(2,1)S(1)} %copy-done.8, f32[512,256]{1,0:T(8,128)S(1)} %collective-permute-done.8.att_low, f32[512,256]{1,0:T(8,128)S(1)} %collective-permute-done.9.att_high, f32[512,256]{1,0:T(8,128)S(1)} %collective-permute-done.10.att_far, ...), custom_call_target="tpu_custom_call" | custom-call | flops 10737418 | bytes 83886 | tf_op jit(solution)/shard_map/product/pallas_call | solution.py:189
  139.9 1.9 %collective-permute-done.11 = f32[16,256,128]{2,1,0:T(8,128)S(1)} collective-permute-done((f32[16,256,128]{2,1,0:T(8,128)S(1)}, f32[16,256,128]{2,1,0:T(8,128)S(1)}, u32[]{:S(2)}, u32[]{:S(2)}) %collective-permute-start.11) | collective-permute-done | bytes 2097184 | tf_op jit(solution)/shard_map/ppermute | solution.py:310
  141.9 1.6 add_multiply_fusion
  143.5 7.0 %all-to-all-start.3 = ((f32[16,256,128]{2,1,0:T(8,128)}), f32[16,256,128]{2,1,0:T(8,128)S(1)}, u32[]{:S(2)}, u32[]{:S(2)}) async-start(f32[16,256,128]{2,1,0:T(8,128)} %add_multiply_fusion), calls=%async_computation.3 | async-start | bytes 4194304 | tf_op jit(solution)/shard_map/all_to_all | solution.py:311
  150.5 0.0 copy-done.15
  150.5 6.7 %fusion = bf16[1,256,2048]{2,1,0:T(8,128)(2,1)} fusion(bf16[256,2048]{1,0:T(8,128)(2,1)S(1)} %copy-done.15, bf16[2048,2048]{1,0:T(8,128)(2,1)} %weight.1), kind=kOutput, calls=%fused_computation.1 | convolution fusion | flops 2148007936 | bytes 10485760 | tf_op jit(solution)/shard_map/dot_general | solution.py:303
  157.2 9.9 %grads.1 = (bf16[256,2048]{1,0:T(8,128)(2,1)}, bf16[256,2048]{1,0:T(8,128)(2,1)}, bf16[256,2048]{1,0:T(8,128)(2,1)}) custom-call(s32[1,2]{1,0:T(1,128)} %docs.7, bf16[256,2048]{1,0:T(8,128)(2,1)} %bitcast.42, bf16[256,2048]{1,0:T(8,128)(2,1)} %bitcast.36, bf16[256,2048]{1,0:T(8,128)(2,1)} %bitcast.39, bf16[256,2048]{1,0:T(8,128)(2,1)} %get-tuple-element.55.g, ...), custom_call_target="tpu_custom_call" | custom-call | flops 13421772 | bytes 94371 | tf_op jit(solution)/shard_map/grads/pallas_call | solution.py:314
  167.2 14.5 %all-to-all-done.3 = f32[16,256,128]{2,1,0:T(8,128)S(1)} async-done(((f32[16,256,128]{2,1,0:T(8,128)}), f32[16,256,128]{2,1,0:T(8,128)S(1)}, u32[]{:S(2)}, u32[]{:S(2)}) %all-to-all-start.3) | async-done | bytes 2097184 | tf_op jit(solution)/shard_map/all_to_all | solution.py:311
  181.7 0.8 reduce_sum.9
  (14 shorter events, 0.0 us)
Async XLA Ops:
  0.6 2.7 %copy-start.4 = (bf16[1,256,2048]{2,1,0:T(8,128)(2,1)S(1)}, bf16[1,256,2048]{2,1,0:T(8,128)(2,1)}, u32[]{:S(2)}) copy-start(bf16[1,256,2048]{2,1,0:T(8,128)(2,1)} %param.10) | copy-start | bytes 3145732
  4.9 38.5 %collective-permute-start = (f32[128,2048]{1,0:T(8,128)}, f32[128,2048]{1,0:T(8,128)S(1)}, u32[]{:S(2)}, u32[]{:S(2)}) collective-permute-start(f32[128,2048]{1,0:T(8,128)} %get-tuple-element.44), channel_id=1, source_target_pairs={{0,32},{32,64},{64,96},{96,0},{1,33},{33,65},{65,97},{97,1},{2,34}... | collective-permute-start | bytes 3145736 | tf_op jit(solution)/shard_map/ppermute | solution.py:213
  6.5 36.9 %collective-permute-start.1 = (f32[128,2048]{1,0:T(8,128)}, f32[128,2048]{1,0:T(8,128)S(1)}, u32[]{:S(2)}, u32[]{:S(2)}) collective-permute-start(f32[128,2048]{1,0:T(8,128)} %get-tuple-element.45), channel_id=1, source_target_pairs={{0,96},{32,0},{64,32},{96,64},{1,97},{33,1},{65,33},{97,65},{2,98}... | collective-permute-start | bytes 3145736 | tf_op jit(solution)/shard_map/ppermute | solution.py:214
  12.2 31.2 %all-to-all-start = ((f32[16,136,128]{2,1,0:T(8,128)}), f32[16,136,128]{2,1,0:T(8,128)S(1)}, u32[]{:S(2)}, u32[]{:S(2)}) async-start(f32[16,136,128]{2,1,0:T(8,128)} %trailing.1), calls=%async_computation | async-start | bytes 2228224 | tf_op jit(solution)/shard_map/all_to_all | solution.py:237
  20.2 22.4 %collective-permute-start.2 = (f32[64,2048]{1,0:T(8,128)}, f32[64,2048]{1,0:T(8,128)S(1)}, u32[]{:S(2)}, u32[]{:S(2)}) collective-permute-start(f32[64,2048]{1,0:T(8,128)} %get-tuple-element.46), channel_id=1, source_target_pairs={{0,32},{32,64},{64,96},{96,0},{1,33},{33,65},{65,97},{97,1},{2,34}... | collective-permute-start | bytes 1572872 | tf_op jit(solution)/shard_map/ppermute | solution.py:215
  20.6 22.8 %collective-permute-start.3 = (f32[64,2048]{1,0:T(8,128)}, f32[64,2048]{1,0:T(8,128)}, u32[]{:S(2)}, u32[]{:S(2)}) collective-permute-start(f32[64,2048]{1,0:T(8,128)} %get-tuple-element.47), channel_id=1, source_target_pairs={{0,96},{32,0},{64,32},{96,64},{1,97},{33,1},{65,33},{97,65},{2,98}... | collective-permute-start | bytes 1572872 | tf_op jit(solution)/shard_map/ppermute | solution.py:216
  42.6 0.8 copy-start.13
  43.4 11.5 %copy-start.9 = (f32[128,2048]{1,0:T(8,128)}, f32[128,2048]{1,0:T(8,128)S(1)}, u32[]{:S(2)}) copy-start(f32[128,2048]{1,0:T(8,128)S(1)} %collective-permute-done.rest_0_) | copy-start | bytes 3145732
  43.4 2.2 %copy-start.11 = (f32[128,2048]{1,0:T(8,128)}, f32[128,2048]{1,0:T(8,128)S(1)}, u32[]{:S(2)}) copy-start(f32[128,2048]{1,0:T(8,128)S(1)} %collective-permute-done.1.rest_5_) | copy-start | bytes 3145732
  43.4 2.0 %copy-start.7 = (f32[16,136,128]{2,1,0:T(8,128)S(1)}, f32[16,136,128]{2,1,0:T(8,128)}, u32[]{:S(2)}) copy-start(f32[16,136,128]{2,1,0:T(8,128)} %get-tuple-element.49.rest_0_) | copy-start | bytes 3342340
  45.6 1.4 copy-start.6
  47.0 44.3 %all-to-all-start.1 = ((f32[16,264,128]{2,1,0:T(8,128)}), f32[16,264,128]{2,1,0:T(8,128)S(1)}, u32[]{:S(2)}, u32[]{:S(2)}) async-start(f32[16,264,128]{2,1,0:T(8,128)} %copy-done.6), calls=%async_computation.1 | async-start | bytes 4325376 | tf_op jit(solution)/shard_map/all_to_all | solution.py:269
  54.9 53.9 %collective-permute-start.6 = (f32[128,2048]{1,0:T(8,128)S(1)}, f32[128,2048]{1,0:T(8,128)}, u32[]{:S(2)}, u32[]{:S(2)}) collective-permute-start(f32[128,2048]{1,0:T(8,128)S(1)} %collective-permute-done.rest_0_), channel_id=1, source_target_pairs={{0,32},{32,64},{64,96},{96,0},{1,33},{33,65},{65,97},{97,1},{2,34}... | collective-permute-start | bytes 3145736 | tf_op jit(solution)/shard_map/ppermute | solution.py:267
  55.9 53.0 %collective-permute-start.7 = (f32[128,2048]{1,0:T(8,128)}, f32[128,2048]{1,0:T(8,128)}, u32[]{:S(2)}, u32[]{:S(2)}) collective-permute-start(f32[128,2048]{1,0:T(8,128)} %copy-done.11), channel_id=1, source_target_pairs={{0,96},{32,0},{64,32},{96,64},{1,97},{33,1},{65,33},{97,65},{2,98}... | collective-permute-start | bytes 3145736 | tf_op jit(solution)/shard_map/ppermute | solution.py:268
  58.2 33.1 %collective-permute-start.4 = (f32[64,2048]{1,0:T(8,128)}, f32[64,2048]{1,0:T(8,128)}, u32[]{:S(2)}, u32[]{:S(2)}) collective-permute-start(f32[64,2048]{1,0:T(8,128)} %get-tuple-element.50), channel_id=1, source_target_pairs={{0,32},{32,64},{64,96},{96,0},{1,33},{33,65},{65,97},{97,1},{2,34}... | collective-permute-start | bytes 1572872 | tf_op jit(solution)/shard_map/ppermute | solution.py:217
  58.2 33.1 %collective-permute-start.5 = (f32[64,2048]{1,0:T(8,128)}, f32[64,2048]{1,0:T(8,128)}, u32[]{:S(2)}, u32[]{:S(2)}) collective-permute-start(f32[64,2048]{1,0:T(8,128)} %get-tuple-element.51), channel_id=1, source_target_pairs={{0,96},{32,0},{64,32},{96,64},{1,97},{33,1},{65,33},{97,65},{2,98}... | collective-permute-start | bytes 1572872 | tf_op jit(solution)/shard_map/ppermute | solution.py:218
  91.3 1.4 copy-start.2
  99.1 1.6 copy-start.3
  100.7 13.5 %copy-start.5 = (bf16[1,256,2048]{2,1,0:T(8,128)(2,1)S(1)}, bf16[1,256,2048]{2,1,0:T(8,128)(2,1)}, u32[]{:S(2)}) copy-start(bf16[1,256,2048]{2,1,0:T(8,128)(2,1)} %param.10) | copy-start | bytes 3145732
  100.7 13.5 %copy-start.14 = (f32[64,2048]{1,0:T(8,128)S(1)}, f32[64,2048]{1,0:T(8,128)}, u32[]{:S(2)}) copy-start(f32[64,2048]{1,0:T(8,128)} %copy-done.13) | copy-start | bytes 1572868
  101.8 22.0 %all-to-all-start.2 = ((f32[16,128,128]{2,1,0:T(8,128)}), f32[16,128,128]{2,1,0:T(8,128)}, u32[]{:S(2)}, u32[]{:S(2)}) async-start(f32[16,128,128]{2,1,0:T(8,128)} %scan.3), calls=%async_computation.2 | async-start | bytes 2097152 | tf_op jit(solution)/shard_map/all_to_all | solution.py:294
  108.8 16.7 %collective-permute-start.10 = (f32[512,256]{1,0:T(8,128)}, f32[512,256]{1,0:T(8,128)S(1)}, u32[]{:S(2)}, u32[]{:S(2)}) collective-permute-start(f32[512,256]{1,0:T(8,128)} %get-tuple-element.75), channel_id=1, source_target_pairs={{0,64},{32,96},{64,0},{96,32},{1,65},{33,97},{65,1},{97,33},{2,66}... | collective-permute-start | bytes 1572872 | tf_op jit(solution)/shard_map/ppermute | solution.py:296
  111.0 21.9 %collective-permute-start.8 = (f32[512,256]{1,0:T(8,128)}, f32[512,256]{1,0:T(8,128)S(1)}, u32[]{:S(2)}, u32[]{:S(2)}) collective-permute-start(f32[512,256]{1,0:T(8,128)} %get-tuple-element.73), channel_id=1, source_target_pairs={{0,32},{32,64},{64,96},{96,0},{1,33},{33,65},{65,97},{97,1},{2,34}... | collective-permute-start | bytes 1572872 | tf_op jit(solution)/shard_map/ppermute | solution.py:297
  112.9 20.3 %collective-permute-start.9 = (f32[512,256]{1,0:T(8,128)}, f32[512,256]{1,0:T(8,128)S(1)}, u32[]{:S(2)}, u32[]{:S(2)}) collective-permute-start(f32[512,256]{1,0:T(8,128)} %get-tuple-element.74), channel_id=1, source_target_pairs={{0,96},{32,0},{64,32},{96,64},{1,97},{33,1},{65,33},{97,65},{2,98}... | collective-permute-start | bytes 1572872 | tf_op jit(solution)/shard_map/ppermute | solution.py:298
  114.3 1.2 copy-start.10
  115.5 1.2 copy-start.12
  116.7 16.5 %copy-start.8 = (bf16[512,256]{1,0:T(8,128)(2,1)S(1)}, bf16[512,256]{1,0:T(8,128)(2,1)}, u32[]{:S(2)}) copy-start(bf16[512,256]{1,0:T(8,128)(2,1)} %get-tuple-element.72.att_own) | copy-start | bytes 786436
  120.0 2.0 %copy-start = (bf16[1024,2048]{1,0:T(8,128)(2,1)}, bf16[1024,2048]{1,0:T(8,128)(2,1)S(1)}, u32[]{:S(2)}) copy-start(bf16[1024,2048]{1,0:T(8,128)(2,1)S(1)} %pack.1.gathered) | copy-start | bytes 12582916
  133.2 2.2 %copy-start.1 = (bf16[1024,2048]{1,0:T(8,128)(2,1)S(1)}, bf16[1024,2048]{1,0:T(8,128)(2,1)}, u32[]{:S(2)}) copy-start(bf16[1024,2048]{1,0:T(8,128)(2,1)} %copy-done) | copy-start | bytes 12582916
  137.6 4.2 %collective-permute-start.11 = (f32[16,256,128]{2,1,0:T(8,128)S(1)}, f32[16,256,128]{2,1,0:T(8,128)S(1)}, u32[]{:S(2)}, u32[]{:S(2)}) collective-permute-start(f32[16,256,128]{2,1,0:T(8,128)S(1)} %product.3), channel_id=1, source_target_pairs={{0,16},{16,0},{1,17},{17,1},{2,18},{18,2},{3,19},{19,3},{4,20},{20... | collective-permute-start | bytes 6291464 | tf_op jit(solution)/shard_map/ppermute | solution.py:310
  143.5 7.0 %copy-start.15 = (bf16[256,2048]{1,0:T(8,128)(2,1)S(1)}, bf16[256,2048]{1,0:T(8,128)(2,1)}, u32[]{:S(2)}) copy-start(bf16[256,2048]{1,0:T(8,128)(2,1)} %get-tuple-element.54) | copy-start | bytes 3145732
  143.5 38.2 %all-to-all-start.3 = ((f32[16,256,128]{2,1,0:T(8,128)}), f32[16,256,128]{2,1,0:T(8,128)S(1)}, u32[]{:S(2)}, u32[]{:S(2)}) async-start(f32[16,256,128]{2,1,0:T(8,128)} %add_multiply_fusion), calls=%async_computation.3 | async-start | bytes 4194304 | tf_op jit(solution)/shard_map/all_to_all | solution.py:311

commit v3 on v2

--- a/solution.py
+++ b/solution.py
@@ -20,6 +20,8 @@
 VMEM = 60 * 1024 * 1024
 SMALL = 24 * 1024 * 1024
 WEIGH = 100
+MIDDLE = 48
+PRODUCT = 15 << 30
 
 
 def mul(a, b, da, db):
@@ -191,7 +193,7 @@
         grid_spec=spec,
         out_shape=jax.ShapeDtypeStruct((width // HDIM, TOKENS, HDIM), F32),
         compiler_params=params(SMALL),
-        cost_estimate=cost(2 * 256 * 1024 * width, 4 * width * 1024),
+        cost_estimate=cost(WEIGH * PRODUCT, WEIGH),
         name="product",
     )(side.astype(jnp.int32).reshape(1), *atts, gathered)
 
@@ -206,8 +208,8 @@
     width = q.shape[1]
     factor = 1.0 / float(TOKENS * 128) ** 0.5
 
-    half = TILE // 2
-    cuts = [go[half * i : half * (i + 1)].astype(F32) for i in range(4)]
+    ends = (0, TILE - MIDDLE, TILE, TILE + MIDDLE, TOKENS)
+    cuts = [go[i:j].astype(F32) for i, j in zip(ends[:-1], ends[1:])]
     top, bottom = go[:TILE].astype(F32), go[TILE:].astype(F32)
     top, bottom, cuts, k, v = lax.optimization_barrier((top, bottom, cuts, k, v))
     low_top = lax.ppermute(top, "y", ring(1))
@@ -267,7 +269,6 @@
     far_top = lax.ppermute(low_top, "y", ring(1))
     far_bottom = lax.ppermute(high_bottom, "y", ring(-1))
     both = lax.all_to_all(scan(False, by_head, leading), ctx, 0, 0, tiled=True)
-    both, low_rest, high_rest = lax.optimization_barrier((both, low_rest, high_rest))
 
     def group(i, w):
         return (w[0] + 6 - i) % 4
@@ -285,14 +286,16 @@
             scratch_shapes=[pltpu.VMEM((4 * HDIM, TOKENS), F32)],
         ),
         out_shape=[tokens, turned, turned, jax.ShapeDtypeStruct(turned.shape, BF16), turned],
-        compiler_params=params(),
+        compiler_params=params(SMALL),
         cost_estimate=cost(2 * 32 * 4 * 128**3, 7 << 20),
         name="attended",
     )(place, docs, q, k, v, both)
     behind, attended = lax.optimization_barrier((both, attended))
     rev_scan = scan(True, behind)
     rev = lax.all_to_all(rev_scan, ctx, 0, 0, tiled=True)
-    far, up, down, far_top, far_bottom = lax.optimization_barrier((far, up, down, far_top, far_bottom))
+    far, up, down, far_top, far_bottom, low_rest, high_rest = lax.optimization_barrier(
+        (far, up, down, far_top, far_bottom, low_rest, high_rest)
+    )
     far = lax.ppermute(far, "y", ring(2))
     up = lax.ppermute(up, "y", ring(1))
     down = lax.ppermute(down, "y", ring(-1))
@@ -303,9 +306,9 @@
     layer_out = jnp.dot(attended, weight, preferred_element_type=F32).astype(BF16)
 
     core = lax.axis_index("core")
-    gathered, rev = lax.optimization_barrier((gathered, rev))
     atts = (att_own, up, down, far)
     given = product(atts, gathered, 1 - core)
+    core, rev = lax.optimization_barrier((core, rev))
     kept = product(atts, gathered, core)
     taken = lax.ppermute(given, "core", [(0, 1), (1, 0)])
     spread = lax.all_to_all((kept + taken) * factor, ctx, 0, 0, tiled=True)

time: 184 us -> 169 us (0.918)
  waiting for transfers between devices: 66.3 us -> 50.4 us
  other arithmetic: 6.63 us -> 9.08 us
    ppermute x1, waiting for transfers between devices: 29.9 us -> 0.17 us  [body(): low_rest = lax.ppermute(cuts[3], 'y', ring(1))]
    all_to_all x1, waiting for transfers between devices: 0.01 us -> 23.1 us  [body(): both = lax.all_to_all(scan(False, by_head, leading), ctx, 0, 0, tiled=True)]
    ppermute x1, waiting for transfers between devices: 7.47 us -> 0.01 us  [body(): up = lax.ppermute(up, 'y', ring(1))]
    ppermute x1, waiting for transfers between devices: 0.26 us -> 5.58 us  [body(): down = lax.ppermute(down, 'y', ring(-1))]
    ppermute x1, waiting for transfers between devices: 8.71 us -> 5.91 us  [body(): low_middle = lax.ppermute(cuts[2], 'y', ring(1))]
    pallas_call x2, Pallas kernels: 4.4 us -> 6.52 us  [product(): pl.pallas_call(product_kernel, grid_spec=spec, out_shape=jax.ShapeDtypeSt...]
    ppermute x1, waiting for transfers between devices: 1.93 us -> 0.01 us  [body(): taken = lax.ppermute(given, 'core', [(0, 1), (1, 0)])]
    unnamed x32 -> x40, local copies, waits for them, and re-layouts: 13.8 us -> 13.9 us
  transfers between devices with their start and end apart: 16 -> 16, of which waited for: 8 -> 6; matrix products, arithmetic and copies ran while one was open for 4% -> 4% of each run, Pallas kernels for 21% -> 24%
where the time goes in v3:
time: 169 us; the launch traced here: 168 us
  waiting for transfers between devices  50.4 us (30%)
  starting transfers between devices  47.3 us (28%)
  Pallas kernels  39.9 us (24%)
  local copies, waits for them, and re-layouts  13.9 us (8%)
  other arithmetic  9.08 us (5%)
  matrix products  6.68 us (4%)
    all_to_all x1, waiting for transfers between devices, body(): both = lax.all_to_all(scan(False, by_head, leading), ctx, 0, 0, tiled=True)  23.1 us
    all_to_all x1, waiting for transfers between devices, body(): spread = lax.all_to_all((kept + taken) * factor, ctx, 0, 0, tiled=True)  14 us
    unnamed x40, local copies, waits for them, and re-layouts  13.9 us
    pallas_call x1, Pallas kernels, body(): pl.pallas_call(leading_kernel, grid=(HEADS // per,), in_specs=[SMEM, whol...  10.4 us
    pallas_call x1, Pallas kernels, body(): pl.pallas_call(grads_kernel, grid=(HEADS // per,), in_specs=[SMEM, block,...  9.92 us
    all_to_all x1, starting transfers between devices, body(): both = lax.all_to_all(scan(False, by_head, leading), ctx, 0, 0, tiled=True)  8.01 us
    all_to_all x1, starting transfers between devices, body(): by_head = lax.all_to_all(trailing, ctx, 0, 0, tiled=True)  7.96 us
    all_to_all x1, starting transfers between devices, body(): rev = lax.all_to_all(rev_scan, ctx, 0, 0, tiled=True)  7.05 us
  transfers between devices with their start and end apart: 16, of which 6 were waited for; matrix products, arithmetic and copies ran while one was open for 4% of the time, Pallas kernels for 24%

profile of v3, /device:TPU:0, one launch (start us, length us, event | category | flops | bytes accessed | tf_op | source)
XLA Modules:
  0.0 168.2 jit_solution(13205463398407242380)
XLA Ops:
  0.6 0.0 copy-start.1
  0.6 2.8 %bitcast_convert_fusion = (f32[128,2048]{1,0:T(8,128)}, f32[128,2048]{1,0:T(8,128)}) fusion(bf16[1,256,2048]{2,1,0:T(8,128)(2,1)} %param.10), kind=kLoop, calls=%fused_computation.3 | loop fusion | flops 524288 | bytes 3145728 | tf_op jit(solution)/shard_map/convert_element_type | solution.py:213
  3.5 1.3 bitcast_convert_fusion.2
  4.8 0.9 bitcast_convert_fusion.4
  5.7 1.7 collective-permute-start
  7.4 1.6 collective-permute-start.1
  9.0 4.1 %trailing.1 = f32[16,136,128]{2,1,0:T(8,128)} custom-call(s32[1,2]{1,0:T(1,128)} %docs.7, bf16[256,2048]{1,0:T(8,128)(2,1)} %bitcast.34, bf16[256,2048]{1,0:T(8,128)(2,1)} %bitcast.37), custom_call_target="tpu_custom_call" | custom-call | flops 1342177 | bytes 31457 | tf_op jit(solution)/shard_map/trailing/pallas_call | solution.py:229
  13.0 8.0 %all-to-all-start = ((f32[16,136,128]{2,1,0:T(8,128)}), f32[16,136,128]{2,1,0:T(8,128)S(1)}, u32[]{:S(2)}, u32[]{:S(2)}) async-start(f32[16,136,128]{2,1,0:T(8,128)} %trailing.1), calls=%async_computation | async-start | bytes 2228224 | tf_op jit(solution)/shard_map/all_to_all | solution.py:239
  21.0 0.4 collective-permute-start.2
  21.4 2.9 %collective-permute-start.3 = (f32[48,2048]{1,0:T(8,128)}, f32[48,2048]{1,0:T(8,128)}, u32[]{:S(2)}, u32[]{:S(2)}) collective-permute-start(f32[48,2048]{1,0:T(8,128)} %get-tuple-element.46), channel_id=1, source_target_pairs={{0,96},{32,0},{64,32},{96,64},{1,97},{33,1},{65,33},{97,65},{2,98}... | collective-permute-start | bytes 1179656 | tf_op jit(solution)/shard_map/ppermute | solution.py:218
  24.3 10.4 %leading.1 = (bf16[256,2048]{1,0:T(8,128)(2,1)}, f32[16,136,128]{2,1,0:T(8,128)}) custom-call(s32[1,2]{1,0:T(1,128)} %docs.7, bf16[256,2048]{1,0:T(8,128)(2,1)} %bitcast.32, bf16[2048,2048]{1,0:T(8,128)(2,1)} %weight.1, bf16[256,2048]{1,0:T(8,128)(2,1)} %bitcast.40), custom_call_target="tpu_custom_call" | custom-call | flops 21474836 | bytes 125829 | tf_op jit(solution)/shard_map/leading/pallas_call | solution.py:241
  34.7 5.9 %collective-permute-done.2.rest_1_ = f32[48,2048]{1,0:T(8,128)S(1)} collective-permute-done((f32[48,2048]{1,0:T(8,128)}, f32[48,2048]{1,0:T(8,128)S(1)}, u32[]{:S(2)}, u32[]{:S(2)}) %collective-permute-start.2) | collective-permute-done | bytes 393248 | tf_op jit(solution)/shard_map/ppermute | solution.py:217
  40.6 0.8 copy-done.15
  41.4 0.0 collective-permute-done.3.rest_4_
  41.4 0.0 all-to-all-done.part
  41.4 0.0 collective-permute-done.rest_0_
  41.4 0.0 copy-start.11
  41.4 0.0 collective-permute-done.1.rest_5_
  41.4 0.0 copy-start.13
  41.4 1.0 copy-done.13
  42.4 1.2 copy-done.10
  43.7 0.2 scan.2
  43.9 1.4 copy-done.6
  45.2 8.0 %all-to-all-start.1 = ((f32[16,264,128]{2,1,0:T(8,128)}), f32[16,264,128]{2,1,0:T(8,128)S(1)}, u32[]{:S(2)}, u32[]{:S(2)}) async-start(f32[16,264,128]{2,1,0:T(8,128)} %copy-done.6), calls=%async_computation.1 | async-start | bytes 4325376 | tf_op jit(solution)/shard_map/all_to_all | solution.py:271
  53.2 1.0 collective-permute-start.4
  54.2 2.3 %collective-permute-start.5 = (f32[128,2048]{1,0:T(8,128)}, f32[128,2048]{1,0:T(8,128)}, u32[]{:S(2)}, u32[]{:S(2)}) collective-permute-start(f32[128,2048]{1,0:T(8,128)} %copy-done.13), channel_id=1, source_target_pairs={{0,96},{32,0},{64,32},{96,64},{1,97},{33,1},{65,33},{97,65},{2,98}... | collective-permute-start | bytes 3145736 | tf_op jit(solution)/shard_map/ppermute | solution.py:270
  56.5 0.0 collective-permute-start.6
  56.5 3.2 %collective-permute-start.7 = (f32[80,2048]{1,0:T(8,128)}, f32[80,2048]{1,0:T(8,128)}, u32[]{:S(2)}, u32[]{:S(2)}) collective-permute-start(f32[80,2048]{1,0:T(8,128)} %get-tuple-element.65), channel_id=1, source_target_pairs={{0,96},{32,0},{64,32},{96,64},{1,97},{33,1},{65,33},{97,65},{2,98}... | collective-permute-start | bytes 1966088 | tf_op jit(solution)/shard_map/ppermute | solution.py:220
  59.8 23.1 %all-to-all-done.1.state.part = f32[16,264,128]{2,1,0:T(8,128)S(1)} async-done(((f32[16,264,128]{2,1,0:T(8,128)}), f32[16,264,128]{2,1,0:T(8,128)S(1)}, u32[]{:S(2)}, u32[]{:S(2)}) %all-to-all-start.1) | async-done | bytes 2162720 | tf_op jit(solution)/shard_map/all_to_all | solution.py:271
  82.9 2.0 %copy-done.4 = bf16[1,256,2048]{2,1,0:T(8,128)(2,1)S(1)} copy-done((bf16[1,256,2048]{2,1,0:T(8,128)(2,1)S(1)}, bf16[1,256,2048]{2,1,0:T(8,128)(2,1)}, u32[]{:S(2)}) %copy-start.4) | copy-done | bytes 1048600
  84.9 1.2 copy-done.5
  86.1 5.4 %attended.1 = (bf16[256,2048]{1,0:T(8,128)(2,1)S(1)}, f32[512,256]{1,0:T(8,128)}, f32[512,256]{1,0:T(8,128)}, bf16[512,256]{1,0:T(8,128)(2,1)S(1)}, f32[512,256]{1,0:T(8,128)}) custom-call(s32[1]{0:T(128)} %bitcast.10.place, s32[1,2]{1,0:T(1,128)S(1)} %copy-done.17, bf16[256,2048]{1,0:T(8,128)(2,1)S(1)} %bitcast.42, bf16[256,2048]{1,0:T(8,128)(2,1)S(1)} %bitcast.36, ...), custom_call_target="tpu_custom_call" | custom-call | flops 5368709 | bytes 73400 | tf_op jit(solution)/shard_map/attended/pallas_call | solution.py:279
  91.6 1.0 copy-done.18
  92.5 0.2 collective-permute-done.6.rest_2_
  92.7 0.0 collective-permute-done.7.rest_3_
  92.7 0.0 collective-permute-done.4.rest_6_
  92.7 0.0 collective-permute-done.5.rest_7_
  92.7 0.5 collective-permute-start.8
  93.2 2.8 %collective-permute-start.9 = (f32[512,256]{1,0:T(8,128)}, f32[512,256]{1,0:T(8,128)}, u32[]{:S(2)}, u32[]{:S(2)}) collective-permute-start(f32[512,256]{1,0:T(8,128)} %get-tuple-element.67), channel_id=1, source_target_pairs={{0,96},{32,0},{64,32},{96,64},{1,97},{33,1},{65,33},{97,65},{2,98}... | collective-permute-start | bytes 1572872 | tf_op jit(solution)/shard_map/ppermute | solution.py:301
  96.0 1.1 collective-permute-start.10
  97.1 0.1 scan.3
  97.2 0.0 copy-start.7
  97.3 1.0 copy-done.7
  98.2 7.1 %all-to-all-start.2 = ((f32[16,128,128]{2,1,0:T(8,128)}), f32[16,128,128]{2,1,0:T(8,128)}, u32[]{:S(2)}, u32[]{:S(2)}) async-start(f32[16,128,128]{2,1,0:T(8,128)} %copy-done.7), calls=%async_computation.2 | async-start | bytes 2097152 | tf_op jit(solution)/shard_map/all_to_all | solution.py:295
  105.3 0.0 copy-start.14
  105.3 1.2 copy-done.14
  106.5 1.0 copy-done.16
  107.5 3.3 %pack.1.gathered = bf16[1024,2048]{1,0:T(8,128)(2,1)S(1)} custom-call(bf16[256,2048]{1,0:T(8,128)(2,1)S(1)} %bitcast.33, f32[128,2048]{1,0:T(8,128)S(1)} %copy-done.12, f32[48,2048]{1,0:T(8,128)S(1)} %copy-done.16, f32[80,2048]{1,0:T(8,128)} %collective-permute-done.6.rest_2_, f32[80,2048]{1,0:T(8,128)} %collective-permute-done.7.rest_3_, ...), custom_call_target="tpu_custom_call" | custom-call | flops 10485 | bytes 125829 | tf_op jit(solution)/shard_map/pack/pallas_call | solution.py:155
  110.9 0.0 copy-start.8
  110.9 0.0 collective-permute-done.8.att_low
  110.9 5.6 %collective-permute-done.9.att_high = f32[512,256]{1,0:T(8,128)} collective-permute-done((f32[512,256]{1,0:T(8,128)}, f32[512,256]{1,0:T(8,128)}, u32[]{:S(2)}, u32[]{:S(2)}) %collective-permute-start.9) | collective-permute-done | bytes 524320 | tf_op jit(solution)/shard_map/ppermute | solution.py:301
  116.5 1.6 collective-permute-done.10.att_far
  118.0 3.3 %product.3 = f32[16,256,128]{2,1,0:T(8,128)S(1)} custom-call(s32[1]{0:T(128)} %bitcast.16.side, bf16[512,256]{1,0:T(8,128)(2,1)S(1)} %get-tuple-element.58.att_own, f32[512,256]{1,0:T(8,128)} %collective-permute-done.8.att_low, f32[512,256]{1,0:T(8,128)} %collective-permute-done.9.att_high, f32[512,256]{1,0:T(8,128)} %collective-permute-done.10.att_far, ...), custom_call_target="tpu_custom_call" | custom-call | flops 16106127360 | bytes 1 | tf_op jit(solution)/shard_map/product/pallas_call | solution.py:191
  121.3 0.1 collective-permute-start.11
  121.4 0.0 all-to-all-done.2.rev
  121.4 2.2 %copy-done.9 = bf16[1024,2048]{1,0:T(8,128)(2,1)S(1)} copy-done((bf16[1024,2048]{1,0:T(8,128)(2,1)S(1)}, bf16[1024,2048]{1,0:T(8,128)(2,1)}, u32[]{:S(2)}) %copy-start.9) | copy-done | bytes 4194328
  123.6 3.3 %product.2 = f32[16,256,128]{2,1,0:T(8,128)S(1)} custom-call(s32[1]{0:T(128)} %bitcast.15.side, bf16[512,256]{1,0:T(8,128)(2,1)S(1)} %get-tuple-element.58.att_own, f32[512,256]{1,0:T(8,128)} %collective-permute-done.8.att_low, f32[512,256]{1,0:T(8,128)} %collective-permute-done.9.att_high, f32[512,256]{1,0:T(8,128)} %collective-permute-done.10.att_far, ...), custom_call_target="tpu_custom_call" | custom-call | flops 16106127360 | bytes 1 | tf_op jit(solution)/shard_map/product/pallas_call | solution.py:191
  126.9 0.0 collective-permute-done.11
  126.9 3.2 %add_multiply_fusion = f32[16,256,128]{2,1,0:T(8,128)} fusion(f32[16,256,128]{2,1,0:T(8,128)S(1)} %product.2, f32[16,256,128]{2,1,0:T(8,128)} %collective-permute-done.11), kind=kLoop, calls=%fused_computation.2 | loop fusion | flops 1048576 | bytes 6291456 | tf_op jit(solution)/shard_map/mul | solution.py:314
  130.1 6.7 %all-to-all-start.3 = ((f32[16,256,128]{2,1,0:T(8,128)}), f32[16,256,128]{2,1,0:T(8,128)S(1)}, u32[]{:S(2)}, u32[]{:S(2)}) async-start(f32[16,256,128]{2,1,0:T(8,128)} %add_multiply_fusion), calls=%async_computation.3 | async-start | bytes 4194304 | tf_op jit(solution)/shard_map/all_to_all | solution.py:314
  136.9 6.7 %fusion = bf16[1,256,2048]{2,1,0:T(8,128)(2,1)} fusion(bf16[256,2048]{1,0:T(8,128)(2,1)S(1)} %copy-done.19, bf16[2048,2048]{1,0:T(8,128)(2,1)} %weight.1), kind=kOutput, calls=%fused_computation.1 | convolution fusion | flops 2148007936 | bytes 10485760 | tf_op jit(solution)/shard_map/dot_general | solution.py:306
  143.5 9.9 %grads.1 = (bf16[256,2048]{1,0:T(8,128)(2,1)}, bf16[256,2048]{1,0:T(8,128)(2,1)}, bf16[256,2048]{1,0:T(8,128)(2,1)}) custom-call(s32[1,2]{1,0:T(1,128)} %docs.7, bf16[256,2048]{1,0:T(8,128)(2,1)} %bitcast.41, bf16[256,2048]{1,0:T(8,128)(2,1)} %bitcast.35, bf16[256,2048]{1,0:T(8,128)(2,1)} %bitcast.38, bf16[256,2048]{1,0:T(8,128)(2,1)} %get-tuple-element.51.g, ...), custom_call_target="tpu_custom_call" | custom-call | flops 13421772 | bytes 94371 | tf_op jit(solution)/shard_map/grads/pallas_call | solution.py:317
  153.5 14.0 %all-to-all-done.3 = f32[16,256,128]{2,1,0:T(8,128)S(1)} async-done(((f32[16,256,128]{2,1,0:T(8,128)}), f32[16,256,128]{2,1,0:T(8,128)S(1)}, u32[]{:S(2)}, u32[]{:S(2)}) %all-to-all-start.3) | async-done | bytes 2097184 | tf_op jit(solution)/shard_map/all_to_all | solution.py:314
  167.4 0.8 reduce_sum.9
  (23 shorter events, 0.0 us)
Async XLA Ops:
  0.6 2.9 %copy-start.1 = (bf16[1,256,2048]{2,1,0:T(8,128)(2,1)S(1)}, bf16[1,256,2048]{2,1,0:T(8,128)(2,1)}, u32[]{:S(2)}) copy-start(bf16[1,256,2048]{2,1,0:T(8,128)(2,1)} %param.10) | copy-start | bytes 3145732
  5.7 35.7 %collective-permute-start = (f32[128,2048]{1,0:T(8,128)}, f32[128,2048]{1,0:T(8,128)S(1)}, u32[]{:S(2)}, u32[]{:S(2)}) collective-permute-start(f32[128,2048]{1,0:T(8,128)} %get-tuple-element.43), channel_id=1, source_target_pairs={{0,32},{32,64},{64,96},{96,0},{1,33},{33,65},{65,97},{97,1},{2,34}... | collective-permute-start | bytes 3145736 | tf_op jit(solution)/shard_map/ppermute | solution.py:215
  7.4 34.0 %collective-permute-start.1 = (f32[128,2048]{1,0:T(8,128)}, f32[128,2048]{1,0:T(8,128)S(1)}, u32[]{:S(2)}, u32[]{:S(2)}) collective-permute-start(f32[128,2048]{1,0:T(8,128)} %get-tuple-element.44), channel_id=1, source_target_pairs={{0,96},{32,0},{64,32},{96,64},{1,97},{33,1},{65,33},{97,65},{2,98}... | collective-permute-start | bytes 3145736 | tf_op jit(solution)/shard_map/ppermute | solution.py:216
  13.0 28.3 %all-to-all-start = ((f32[16,136,128]{2,1,0:T(8,128)}), f32[16,136,128]{2,1,0:T(8,128)S(1)}, u32[]{:S(2)}, u32[]{:S(2)}) async-start(f32[16,136,128]{2,1,0:T(8,128)} %trailing.1), calls=%async_computation | async-start | bytes 2228224 | tf_op jit(solution)/shard_map/all_to_all | solution.py:239
  21.0 19.6 %collective-permute-start.2 = (f32[48,2048]{1,0:T(8,128)}, f32[48,2048]{1,0:T(8,128)S(1)}, u32[]{:S(2)}, u32[]{:S(2)}) collective-permute-start(f32[48,2048]{1,0:T(8,128)} %get-tuple-element.45), channel_id=1, source_target_pairs={{0,32},{32,64},{64,96},{96,0},{1,33},{33,65},{65,97},{97,1},{2,34}... | collective-permute-start | bytes 1179656 | tf_op jit(solution)/shard_map/ppermute | solution.py:217
  21.4 19.9 %collective-permute-start.3 = (f32[48,2048]{1,0:T(8,128)}, f32[48,2048]{1,0:T(8,128)}, u32[]{:S(2)}, u32[]{:S(2)}) collective-permute-start(f32[48,2048]{1,0:T(8,128)} %get-tuple-element.46), channel_id=1, source_target_pairs={{0,96},{32,0},{64,32},{96,64},{1,97},{33,1},{65,33},{97,65},{2,98}... | collective-permute-start | bytes 1179656 | tf_op jit(solution)/shard_map/ppermute | solution.py:218
  40.6 0.8 copy-start.15
  41.4 2.4 %copy-start.11 = (f32[128,2048]{1,0:T(8,128)}, f32[128,2048]{1,0:T(8,128)S(1)}, u32[]{:S(2)}) copy-start(f32[128,2048]{1,0:T(8,128)S(1)} %collective-permute-done.rest_0_) | copy-start | bytes 3145732
  41.4 1.0 copy-start.13
  42.4 1.2 copy-start.10
  43.9 1.4 copy-start.6
  45.2 37.7 %copy-start.3 = (bf16[1,256,2048]{2,1,0:T(8,128)(2,1)S(1)}, bf16[1,256,2048]{2,1,0:T(8,128)(2,1)}, u32[]{:S(2)}) copy-start(bf16[1,256,2048]{2,1,0:T(8,128)(2,1)} %param.7) | copy-start | bytes 3145732
  45.2 37.7 %copy-start.17 = (s32[1,2]{1,0:T(1,128)S(1)}, s32[1,2]{1,0:T(1,128)}, u32[]{:S(2)}) copy-start(s32[1,2]{1,0:T(1,128)} %docs.7) | copy-start | bytes 28
  45.2 37.7 %all-to-all-start.1 = ((f32[16,264,128]{2,1,0:T(8,128)}), f32[16,264,128]{2,1,0:T(8,128)S(1)}, u32[]{:S(2)}, u32[]{:S(2)}) async-start(f32[16,264,128]{2,1,0:T(8,128)} %copy-done.6), calls=%async_computation.1 | async-start | bytes 4325376 | tf_op jit(solution)/shard_map/all_to_all | solution.py:271
  53.2 39.5 %collective-permute-start.4 = (f32[128,2048]{1,0:T(8,128)}, f32[128,2048]{1,0:T(8,128)}, u32[]{:S(2)}, u32[]{:S(2)}) collective-permute-start(f32[128,2048]{1,0:T(8,128)} %copy-done.11), channel_id=1, source_target_pairs={{0,32},{32,64},{64,96},{96,0},{1,33},{33,65},{65,97},{97,1},{2,34}... | collective-permute-start | bytes 3145736 | tf_op jit(solution)/shard_map/ppermute | solution.py:269
  54.2 38.5 %collective-permute-start.5 = (f32[128,2048]{1,0:T(8,128)}, f32[128,2048]{1,0:T(8,128)}, u32[]{:S(2)}, u32[]{:S(2)}) collective-permute-start(f32[128,2048]{1,0:T(8,128)} %copy-done.13), channel_id=1, source_target_pairs={{0,96},{32,0},{64,32},{96,64},{1,97},{33,1},{65,33},{97,65},{2,98}... | collective-permute-start | bytes 3145736 | tf_op jit(solution)/shard_map/ppermute | solution.py:270
  56.5 36.2 %collective-permute-start.6 = (f32[80,2048]{1,0:T(8,128)}, f32[80,2048]{1,0:T(8,128)}, u32[]{:S(2)}, u32[]{:S(2)}) collective-permute-start(f32[80,2048]{1,0:T(8,128)} %get-tuple-element.64), channel_id=1, source_target_pairs={{0,32},{32,64},{64,96},{96,0},{1,33},{33,65},{65,97},{97,1},{2,34}... | collective-permute-start | bytes 1966088 | tf_op jit(solution)/shard_map/ppermute | solution.py:219
  56.5 36.2 %collective-permute-start.7 = (f32[80,2048]{1,0:T(8,128)}, f32[80,2048]{1,0:T(8,128)}, u32[]{:S(2)}, u32[]{:S(2)}) collective-permute-start(f32[80,2048]{1,0:T(8,128)} %get-tuple-element.65), channel_id=1, source_target_pairs={{0,96},{32,0},{64,32},{96,64},{1,97},{33,1},{65,33},{97,65},{2,98}... | collective-permute-start | bytes 1966088 | tf_op jit(solution)/shard_map/ppermute | solution.py:220
  82.9 14.2 %copy-start = (f32[16,264,128]{2,1,0:T(8,128)}, f32[16,264,128]{2,1,0:T(8,128)S(1)}, u32[]{:S(2)}) copy-start(f32[16,264,128]{2,1,0:T(8,128)S(1)} %all-to-all-done.1.state.part) | copy-start | bytes 6488068
  82.9 2.0 %copy-start.4 = (bf16[1,256,2048]{2,1,0:T(8,128)(2,1)S(1)}, bf16[1,256,2048]{2,1,0:T(8,128)(2,1)}, u32[]{:S(2)}) copy-start(bf16[1,256,2048]{2,1,0:T(8,128)(2,1)} %param.8) | copy-start | bytes 3145732
  84.9 1.2 copy-start.5
  91.6 1.0 copy-start.18
  92.7 18.2 %collective-permute-start.8 = (f32[512,256]{1,0:T(8,128)}, f32[512,256]{1,0:T(8,128)}, u32[]{:S(2)}, u32[]{:S(2)}) collective-permute-start(f32[512,256]{1,0:T(8,128)} %get-tuple-element.66), channel_id=1, source_target_pairs={{0,32},{32,64},{64,96},{96,0},{1,33},{33,65},{65,97},{97,1},{2,34}... | collective-permute-start | bytes 1572872 | tf_op jit(solution)/shard_map/ppermute | solution.py:300
  93.2 23.3 %collective-permute-start.9 = (f32[512,256]{1,0:T(8,128)}, f32[512,256]{1,0:T(8,128)}, u32[]{:S(2)}, u32[]{:S(2)}) collective-permute-start(f32[512,256]{1,0:T(8,128)} %get-tuple-element.67), channel_id=1, source_target_pairs={{0,96},{32,0},{64,32},{96,64},{1,97},{33,1},{65,33},{97,65},{2,98}... | collective-permute-start | bytes 1572872 | tf_op jit(solution)/shard_map/ppermute | solution.py:301
  96.0 22.0 %collective-permute-start.10 = (f32[512,256]{1,0:T(8,128)}, f32[512,256]{1,0:T(8,128)}, u32[]{:S(2)}, u32[]{:S(2)}) collective-permute-start(f32[512,256]{1,0:T(8,128)} %get-tuple-element.68), channel_id=1, source_target_pairs={{0,64},{32,96},{64,0},{96,32},{1,65},{33,97},{65,1},{97,33},{2,66}... | collective-permute-start | bytes 1572872 | tf_op jit(solution)/shard_map/ppermute | solution.py:299
  97.1 8.2 %copy-start.2 = (bf16[1,256,2048]{2,1,0:T(8,128)(2,1)S(1)}, bf16[1,256,2048]{2,1,0:T(8,128)(2,1)}, u32[]{:S(2)}) copy-start(bf16[1,256,2048]{2,1,0:T(8,128)(2,1)} %param.10) | copy-start | bytes 3145732
  97.2 1.0 copy-start.7
  98.2 7.1 %copy-start.12 = (f32[128,2048]{1,0:T(8,128)S(1)}, f32[128,2048]{1,0:T(8,128)}, u32[]{:S(2)}) copy-start(f32[128,2048]{1,0:T(8,128)} %copy-done.11) | copy-start | bytes 3145732
  98.2 23.2 %all-to-all-start.2 = ((f32[16,128,128]{2,1,0:T(8,128)}), f32[16,128,128]{2,1,0:T(8,128)}, u32[]{:S(2)}, u32[]{:S(2)}) async-start(f32[16,128,128]{2,1,0:T(8,128)} %copy-done.7), calls=%async_computation.2 | async-start | bytes 2097152 | tf_op jit(solution)/shard_map/all_to_all | solution.py:295
  105.3 1.2 copy-start.14
  106.5 1.0 copy-start.16
  110.9 10.4 %copy-start.8 = (bf16[1024,2048]{1,0:T(8,128)(2,1)}, bf16[1024,2048]{1,0:T(8,128)(2,1)S(1)}, u32[]{:S(2)}) copy-start(bf16[1024,2048]{1,0:T(8,128)(2,1)S(1)} %pack.1.gathered) | copy-start | bytes 12582916
  121.3 5.6 %collective-permute-start.11 = (f32[16,256,128]{2,1,0:T(8,128)S(1)}, f32[16,256,128]{2,1,0:T(8,128)}, u32[]{:S(2)}, u32[]{:S(2)}) collective-permute-start(f32[16,256,128]{2,1,0:T(8,128)S(1)} %product.3), channel_id=1, source_target_pairs={{0,16},{16,0},{1,17},{17,1},{2,18},{18,2},{3,19},{19,3},{4,20},{20... | collective-permute-start | bytes 6291464 | tf_op jit(solution)/shard_map/ppermute | solution.py:313
  121.4 2.2 %copy-start.9 = (bf16[1024,2048]{1,0:T(8,128)(2,1)S(1)}, bf16[1024,2048]{1,0:T(8,128)(2,1)}, u32[]{:S(2)}) copy-start(bf16[1024,2048]{1,0:T(8,128)(2,1)} %copy-done.8) | copy-start | bytes 12582916
  130.1 6.7 %copy-start.19 = (bf16[256,2048]{1,0:T(8,128)(2,1)S(1)}, bf16[256,2048]{1,0:T(8,128)(2,1)}, u32[]{:S(2)}) copy-start(bf16[256,2048]{1,0:T(8,128)(2,1)} %copy-done.18) | copy-start | bytes 3145732
  130.1 37.3 %all-to-all-start.3 = ((f32[16,256,128]{2,1,0:T(8,128)}), f32[16,256,128]{2,1,0:T(8,128)S(1)}, u32[]{:S(2)}, u32[]{:S(2)}) async-start(f32[16,256,128]{2,1,0:T(8,128)} %add_multiply_fusion), calls=%async_computation.3 | async-start | bytes 4194304 | tf_op jit(solution)/shard_map/all_to_all | solution.py:314

commit v4 on v3

--- a/solution.py
+++ b/solution.py
@@ -20,7 +20,6 @@
 VMEM = 60 * 1024 * 1024
 SMALL = 24 * 1024 * 1024
 WEIGH = 100
-MIDDLE = 48
 PRODUCT = 15 << 30
 
 
@@ -208,16 +207,10 @@
     width = q.shape[1]
     factor = 1.0 / float(TOKENS * 128) ** 0.5
 
-    ends = (0, TILE - MIDDLE, TILE, TILE + MIDDLE, TOKENS)
-    cuts = [go[i:j].astype(F32) for i, j in zip(ends[:-1], ends[1:])]
     top, bottom = go[:TILE].astype(F32), go[TILE:].astype(F32)
-    top, bottom, cuts, k, v = lax.optimization_barrier((top, bottom, cuts, k, v))
+    top, bottom, k, v = lax.optimization_barrier((top, bottom, k, v))
     low_top = lax.ppermute(top, "y", ring(1))
     high_bottom = lax.ppermute(bottom, "y", ring(-1))
-    low_middle = lax.ppermute(cuts[2], "y", ring(1))
-    high_middle = lax.ppermute(cuts[1], "y", ring(-1))
-    low_rest = lax.ppermute(cuts[3], "y", ring(1))
-    high_rest = lax.ppermute(cuts[0], "y", ring(-1))
 
     per = 2
     block = pl.BlockSpec((TOKENS, per * HDIM), lambda i: (0, i))
@@ -237,6 +230,9 @@
         name="trailing",
     )(docs, k, v)
     by_head = lax.all_to_all(trailing, ctx, 0, 0, tiled=True)
+
+    low_bottom = lax.ppermute(bottom, "y", ring(1))
+    high_top = lax.ppermute(top, "y", ring(-1))
 
     g, leading = pl.pallas_call(
         leading_kernel,
@@ -263,12 +259,12 @@
             name="scan",
         )(*parts)
 
-    by_head, leading, low_top, high_bottom, low_middle, high_middle = lax.optimization_barrier(
-        (by_head, leading, low_top, high_bottom, low_middle, high_middle)
-    )
+    by_head, leading, low_top, high_bottom = lax.optimization_barrier((by_head, leading, low_top, high_bottom))
     far_top = lax.ppermute(low_top, "y", ring(1))
     far_bottom = lax.ppermute(high_bottom, "y", ring(-1))
-    both = lax.all_to_all(scan(False, by_head, leading), ctx, 0, 0, tiled=True)
+    state = lax.all_to_all(scan(False, by_head), ctx, 0, 0, tiled=True)
+    leading, state, low_bottom, high_top = lax.optimization_barrier((leading, state, low_bottom, high_top))
+    rev_by_head = lax.all_to_all(leading, ctx, 0, 0, tiled=True)
 
     def group(i, w):
         return (w[0] + 6 - i) % 4
@@ -289,23 +285,21 @@
         compiler_params=params(SMALL),
         cost_estimate=cost(2 * 32 * 4 * 128**3, 7 << 20),
         name="attended",
-    )(place, docs, q, k, v, both)
-    behind, attended = lax.optimization_barrier((both, attended))
-    rev_scan = scan(True, behind)
-    rev = lax.all_to_all(rev_scan, ctx, 0, 0, tiled=True)
-    far, up, down, far_top, far_bottom, low_rest, high_rest = lax.optimization_barrier(
-        (far, up, down, far_top, far_bottom, low_rest, high_rest)
-    )
+    )(place, docs, q, k, v, state)
+    rev_scan = scan(True, rev_by_head)
+    far, up, down, far_top, far_bottom = lax.optimization_barrier((far, up, down, far_top, far_bottom))
     far = lax.ppermute(far, "y", ring(2))
     up = lax.ppermute(up, "y", ring(1))
     down = lax.ppermute(down, "y", ring(-1))
     gathered = pack(
-        go, (low_top, low_middle, low_rest, high_rest, high_middle, high_bottom, far_top, far_bottom)
+        go, (low_top, low_bottom, high_top, high_bottom, far_top, far_bottom)
     )
 
     layer_out = jnp.dot(attended, weight, preferred_element_type=F32).astype(BF16)
 
     core = lax.axis_index("core")
+    gathered, rev_scan = lax.optimization_barrier((gathered, rev_scan))
+    rev = lax.all_to_all(rev_scan, ctx, 0, 0, tiled=True)
     atts = (att_own, up, down, far)
     given = product(atts, gathered, 1 - core)
     core, rev = lax.optimization_barrier((core, rev))
@@ -320,10 +314,10 @@
         in_specs=[SMEM, block, block, block, block, matrix, matrix],
         out_specs=[block, block, block],
         out_shape=[tokens, tokens, tokens],
-        compiler_params=params(),
+        compiler_params=params(SMALL),
         cost_estimate=cost(2 * 32 * 10 * 128**3, 9 << 20),
         name="grads",
-    )(docs, q, k, v, g, both, rev)
+    )(docs, q, k, v, g, state, rev)
     return layer_out[None], grad_q[None], grad_k[None], grad_v[None], grad_weight
 
 

time: 169 us -> 159 us (0.941)
  waiting for transfers between devices: 50.4 us -> 43 us
  starting transfers between devices: 47.3 us -> 42.1 us
    all_to_all x1 -> x2, waiting for transfers between devices: 23.1 us -> 3.49 us  [the longest x1 3.49 us: body(): state = lax.all_to_all(scan(False, by_head), ctx, 0, 0, tiled=True)]
    all_to_all x1, waiting for transfers between devices: 0.01 us -> 6.41 us  [body(): rev = lax.all_to_all(rev_scan, ctx, 0, 0, tiled=True)]
    ppermute x1, waiting for transfers between devices: 0.01 us -> 5.5 us  [body(): far_top = lax.ppermute(low_top, 'y', ring(1))]
    all_to_all x1, waiting for transfers between devices: 0.01 us -> 5.27 us  [body(): by_head = lax.all_to_all(trailing, ctx, 0, 0, tiled=True)]
    ppermute x1, waiting for transfers between devices: 5.58 us -> 0.77 us  [body(): down = lax.ppermute(down, 'y', ring(-1))]
    ppermute x4 -> x2, starting transfers between devices: 6.54 us -> 2.09 us  [the longest x1 1.87 us: body(): high_top = lax.ppermute(top, 'y', ring(-1))]
    all_to_all x1, waiting for transfers between devices: 14 us -> 11.6 us  [body(): spread = lax.all_to_all((kept + taken) * factor, ctx, 0, 0, tiled=True)]
    all_to_all x1, starting transfers between devices: 6.72 us -> 4.44 us  [body(): spread = lax.all_to_all((kept + taken) * factor, ctx, 0, 0, tiled=True)]
  transfers between devices with their start and end apart: 16 -> 15, of which waited for: 6 -> 8; matrix products, arithmetic and copies ran while one was open for 4% -> 5% of each run, Pallas kernels for 24% -> 26%
where the time goes in v4:
time: 159 us; the launch traced here: 158 us
  waiting for transfers between devices  43 us (27%)
  starting transfers between devices  42.1 us (26%)
  Pallas kernels  41.1 us (26%)
  local copies, waits for them, and re-layouts  15.2 us (10%)
  other arithmetic  8.3 us (5%)
  matrix products  7.15 us (4%)
    unnamed x34, local copies, waits for them, and re-layouts  15.2 us
    all_to_all x1, waiting for transfers between devices, body(): spread = lax.all_to_all((kept + taken) * factor, ctx, 0, 0, tiled=True)  11.6 us
    pallas_call x1, Pallas kernels, body(): pl.pallas_call(leading_kernel, grid=(HEADS // per,), in_specs=[SMEM, whol...  10.4 us
    pallas_call x1, Pallas kernels, body(): pl.pallas_call(grads_kernel, grid=(HEADS // per,), in_specs=[SMEM, block,...  9.02 us
    ppermute x1, waiting for transfers between devices, body(): high_top = lax.ppermute(top, 'y', ring(-1))  8.29 us
    all_to_all x1, starting transfers between devices, body(): by_head = lax.all_to_all(trailing, ctx, 0, 0, tiled=True)  7.96 us
    all_to_all x1, starting transfers between devices, body(): rev = lax.all_to_all(rev_scan, ctx, 0, 0, tiled=True)  7.93 us
    pallas_call x2, Pallas kernels, product(): pl.pallas_call(product_kernel, grid_spec=spec, out_shape=jax.ShapeDtypeSt...  7.57 us
  transfers between devices with their start and end apart: 15, of which 8 were waited for; matrix products, arithmetic and copies ran while one was open for 5% of the time, Pallas kernels for 26%

profile of v4, /device:TPU:0, one launch (start us, length us, event | category | flops | bytes accessed | tf_op | source)
XLA Modules:
  0.0 157.7 jit_solution(983725950653856904)
XLA Ops:
  0.6 2.8 %bitcast_convert_fusion = (f32[128,2048]{1,0:T(8,128)}, f32[128,2048]{1,0:T(8,128)}) fusion(bf16[1,256,2048]{2,1,0:T(8,128)(2,1)} %param.10), kind=kLoop, calls=%fused_computation.3 | loop fusion | flops 524288 | bytes 3145728 | tf_op jit(solution)/shard_map/convert_element_type | solution.py:210
  3.4 1.7 %collective-permute-start = (f32[128,2048]{1,0:T(8,128)}, f32[128,2048]{1,0:T(8,128)S(1)}, u32[]{:S(2)}, u32[]{:S(2)}) collective-permute-start(f32[128,2048]{1,0:T(8,128)} %get-tuple-element.39), channel_id=1, source_target_pairs={{0,32},{32,64},{64,96},{96,0},{1,33},{33,65},{65,97},{97,1},{2,34}... | collective-permute-start | bytes 3145736 | tf_op jit(solution)/shard_map/ppermute | solution.py:212
  5.1 1.6 %collective-permute-start.1 = (f32[128,2048]{1,0:T(8,128)}, f32[128,2048]{1,0:T(8,128)S(1)}, u32[]{:S(2)}, u32[]{:S(2)}) collective-permute-start(f32[128,2048]{1,0:T(8,128)} %get-tuple-element.40), channel_id=1, source_target_pairs={{0,96},{32,0},{64,32},{96,64},{1,97},{33,1},{65,33},{97,65},{2,98}... | collective-permute-start | bytes 3145736 | tf_op jit(solution)/shard_map/ppermute | solution.py:213
  6.6 4.1 %trailing.1 = f32[16,136,128]{2,1,0:T(8,128)} custom-call(s32[1,2]{1,0:T(1,128)} %docs.7, bf16[256,2048]{1,0:T(8,128)(2,1)} %bitcast.20, bf16[256,2048]{1,0:T(8,128)(2,1)} %bitcast.23), custom_call_target="tpu_custom_call" | custom-call | flops 1342177 | bytes 31457 | tf_op jit(solution)/shard_map/trailing/pallas_call | solution.py:222
  10.7 8.0 %all-to-all-start = ((f32[16,136,128]{2,1,0:T(8,128)}), f32[16,136,128]{2,1,0:T(8,128)S(1)}, u32[]{:S(2)}, u32[]{:S(2)}) async-start(f32[16,136,128]{2,1,0:T(8,128)} %trailing.1), calls=%async_computation | async-start | bytes 2228224 | tf_op jit(solution)/shard_map/all_to_all | solution.py:232
  18.7 1.9 %collective-permute-start.3 = (f32[128,2048]{1,0:T(8,128)}, f32[128,2048]{1,0:T(8,128)}, u32[]{:S(2)}, u32[]{:S(2)}) collective-permute-start(f32[128,2048]{1,0:T(8,128)} %get-tuple-element.39), channel_id=1, source_target_pairs={{0,96},{32,0},{64,32},{96,64},{1,97},{33,1},{65,33},{97,65},{2,98}... | collective-permute-start | bytes 3145736 | tf_op jit(solution)/shard_map/ppermute | solution.py:235
  20.6 0.2 collective-permute-start.2
  20.8 10.4 %leading.1 = (bf16[256,2048]{1,0:T(8,128)(2,1)}, f32[16,136,128]{2,1,0:T(8,128)}) custom-call(s32[1,2]{1,0:T(1,128)} %docs.7, bf16[256,2048]{1,0:T(8,128)(2,1)} %bitcast.29, bf16[2048,2048]{1,0:T(8,128)(2,1)} %weight.1, bf16[256,2048]{1,0:T(8,128)(2,1)} %bitcast.26), custom_call_target="tpu_custom_call" | custom-call | flops 21474836 | bytes 125829 | tf_op jit(solution)/shard_map/leading/pallas_call | solution.py:237
  31.2 5.3 %all-to-all-done.part = f32[16,136,128]{2,1,0:T(8,128)S(1)} async-done(((f32[16,136,128]{2,1,0:T(8,128)}), f32[16,136,128]{2,1,0:T(8,128)S(1)}, u32[]{:S(2)}, u32[]{:S(2)}) %all-to-all-start) | async-done | bytes 1114144 | tf_op jit(solution)/shard_map/all_to_all | solution.py:232
  36.5 0.0 collective-permute-done.rest_0_
  36.5 0.0 collective-permute-done.1.rest_3_
  36.5 0.0 copy-start.13
  36.5 1.0 copy-done.11
  37.4 0.1 scan.2
  37.5 0.0 copy-start.6
  37.6 1.0 copy-done.6
  38.5 0.0 copy-done.13
  38.5 3.8 %all-to-all-start.1 = ((f32[16,128,128]{2,1,0:T(8,128)}), f32[16,128,128]{2,1,0:T(8,128)S(1)}, u32[]{:S(2)}, u32[]{:S(2)}) async-start(f32[16,128,128]{2,1,0:T(8,128)} %copy-done.6), calls=%async_computation.1 | async-start | bytes 2097152 | tf_op jit(solution)/shard_map/all_to_all | solution.py:265
  42.3 0.3 collective-permute-start.4
  42.7 3.0 %collective-permute-start.5 = (f32[128,2048]{1,0:T(8,128)}, f32[128,2048]{1,0:T(8,128)}, u32[]{:S(2)}, u32[]{:S(2)}) collective-permute-start(f32[128,2048]{1,0:T(8,128)} %copy-done.13), channel_id=1, source_target_pairs={{0,96},{32,0},{64,32},{96,64},{1,97},{33,1},{65,33},{97,65},{2,98}... | collective-permute-start | bytes 3145736 | tf_op jit(solution)/shard_map/ppermute | solution.py:264
  45.6 8.3 %collective-permute-done.3.rest_2_ = f32[128,2048]{1,0:T(8,128)} collective-permute-done((f32[128,2048]{1,0:T(8,128)}, f32[128,2048]{1,0:T(8,128)}, u32[]{:S(2)}, u32[]{:S(2)}) %collective-permute-start.3) | collective-permute-done | bytes 1048608 | tf_op jit(solution)/shard_map/ppermute | solution.py:235
  53.9 0.0 collective-permute-done.2.rest_1_
  53.9 3.5 %all-to-all-done.1.state = f32[16,128,128]{2,1,0:T(8,128)S(1)} async-done(((f32[16,128,128]{2,1,0:T(8,128)}), f32[16,128,128]{2,1,0:T(8,128)S(1)}, u32[]{:S(2)}, u32[]{:S(2)}) %all-to-all-start.1) | async-done | bytes 1048608 | tf_op jit(solution)/shard_map/all_to_all | solution.py:265
  57.4 4.4 %all-to-all-start.2 = ((f32[16,136,128]{2,1,0:T(8,128)}), f32[16,136,128]{2,1,0:T(8,128)}, u32[]{:S(2)}, u32[]{:S(2)}) async-start(f32[16,136,128]{2,1,0:T(8,128)} %get-tuple-element.55), calls=%async_computation.2 | async-start | bytes 2228224 | tf_op jit(solution)/shard_map/all_to_all | solution.py:267
  61.9 0.0 copy-done
  61.9 0.0 copy-done.1
  61.9 0.0 copy-done.15
  61.9 0.0 copy-start.2
  61.9 1.2 copy-done.2
  63.1 5.3 %attended.1 = (bf16[256,2048]{1,0:T(8,128)(2,1)S(1)}, f32[512,256]{1,0:T(8,128)}, f32[512,256]{1,0:T(8,128)}, bf16[512,256]{1,0:T(8,128)(2,1)S(1)}, f32[512,256]{1,0:T(8,128)}) custom-call(s32[1]{0:T(128)} %bitcast.place, s32[1,2]{1,0:T(1,128)S(1)} %copy-done.15, bf16[256,2048]{1,0:T(8,128)(2,1)S(1)} %bitcast.27, bf16[256,2048]{1,0:T(8,128)(2,1)S(1)} %bitcast.21, ...), custom_call_target="tpu_custom_call" | custom-call | flops 5368709 | bytes 73400 | tf_op jit(solution)/shard_map/attended/pallas_call | solution.py:275
  68.4 1.0 copy-done.16
  69.4 5.5 %collective-permute-done.4.rest_4_ = f32[128,2048]{1,0:T(8,128)} collective-permute-done((f32[128,2048]{1,0:T(8,128)}, f32[128,2048]{1,0:T(8,128)}, u32[]{:S(2)}, u32[]{:S(2)}) %collective-permute-start.4) | collective-permute-done | bytes 1048608 | tf_op jit(solution)/shard_map/ppermute | solution.py:263
  74.9 0.0 collective-permute-done.5.rest_5_
  74.9 1.6 collective-permute-start.6
  76.5 1.7 %collective-permute-start.7 = (f32[512,256]{1,0:T(8,128)}, f32[512,256]{1,0:T(8,128)}, u32[]{:S(2)}, u32[]{:S(2)}) collective-permute-start(f32[512,256]{1,0:T(8,128)} %get-tuple-element.64), channel_id=1, source_target_pairs={{0,96},{32,0},{64,32},{96,64},{1,97},{33,1},{65,33},{97,65},{2,98}... | collective-permute-start | bytes 1572872 | tf_op jit(solution)/shard_map/ppermute | solution.py:293
  78.2 1.7 %collective-permute-start.8 = (f32[512,256]{1,0:T(8,128)}, f32[512,256]{1,0:T(8,128)}, u32[]{:S(2)}, u32[]{:S(2)}) collective-permute-start(f32[512,256]{1,0:T(8,128)} %get-tuple-element.65), channel_id=1, source_target_pairs={{0,64},{32,96},{64,0},{96,32},{1,65},{33,97},{65,1},{97,33},{2,66}... | collective-permute-start | bytes 1572872 | tf_op jit(solution)/shard_map/ppermute | solution.py:291
  79.9 1.2 copy-done.4
  81.1 1.2 copy-done.12
  82.3 1.2 copy-done.14
  83.5 3.3 %pack.1.gathered = bf16[1024,2048]{1,0:T(8,128)(2,1)S(1)} custom-call(bf16[256,2048]{1,0:T(8,128)(2,1)S(1)} %bitcast.30, f32[128,2048]{1,0:T(8,128)S(1)} %copy-done.12, f32[128,2048]{1,0:T(8,128)} %collective-permute-done.2.rest_1_, f32[128,2048]{1,0:T(8,128)} %collective-permute-done.3.rest_2_, f32[128,2048]{1,0:T(8,128)S(1)} %copy-done.14, ...), custom_call_target="tpu_custom_call" | custom-call | flops 10485 | bytes 125829 | tf_op jit(solution)/shard_map/pack/pallas_call | solution.py:154
  86.8 2.1 %copy-done.7 = bf16[1024,2048]{1,0:T(8,128)(2,1)} copy-done((bf16[1024,2048]{1,0:T(8,128)(2,1)}, bf16[1024,2048]{1,0:T(8,128)(2,1)S(1)}, u32[]{:S(2)}) %copy-start.7) | copy-done | bytes 4194328
  88.9 0.0 all-to-all-done.2.part
  88.9 1.4 scan.3
  90.2 0.0 copy-start.5
  90.2 1.0 copy-done.5
  91.2 7.9 %all-to-all-start.3 = ((f32[16,128,128]{2,1,0:T(8,128)}), f32[16,128,128]{2,1,0:T(8,128)}, u32[]{:S(2)}, u32[]{:S(2)}) async-start(f32[16,128,128]{2,1,0:T(8,128)} %copy-done.5), calls=%async_computation.3 | async-start | bytes 2097152 | tf_op jit(solution)/shard_map/all_to_all | solution.py:302
  99.1 0.0 collective-permute-done.6.att_low
  99.2 0.8 collective-permute-done.7.att_high
  99.9 1.6 collective-permute-done.8.att_far
  101.5 2.2 %copy-done.8 = bf16[1024,2048]{1,0:T(8,128)(2,1)S(1)} copy-done((bf16[1024,2048]{1,0:T(8,128)(2,1)S(1)}, bf16[1024,2048]{1,0:T(8,128)(2,1)}, u32[]{:S(2)}) %copy-start.8) | copy-done | bytes 4194328
  103.7 4.3 %product.3 = f32[16,256,128]{2,1,0:T(8,128)} custom-call(s32[1]{0:T(128)} %bitcast.12.side, bf16[512,256]{1,0:T(8,128)(2,1)S(1)} %get-tuple-element.62.att_own, f32[512,256]{1,0:T(8,128)} %collective-permute-done.6.att_low, f32[512,256]{1,0:T(8,128)} %collective-permute-done.7.att_high, f32[512,256]{1,0:T(8,128)} %collective-permute-done.8.att_far, ...), custom_call_target="tpu_custom_call" | custom-call | flops 16106127360 | bytes 1 | tf_op jit(solution)/shard_map/product/pallas_call | solution.py:190
  108.0 0.0 collective-permute-start.9
  108.0 6.4 %all-to-all-done.3.rev = f32[16,128,128]{2,1,0:T(8,128)} async-done(((f32[16,128,128]{2,1,0:T(8,128)}), f32[16,128,128]{2,1,0:T(8,128)}, u32[]{:S(2)}, u32[]{:S(2)}) %all-to-all-start.3) | async-done | bytes 1048608 | tf_op jit(solution)/shard_map/all_to_all | solution.py:302
  114.4 2.2 %copy-done.9 = bf16[1024,2048]{1,0:T(8,128)(2,1)S(1)} copy-done((bf16[1024,2048]{1,0:T(8,128)(2,1)S(1)}, bf16[1024,2048]{1,0:T(8,128)(2,1)}, u32[]{:S(2)}) %copy-start.9) | copy-done | bytes 4194328
  116.6 3.3 %product.2 = f32[16,256,128]{2,1,0:T(8,128)S(1)} custom-call(s32[1]{0:T(128)} %bitcast.11.side, bf16[512,256]{1,0:T(8,128)(2,1)S(1)} %get-tuple-element.62.att_own, f32[512,256]{1,0:T(8,128)} %collective-permute-done.6.att_low, f32[512,256]{1,0:T(8,128)} %collective-permute-done.7.att_high, f32[512,256]{1,0:T(8,128)} %collective-permute-done.8.att_far, ...), custom_call_target="tpu_custom_call" | custom-call | flops 16106127360 | bytes 1 | tf_op jit(solution)/shard_map/product/pallas_call | solution.py:190
  119.8 0.0 collective-permute-done.9
  119.9 3.2 %add_multiply_fusion = f32[16,256,128]{2,1,0:T(8,128)} fusion(f32[16,256,128]{2,1,0:T(8,128)S(1)} %product.2, f32[16,256,128]{2,1,0:T(8,128)} %collective-permute-done.9), kind=kLoop, calls=%fused_computation.2 | loop fusion | flops 1048576 | bytes 6291456 | tf_op jit(solution)/shard_map/mul | solution.py:308
  123.0 4.4 %all-to-all-start.4 = ((f32[16,256,128]{2,1,0:T(8,128)}), f32[16,256,128]{2,1,0:T(8,128)}, u32[]{:S(2)}, u32[]{:S(2)}) async-start(f32[16,256,128]{2,1,0:T(8,128)} %add_multiply_fusion), calls=%async_computation.4 | async-start | bytes 4194304 | tf_op jit(solution)/shard_map/all_to_all | solution.py:308
  127.5 0.0 copy-start.3
  127.5 0.0 copy-start.10
  127.5 7.1 %fusion = bf16[1,256,2048]{2,1,0:T(8,128)(2,1)} fusion(bf16[256,2048]{1,0:T(8,128)(2,1)} %copy-done.16, bf16[2048,2048]{1,0:T(8,128)(2,1)} %weight.1), kind=kOutput, calls=%fused_computation.1 | convolution fusion | flops 2148007936 | bytes 10485760 | tf_op jit(solution)/shard_map/dot_general | solution.py:298
  134.7 9.0 %grads.1 = (bf16[256,2048]{1,0:T(8,128)(2,1)}, bf16[256,2048]{1,0:T(8,128)(2,1)}, bf16[256,2048]{1,0:T(8,128)(2,1)}) custom-call(s32[1,2]{1,0:T(1,128)S(1)} %copy-done.15, bf16[256,2048]{1,0:T(8,128)(2,1)S(1)} %bitcast.28, bf16[256,2048]{1,0:T(8,128)(2,1)S(1)} %bitcast.22, bf16[256,2048]{1,0:T(8,128)(2,1)S(1)} %bitcast.25, bf16[256,2048]{1,0:T(8,128)(2,1)S(1)} %copy-done.10, ...), custom_call_target="tpu_custom_call" | custom-call | flops 13421772 | bytes 94371 | tf_op jit(solution)/shard_map/grads/pallas_call | solution.py:311
  143.7 11.6 %all-to-all-done.4 = f32[16,256,128]{2,1,0:T(8,128)} async-done(((f32[16,256,128]{2,1,0:T(8,128)}), f32[16,256,128]{2,1,0:T(8,128)}, u32[]{:S(2)}, u32[]{:S(2)}) %all-to-all-start.4) | async-done | bytes 2097184 | tf_op jit(solution)/shard_map/all_to_all | solution.py:308
  155.3 2.4 %reduce_sum.9 = f32[256,128]{1,0:T(8,128)} reduce(f32[16,256,128]{2,1,0:T(8,128)} %all-to-all-done.4, f32[]{:T(128)} %constant.17.clone.1), dimensions={0}, to_apply=%region_0.0 | reduce | flops 491520 | bytes 2228228 | tf_op jit(solution)/shard_map/reduce_sum | solution.py:309
  (13 shorter events, 0.0 us)
Async XLA Ops:
  3.4 33.1 %collective-permute-start = (f32[128,2048]{1,0:T(8,128)}, f32[128,2048]{1,0:T(8,128)S(1)}, u32[]{:S(2)}, u32[]{:S(2)}) collective-permute-start(f32[128,2048]{1,0:T(8,128)} %get-tuple-element.39), channel_id=1, source_target_pairs={{0,32},{32,64},{64,96},{96,0},{1,33},{33,65},{65,97},{97,1},{2,34}... | collective-permute-start | bytes 3145736 | tf_op jit(solution)/shard_map/ppermute | solution.py:212
  5.1 31.4 %collective-permute-start.1 = (f32[128,2048]{1,0:T(8,128)}, f32[128,2048]{1,0:T(8,128)S(1)}, u32[]{:S(2)}, u32[]{:S(2)}) collective-permute-start(f32[128,2048]{1,0:T(8,128)} %get-tuple-element.40), channel_id=1, source_target_pairs={{0,96},{32,0},{64,32},{96,64},{1,97},{33,1},{65,33},{97,65},{2,98}... | collective-permute-start | bytes 3145736 | tf_op jit(solution)/shard_map/ppermute | solution.py:213
  10.7 25.7 %all-to-all-start = ((f32[16,136,128]{2,1,0:T(8,128)}), f32[16,136,128]{2,1,0:T(8,128)S(1)}, u32[]{:S(2)}, u32[]{:S(2)}) async-start(f32[16,136,128]{2,1,0:T(8,128)} %trailing.1), calls=%async_computation | async-start | bytes 2228224 | tf_op jit(solution)/shard_map/all_to_all | solution.py:232
  18.7 35.2 %collective-permute-start.3 = (f32[128,2048]{1,0:T(8,128)}, f32[128,2048]{1,0:T(8,128)}, u32[]{:S(2)}, u32[]{:S(2)}) collective-permute-start(f32[128,2048]{1,0:T(8,128)} %get-tuple-element.39), channel_id=1, source_target_pairs={{0,96},{32,0},{64,32},{96,64},{1,97},{33,1},{65,33},{97,65},{2,98}... | collective-permute-start | bytes 3145736 | tf_op jit(solution)/shard_map/ppermute | solution.py:235
  20.6 33.4 %collective-permute-start.2 = (f32[128,2048]{1,0:T(8,128)}, f32[128,2048]{1,0:T(8,128)}, u32[]{:S(2)}, u32[]{:S(2)}) collective-permute-start(f32[128,2048]{1,0:T(8,128)} %get-tuple-element.40), channel_id=1, source_target_pairs={{0,32},{32,64},{64,96},{96,0},{1,33},{33,65},{65,97},{97,1},{2,34}... | collective-permute-start | bytes 3145736 | tf_op jit(solution)/shard_map/ppermute | solution.py:234
  36.5 1.0 copy-start.11
  36.5 2.1 %copy-start.13 = (f32[128,2048]{1,0:T(8,128)}, f32[128,2048]{1,0:T(8,128)S(1)}, u32[]{:S(2)}) copy-start(f32[128,2048]{1,0:T(8,128)S(1)} %collective-permute-done.1.rest_3_) | copy-start | bytes 3145732
  37.5 1.0 copy-start.6
  38.5 23.4 %copy-start = (bf16[1,256,2048]{2,1,0:T(8,128)(2,1)S(1)}, bf16[1,256,2048]{2,1,0:T(8,128)(2,1)}, u32[]{:S(2)}) copy-start(bf16[1,256,2048]{2,1,0:T(8,128)(2,1)} %param.7) | copy-start | bytes 3145732
  38.5 23.4 %copy-start.1 = (bf16[1,256,2048]{2,1,0:T(8,128)(2,1)S(1)}, bf16[1,256,2048]{2,1,0:T(8,128)(2,1)}, u32[]{:S(2)}) copy-start(bf16[1,256,2048]{2,1,0:T(8,128)(2,1)} %param.8) | copy-start | bytes 3145732
  38.5 23.4 %copy-start.15 = (s32[1,2]{1,0:T(1,128)S(1)}, s32[1,2]{1,0:T(1,128)}, u32[]{:S(2)}) copy-start(s32[1,2]{1,0:T(1,128)} %docs.7) | copy-start | bytes 28
  38.5 18.9 %all-to-all-start.1 = ((f32[16,128,128]{2,1,0:T(8,128)}), f32[16,128,128]{2,1,0:T(8,128)S(1)}, u32[]{:S(2)}, u32[]{:S(2)}) async-start(f32[16,128,128]{2,1,0:T(8,128)} %copy-done.6), calls=%async_computation.1 | async-start | bytes 2097152 | tf_op jit(solution)/shard_map/all_to_all | solution.py:265
  42.3 32.6 %collective-permute-start.4 = (f32[128,2048]{1,0:T(8,128)}, f32[128,2048]{1,0:T(8,128)}, u32[]{:S(2)}, u32[]{:S(2)}) collective-permute-start(f32[128,2048]{1,0:T(8,128)} %copy-done.11), channel_id=1, source_target_pairs={{0,32},{32,64},{64,96},{96,0},{1,33},{33,65},{65,97},{97,1},{2,34}... | collective-permute-start | bytes 3145736 | tf_op jit(solution)/shard_map/ppermute | solution.py:263
  42.7 32.3 %collective-permute-start.5 = (f32[128,2048]{1,0:T(8,128)}, f32[128,2048]{1,0:T(8,128)}, u32[]{:S(2)}, u32[]{:S(2)}) collective-permute-start(f32[128,2048]{1,0:T(8,128)} %copy-done.13), channel_id=1, source_target_pairs={{0,96},{32,0},{64,32},{96,64},{1,97},{33,1},{65,33},{97,65},{2,98}... | collective-permute-start | bytes 3145736 | tf_op jit(solution)/shard_map/ppermute | solution.py:264
  57.4 31.4 %all-to-all-start.2 = ((f32[16,136,128]{2,1,0:T(8,128)}), f32[16,136,128]{2,1,0:T(8,128)}, u32[]{:S(2)}, u32[]{:S(2)}) async-start(f32[16,136,128]{2,1,0:T(8,128)} %get-tuple-element.55), calls=%async_computation.2 | async-start | bytes 2228224 | tf_op jit(solution)/shard_map/all_to_all | solution.py:267
  61.9 1.2 copy-start.2
  68.4 1.0 copy-start.16
  74.9 24.2 %collective-permute-start.6 = (f32[512,256]{1,0:T(8,128)}, f32[512,256]{1,0:T(8,128)}, u32[]{:S(2)}, u32[]{:S(2)}) collective-permute-start(f32[512,256]{1,0:T(8,128)} %get-tuple-element.63), channel_id=1, source_target_pairs={{0,32},{32,64},{64,96},{96,0},{1,33},{33,65},{65,97},{97,1},{2,34}... | collective-permute-start | bytes 1572872 | tf_op jit(solution)/shard_map/ppermute | solution.py:292
  76.5 23.4 %collective-permute-start.7 = (f32[512,256]{1,0:T(8,128)}, f32[512,256]{1,0:T(8,128)}, u32[]{:S(2)}, u32[]{:S(2)}) collective-permute-start(f32[512,256]{1,0:T(8,128)} %get-tuple-element.64), channel_id=1, source_target_pairs={{0,96},{32,0},{64,32},{96,64},{1,97},{33,1},{65,33},{97,65},{2,98}... | collective-permute-start | bytes 1572872 | tf_op jit(solution)/shard_map/ppermute | solution.py:293
  78.2 23.3 %collective-permute-start.8 = (f32[512,256]{1,0:T(8,128)}, f32[512,256]{1,0:T(8,128)}, u32[]{:S(2)}, u32[]{:S(2)}) collective-permute-start(f32[512,256]{1,0:T(8,128)} %get-tuple-element.65), channel_id=1, source_target_pairs={{0,64},{32,96},{64,0},{96,32},{1,65},{33,97},{65,1},{97,33},{2,66}... | collective-permute-start | bytes 1572872 | tf_op jit(solution)/shard_map/ppermute | solution.py:291
  79.9 1.2 copy-start.4
  81.1 1.2 copy-start.12
  82.3 1.2 copy-start.14
  86.8 2.1 %copy-start.7 = (bf16[1024,2048]{1,0:T(8,128)(2,1)}, bf16[1024,2048]{1,0:T(8,128)(2,1)S(1)}, u32[]{:S(2)}) copy-start(bf16[1024,2048]{1,0:T(8,128)(2,1)S(1)} %pack.1.gathered) | copy-start | bytes 12582916
  90.2 1.0 copy-start.5
  91.2 23.2 %all-to-all-start.3 = ((f32[16,128,128]{2,1,0:T(8,128)}), f32[16,128,128]{2,1,0:T(8,128)}, u32[]{:S(2)}, u32[]{:S(2)}) async-start(f32[16,128,128]{2,1,0:T(8,128)} %copy-done.5), calls=%async_computation.3 | async-start | bytes 2097152 | tf_op jit(solution)/shard_map/all_to_all | solution.py:302
  101.5 2.2 %copy-start.8 = (bf16[1024,2048]{1,0:T(8,128)(2,1)S(1)}, bf16[1024,2048]{1,0:T(8,128)(2,1)}, u32[]{:S(2)}) copy-start(bf16[1024,2048]{1,0:T(8,128)(2,1)} %copy-done.7) | copy-start | bytes 12582916
  108.0 11.9 %collective-permute-start.9 = (f32[16,256,128]{2,1,0:T(8,128)}, f32[16,256,128]{2,1,0:T(8,128)}, u32[]{:S(2)}, u32[]{:S(2)}) collective-permute-start(f32[16,256,128]{2,1,0:T(8,128)} %product.3), channel_id=1, source_target_pairs={{0,16},{16,0},{1,17},{17,1},{2,18},{18,2},{3,19},{19,3},{4,20},{20... | collective-permute-start | bytes 6291464 | tf_op jit(solution)/shard_map/ppermute | solution.py:307
  114.4 2.2 %copy-start.9 = (bf16[1024,2048]{1,0:T(8,128)(2,1)S(1)}, bf16[1024,2048]{1,0:T(8,128)(2,1)}, u32[]{:S(2)}) copy-start(bf16[1024,2048]{1,0:T(8,128)(2,1)} %copy-done.7) | copy-start | bytes 12582916
  123.0 32.3 %all-to-all-start.4 = ((f32[16,256,128]{2,1,0:T(8,128)}), f32[16,256,128]{2,1,0:T(8,128)}, u32[]{:S(2)}, u32[]{:S(2)}) async-start(f32[16,256,128]{2,1,0:T(8,128)} %add_multiply_fusion), calls=%async_computation.4 | async-start | bytes 4194304 | tf_op jit(solution)/shard_map/all_to_all | solution.py:308
  127.5 7.2 %copy-start.3 = (bf16[1,256,2048]{2,1,0:T(8,128)(2,1)S(1)}, bf16[1,256,2048]{2,1,0:T(8,128)(2,1)}, u32[]{:S(2)}) copy-start(bf16[1,256,2048]{2,1,0:T(8,128)(2,1)} %param.6) | copy-start | bytes 3145732
  127.5 7.2 %copy-start.10 = (bf16[256,2048]{1,0:T(8,128)(2,1)S(1)}, bf16[256,2048]{1,0:T(8,128)(2,1)}, u32[]{:S(2)}) copy-start(bf16[256,2048]{1,0:T(8,128)(2,1)} %get-tuple-element.45.g) | copy-start | bytes 3145732

commit v5 on v4

--- a/solution.py
+++ b/solution.py
@@ -157,7 +157,7 @@
         in_specs=[cols(TOKENS)] + [cols(other.shape[0]) for other in others],
         out_specs=cols(4 * TOKENS),
         out_shape=jax.ShapeDtypeStruct((4 * TOKENS, width), BF16),
-        compiler_params=params(SMALL),
+        compiler_params=params(),
         cost_estimate=cost(1 << 20, 12 << 20),
         name="pack",
     )(own, *others)
@@ -191,7 +191,7 @@
         product_kernel,
         grid_spec=spec,
         out_shape=jax.ShapeDtypeStruct((width // HDIM, TOKENS, HDIM), F32),
-        compiler_params=params(SMALL),
+        compiler_params=params(),
         cost_estimate=cost(WEIGH * PRODUCT, WEIGH),
         name="product",
     )(side.astype(jnp.int32).reshape(1), *atts, gathered)
@@ -291,6 +291,7 @@
     far = lax.ppermute(far, "y", ring(2))
     up = lax.ppermute(up, "y", ring(1))
     down = lax.ppermute(down, "y", ring(-1))
+    far_top, rev_scan = lax.optimization_barrier((far_top, rev_scan))
     gathered = pack(
         go, (low_top, low_bottom, high_top, high_bottom, far_top, far_bottom)
     )
@@ -298,7 +299,6 @@
     layer_out = jnp.dot(attended, weight, preferred_element_type=F32).astype(BF16)
 
     core = lax.axis_index("core")
-    gathered, rev_scan = lax.optimization_barrier((gathered, rev_scan))
     rev = lax.all_to_all(rev_scan, ctx, 0, 0, tiled=True)
     atts = (att_own, up, down, far)
     given = product(atts, gathered, 1 - core)

time: 159 us -> 158 us (level)
  local copies, waits for them, and re-layouts: 15.2 us -> 5.8 us
  Pallas kernels: 41.1 us -> 46.5 us
  starting transfers between devices: 42.1 us -> 46.8 us
  waiting for transfers between devices: 43 us -> 41 us
    unnamed x34 -> x24, local copies, waits for them, and re-layouts: 15.2 us -> 5.8 us
    ppermute x1, waiting for transfers between devices: 0.01 us -> 7.81 us  [body(): low_bottom = lax.ppermute(bottom, 'y', ring(1))]
    ppermute x1, waiting for transfers between devices: 8.29 us -> 0.51 us  [body(): high_top = lax.ppermute(top, 'y', ring(-1))]
    all_to_all x1, waiting for transfers between devices: 6.41 us -> 0.01 us  [body(): rev = lax.all_to_all(rev_scan, ctx, 0, 0, tiled=True)]
    ppermute x1, waiting for transfers between devices: 0.77 us -> 4.32 us  [body(): down = lax.ppermute(down, 'y', ring(-1))]
    all_to_all x1, starting transfers between devices: 4.44 us -> 7.83 us  [body(): spread = lax.all_to_all((kept + taken) * factor, ctx, 0, 0, tiled=True)]
    pallas_call x2, Pallas kernels: 7.57 us -> 10.8 us  [product(): pl.pallas_call(product_kernel, grid_spec=spec, out_shape=jax.ShapeDtypeSt...]
    all_to_all x1, waiting for transfers between devices: 11.6 us -> 14.4 us  [body(): spread = lax.all_to_all((kept + taken) * factor, ctx, 0, 0, tiled=True)]
  transfers between devices with their start and end apart: 15 -> 15, of which waited for: 8 -> 8; matrix products, arithmetic and copies ran while one was open for 5% -> 5% of each run, Pallas kernels for 26% -> 30%
where the time goes in v5:
time: 158 us; the launch traced here: 157 us
  starting transfers between devices  46.8 us (30%)
  Pallas kernels  46.5 us (29%)
  waiting for transfers between devices  41 us (26%)
  other arithmetic  8.98 us (6%)
  matrix products  7.15 us (5%)
  local copies, waits for them, and re-layouts  5.8 us (4%)
    all_to_all x1, waiting for transfers between devices, body(): spread = lax.all_to_all((kept + taken) * factor, ctx, 0, 0, tiled=True)  14.4 us
    pallas_call x2, Pallas kernels, product(): pl.pallas_call(product_kernel, grid_spec=spec, out_shape=jax.ShapeDtypeSt...  10.8 us
    pallas_call x1, Pallas kernels, body(): pl.pallas_call(leading_kernel, grid=(HEADS // per,), in_specs=[SMEM, whol...  10.4 us
    pallas_call x1, Pallas kernels, body(): pl.pallas_call(grads_kernel, grid=(HEADS // per,), in_specs=[SMEM, block,...  9.06 us
    all_to_all x1, starting transfers between devices, body(): by_head = lax.all_to_all(trailing, ctx, 0, 0, tiled=True)  7.96 us
    all_to_all x1, starting transfers between devices, body(): rev = lax.all_to_all(rev_scan, ctx, 0, 0, tiled=True)  7.93 us
    all_to_all x1, starting transfers between devices, body(): spread = lax.all_to_all((kept + taken) * factor, ctx, 0, 0, tiled=True)  7.83 us
    ppermute x1, waiting for transfers between devices, body(): low_bottom = lax.ppermute(bottom, 'y', ring(1))  7.81 us
  transfers between devices with their start and end apart: 15, of which 8 were waited for; matrix products, arithmetic and copies ran while one was open for 5% of the time, Pallas kernels for 30%

profile of v5, /device:TPU:0, one launch (start us, length us, event | category | flops | bytes accessed | tf_op | source)
XLA Modules:
  0.0 157.0 jit_solution(6557878904195072010)
XLA Ops:
  0.6 2.8 %bitcast_convert_fusion = (f32[128,2048]{1,0:T(8,128)}, f32[128,2048]{1,0:T(8,128)}) fusion(bf16[1,256,2048]{2,1,0:T(8,128)(2,1)} %param.10), kind=kLoop, calls=%fused_computation.3 | loop fusion | flops 524288 | bytes 3145728 | tf_op jit(solution)/shard_map/convert_element_type | solution.py:210
  3.4 1.7 %collective-permute-start = (f32[128,2048]{1,0:T(8,128)}, f32[128,2048]{1,0:T(8,128)S(1)}, u32[]{:S(2)}, u32[]{:S(2)}) collective-permute-start(f32[128,2048]{1,0:T(8,128)} %get-tuple-element.39), channel_id=1, source_target_pairs={{0,32},{32,64},{64,96},{96,0},{1,33},{33,65},{65,97},{97,1},{2,34}... | collective-permute-start | bytes 3145736 | tf_op jit(solution)/shard_map/ppermute | solution.py:212
  5.1 1.6 %collective-permute-start.1 = (f32[128,2048]{1,0:T(8,128)}, f32[128,2048]{1,0:T(8,128)S(1)}, u32[]{:S(2)}, u32[]{:S(2)}) collective-permute-start(f32[128,2048]{1,0:T(8,128)} %get-tuple-element.40), channel_id=1, source_target_pairs={{0,96},{32,0},{64,32},{96,64},{1,97},{33,1},{65,33},{97,65},{2,98}... | collective-permute-start | bytes 3145736 | tf_op jit(solution)/shard_map/ppermute | solution.py:213
  6.6 4.1 %trailing.1 = f32[16,136,128]{2,1,0:T(8,128)} custom-call(s32[1,2]{1,0:T(1,128)} %docs.7, bf16[256,2048]{1,0:T(8,128)(2,1)} %bitcast.20, bf16[256,2048]{1,0:T(8,128)(2,1)} %bitcast.23), custom_call_target="tpu_custom_call" | custom-call | flops 1342177 | bytes 31457 | tf_op jit(solution)/shard_map/trailing/pallas_call | solution.py:222
  10.7 8.0 %all-to-all-start = ((f32[16,136,128]{2,1,0:T(8,128)}), f32[16,136,128]{2,1,0:T(8,128)S(1)}, u32[]{:S(2)}, u32[]{:S(2)}) async-start(f32[16,136,128]{2,1,0:T(8,128)} %trailing.1), calls=%async_computation | async-start | bytes 2228224 | tf_op jit(solution)/shard_map/all_to_all | solution.py:232
  18.7 0.4 collective-permute-start.2
  19.1 2.9 %collective-permute-start.3 = (f32[128,2048]{1,0:T(8,128)}, f32[128,2048]{1,0:T(8,128)}, u32[]{:S(2)}, u32[]{:S(2)}) collective-permute-start(f32[128,2048]{1,0:T(8,128)} %get-tuple-element.39), channel_id=1, source_target_pairs={{0,96},{32,0},{64,32},{96,64},{1,97},{33,1},{65,33},{97,65},{2,98}... | collective-permute-start | bytes 3145736 | tf_op jit(solution)/shard_map/ppermute | solution.py:235
  22.0 10.4 %leading.1 = (bf16[256,2048]{1,0:T(8,128)(2,1)}, f32[16,136,128]{2,1,0:T(8,128)}) custom-call(s32[1,2]{1,0:T(1,128)} %docs.7, bf16[256,2048]{1,0:T(8,128)(2,1)} %bitcast.29, bf16[2048,2048]{1,0:T(8,128)(2,1)} %weight.1, bf16[256,2048]{1,0:T(8,128)(2,1)} %bitcast.26), custom_call_target="tpu_custom_call" | custom-call | flops 21474836 | bytes 125829 | tf_op jit(solution)/shard_map/leading/pallas_call | solution.py:237
  32.3 4.1 %all-to-all-done.part = f32[16,136,128]{2,1,0:T(8,128)S(1)} async-done(((f32[16,136,128]{2,1,0:T(8,128)}), f32[16,136,128]{2,1,0:T(8,128)S(1)}, u32[]{:S(2)}, u32[]{:S(2)}) %all-to-all-start) | async-done | bytes 1114144 | tf_op jit(solution)/shard_map/all_to_all | solution.py:232
  36.4 0.0 collective-permute-done.rest_0_
  36.4 0.0 copy-start.10
  36.4 0.0 collective-permute-done.1.rest_3_
  36.4 0.0 copy-start.11
  36.5 0.9 copy-done.10
  37.4 0.1 scan.2
  37.5 0.0 copy-start.5
  37.5 1.0 copy-done.5
  38.5 0.0 copy-start
  38.5 0.0 copy-start.1
  38.5 0.0 copy-done.11
  38.5 3.8 %all-to-all-start.1 = ((f32[16,128,128]{2,1,0:T(8,128)}), f32[16,128,128]{2,1,0:T(8,128)S(1)}, u32[]{:S(2)}, u32[]{:S(2)}) async-start(f32[16,128,128]{2,1,0:T(8,128)} %copy-done.5), calls=%async_computation.1 | async-start | bytes 2097152 | tf_op jit(solution)/shard_map/all_to_all | solution.py:265
  42.3 0.3 collective-permute-start.4
  42.6 3.0 %collective-permute-start.5 = (f32[128,2048]{1,0:T(8,128)}, f32[128,2048]{1,0:T(8,128)}, u32[]{:S(2)}, u32[]{:S(2)}) collective-permute-start(f32[128,2048]{1,0:T(8,128)} %copy-done.11), channel_id=1, source_target_pairs={{0,96},{32,0},{64,32},{96,64},{1,97},{33,1},{65,33},{97,65},{2,98}... | collective-permute-start | bytes 3145736 | tf_op jit(solution)/shard_map/ppermute | solution.py:264
  45.6 7.8 %collective-permute-done.2.rest_1_ = f32[128,2048]{1,0:T(8,128)} collective-permute-done((f32[128,2048]{1,0:T(8,128)}, f32[128,2048]{1,0:T(8,128)}, u32[]{:S(2)}, u32[]{:S(2)}) %collective-permute-start.2) | collective-permute-done | bytes 1048608 | tf_op jit(solution)/shard_map/ppermute | solution.py:234
  53.4 0.5 collective-permute-done.3.rest_2_
  53.9 3.5 %all-to-all-done.1.state = f32[16,128,128]{2,1,0:T(8,128)S(1)} async-done(((f32[16,128,128]{2,1,0:T(8,128)}), f32[16,128,128]{2,1,0:T(8,128)S(1)}, u32[]{:S(2)}, u32[]{:S(2)}) %all-to-all-start.1) | async-done | bytes 1048608 | tf_op jit(solution)/shard_map/all_to_all | solution.py:265
  57.4 4.5 %all-to-all-start.2 = ((f32[16,136,128]{2,1,0:T(8,128)}), f32[16,136,128]{2,1,0:T(8,128)}, u32[]{:S(2)}, u32[]{:S(2)}) async-start(f32[16,136,128]{2,1,0:T(8,128)} %get-tuple-element.52), calls=%async_computation.2 | async-start | bytes 2228224 | tf_op jit(solution)/shard_map/all_to_all | solution.py:267
  61.9 0.0 copy-done
  61.9 0.0 copy-done.1
  61.9 0.0 copy-done.7
  61.9 0.0 copy-start.2
  61.9 1.2 copy-done.2
  63.1 5.3 %attended.1 = (bf16[256,2048]{1,0:T(8,128)(2,1)S(1)}, f32[512,256]{1,0:T(8,128)}, f32[512,256]{1,0:T(8,128)}, bf16[512,256]{1,0:T(8,128)(2,1)S(1)}, f32[512,256]{1,0:T(8,128)}) custom-call(s32[1]{0:T(128)} %bitcast.place, s32[1,2]{1,0:T(1,128)S(1)} %copy-done.7, bf16[256,2048]{1,0:T(8,128)(2,1)S(1)} %bitcast.27, bf16[256,2048]{1,0:T(8,128)(2,1)S(1)} %bitcast.21, ...), custom_call_target="tpu_custom_call" | custom-call | flops 5368709 | bytes 73400 | tf_op jit(solution)/shard_map/attended/pallas_call | solution.py:275
  68.4 1.0 copy-done.8
  69.4 0.7 copy-done.9
  70.1 4.8 %collective-permute-done.4.rest_4_ = f32[128,2048]{1,0:T(8,128)} collective-permute-done((f32[128,2048]{1,0:T(8,128)}, f32[128,2048]{1,0:T(8,128)}, u32[]{:S(2)}, u32[]{:S(2)}) %collective-permute-start.4) | collective-permute-done | bytes 1048608 | tf_op jit(solution)/shard_map/ppermute | solution.py:263
  74.9 0.0 collective-permute-done.5.rest_5_
  74.9 1.6 %collective-permute-start.6 = (f32[512,256]{1,0:T(8,128)}, f32[512,256]{1,0:T(8,128)}, u32[]{:S(2)}, u32[]{:S(2)}) collective-permute-start(f32[512,256]{1,0:T(8,128)} %get-tuple-element.60), channel_id=1, source_target_pairs={{0,32},{32,64},{64,96},{96,0},{1,33},{33,65},{65,97},{97,1},{2,34}... | collective-permute-start | bytes 1572872 | tf_op jit(solution)/shard_map/ppermute | solution.py:292
  76.5 1.7 %collective-permute-start.7 = (f32[512,256]{1,0:T(8,128)}, f32[512,256]{1,0:T(8,128)}, u32[]{:S(2)}, u32[]{:S(2)}) collective-permute-start(f32[512,256]{1,0:T(8,128)} %get-tuple-element.61), channel_id=1, source_target_pairs={{0,96},{32,0},{64,32},{96,64},{1,97},{33,1},{65,33},{97,65},{2,98}... | collective-permute-start | bytes 1572872 | tf_op jit(solution)/shard_map/ppermute | solution.py:293
  78.2 1.7 %collective-permute-start.8 = (f32[512,256]{1,0:T(8,128)}, f32[512,256]{1,0:T(8,128)}, u32[]{:S(2)}, u32[]{:S(2)}) collective-permute-start(f32[512,256]{1,0:T(8,128)} %get-tuple-element.62), channel_id=1, source_target_pairs={{0,64},{32,96},{64,0},{96,32},{1,65},{33,97},{65,1},{97,33},{2,66}... | collective-permute-start | bytes 1572872 | tf_op jit(solution)/shard_map/ppermute | solution.py:291
  79.9 0.0 all-to-all-done.2.part
  79.9 1.4 scan.3
  81.2 0.0 copy-start.4
  81.2 1.0 copy-done.4
  82.2 7.9 %all-to-all-start.3 = ((f32[16,128,128]{2,1,0:T(8,128)}), f32[16,128,128]{2,1,0:T(8,128)}, u32[]{:S(2)}, u32[]{:S(2)}) async-start(f32[16,128,128]{2,1,0:T(8,128)} %copy-done.4), calls=%async_computation.3 | async-start | bytes 2097152 | tf_op jit(solution)/shard_map/all_to_all | solution.py:302
  90.1 5.5 %pack.1.gathered = bf16[1024,2048]{1,0:T(8,128)(2,1)} custom-call(bf16[256,2048]{1,0:T(8,128)(2,1)} %bitcast.30, f32[128,2048]{1,0:T(8,128)} %copy-done.10, f32[128,2048]{1,0:T(8,128)} %collective-permute-done.2.rest_1_, f32[128,2048]{1,0:T(8,128)} %collective-permute-done.3.rest_2_, f32[128,2048]{1,0:T(8,128)} %copy-done.11, ...), custom_call_target="tpu_custom_call" | custom-call | flops 10485 | bytes 125829 | tf_op jit(solution)/shard_map/pack/pallas_call | solution.py:154
  95.6 0.0 collective-permute-done.6.att_low
  95.6 4.3 %collective-permute-done.7.att_high = f32[512,256]{1,0:T(8,128)} collective-permute-done((f32[512,256]{1,0:T(8,128)}, f32[512,256]{1,0:T(8,128)}, u32[]{:S(2)}, u32[]{:S(2)}) %collective-permute-start.7) | collective-permute-done | bytes 524320 | tf_op jit(solution)/shard_map/ppermute | solution.py:293
  99.9 1.6 collective-permute-done.8.att_far
  101.5 5.4 %product.3 = f32[16,256,128]{2,1,0:T(8,128)} custom-call(s32[1]{0:T(128)} %bitcast.12.side, bf16[512,256]{1,0:T(8,128)(2,1)} %copy-done.9, f32[512,256]{1,0:T(8,128)} %collective-permute-done.6.att_low, f32[512,256]{1,0:T(8,128)} %collective-permute-done.7.att_high, f32[512,256]{1,0:T(8,128)} %collective-permute-done.8.att_far, bf16[1024,2048]{1,0:T(8,128)(2,1)} %pack.1.gathered), custom_call_target="tpu_custom_call" | custom-call | flops 16106127360 | bytes 1 | tf_op jit(solution)/shard_map/product/pallas_call | solution.py:190
  106.9 0.0 collective-permute-start.9
  106.9 0.0 all-to-all-done.3.rev
  106.9 5.4 %product.2 = f32[16,256,128]{2,1,0:T(8,128)} custom-call(s32[1]{0:T(128)} %bitcast.11.side, bf16[512,256]{1,0:T(8,128)(2,1)} %copy-done.9, f32[512,256]{1,0:T(8,128)} %collective-permute-done.6.att_low, f32[512,256]{1,0:T(8,128)} %collective-permute-done.7.att_high, f32[512,256]{1,0:T(8,128)} %collective-permute-done.8.att_far, bf16[1024,2048]{1,0:T(8,128)(2,1)} %pack.1.gathered), custom_call_target="tpu_custom_call" | custom-call | flops 16106127360 | bytes 1 | tf_op jit(solution)/shard_map/product/pallas_call | solution.py:190
  112.3 0.0 collective-permute-done.9
  112.3 3.9 %add_multiply_fusion = f32[16,256,128]{2,1,0:T(8,128)} fusion(f32[16,256,128]{2,1,0:T(8,128)} %product.2, f32[16,256,128]{2,1,0:T(8,128)} %collective-permute-done.9), kind=kLoop, calls=%fused_computation.2 | loop fusion | flops 1048576 | bytes 6291456 | tf_op jit(solution)/shard_map/mul | solution.py:308
  116.2 7.8 %all-to-all-start.4 = ((f32[16,256,128]{2,1,0:T(8,128)}), f32[16,256,128]{2,1,0:T(8,128)}, u32[]{:S(2)}, u32[]{:S(2)}) async-start(f32[16,256,128]{2,1,0:T(8,128)} %add_multiply_fusion), calls=%async_computation.4 | async-start | bytes 4194304 | tf_op jit(solution)/shard_map/all_to_all | solution.py:308
  124.0 0.0 copy-start.3
  124.0 0.0 copy-start.6
  124.0 7.1 %fusion = bf16[1,256,2048]{2,1,0:T(8,128)(2,1)} fusion(bf16[256,2048]{1,0:T(8,128)(2,1)} %copy-done.8, bf16[2048,2048]{1,0:T(8,128)(2,1)} %weight.1), kind=kOutput, calls=%fused_computation.1 | convolution fusion | flops 2148007936 | bytes 10485760 | tf_op jit(solution)/shard_map/dot_general | solution.py:299
  131.2 0.0 copy-done.3
  131.2 0.0 copy-done.6
  131.2 9.1 %grads.1 = (bf16[256,2048]{1,0:T(8,128)(2,1)}, bf16[256,2048]{1,0:T(8,128)(2,1)}, bf16[256,2048]{1,0:T(8,128)(2,1)}) custom-call(s32[1,2]{1,0:T(1,128)S(1)} %copy-done.7, bf16[256,2048]{1,0:T(8,128)(2,1)S(1)} %bitcast.28, bf16[256,2048]{1,0:T(8,128)(2,1)S(1)} %bitcast.22, bf16[256,2048]{1,0:T(8,128)(2,1)S(1)} %bitcast.25, bf16[256,2048]{1,0:T(8,128)(2,1)S(1)} %copy-done.6, ...), custom_call_target="tpu_custom_call" | custom-call | flops 13421772 | bytes 94371 | tf_op jit(solution)/shard_map/grads/pallas_call | solution.py:311
  140.2 14.4 %all-to-all-done.4 = f32[16,256,128]{2,1,0:T(8,128)} async-done(((f32[16,256,128]{2,1,0:T(8,128)}), f32[16,256,128]{2,1,0:T(8,128)}, u32[]{:S(2)}, u32[]{:S(2)}) %all-to-all-start.4) | async-done | bytes 2097184 | tf_op jit(solution)/shard_map/all_to_all | solution.py:308
  154.7 2.4 %reduce_sum.9 = f32[256,128]{1,0:T(8,128)} reduce(f32[16,256,128]{2,1,0:T(8,128)} %all-to-all-done.4, f32[]{:T(128)} %constant.17.clone.1), dimensions={0}, to_apply=%region_0.0 | reduce | flops 491520 | bytes 2228228 | tf_op jit(solution)/shard_map/reduce_sum | solution.py:309
  (3 shorter events, 0.0 us)
Async XLA Ops:
  3.4 33.0 %collective-permute-start = (f32[128,2048]{1,0:T(8,128)}, f32[128,2048]{1,0:T(8,128)S(1)}, u32[]{:S(2)}, u32[]{:S(2)}) collective-permute-start(f32[128,2048]{1,0:T(8,128)} %get-tuple-element.39), channel_id=1, source_target_pairs={{0,32},{32,64},{64,96},{96,0},{1,33},{33,65},{65,97},{97,1},{2,34}... | collective-permute-start | bytes 3145736 | tf_op jit(solution)/shard_map/ppermute | solution.py:212
  5.1 31.4 %collective-permute-start.1 = (f32[128,2048]{1,0:T(8,128)}, f32[128,2048]{1,0:T(8,128)S(1)}, u32[]{:S(2)}, u32[]{:S(2)}) collective-permute-start(f32[128,2048]{1,0:T(8,128)} %get-tuple-element.40), channel_id=1, source_target_pairs={{0,96},{32,0},{64,32},{96,64},{1,97},{33,1},{65,33},{97,65},{2,98}... | collective-permute-start | bytes 3145736 | tf_op jit(solution)/shard_map/ppermute | solution.py:213
  10.7 25.7 %all-to-all-start = ((f32[16,136,128]{2,1,0:T(8,128)}), f32[16,136,128]{2,1,0:T(8,128)S(1)}, u32[]{:S(2)}, u32[]{:S(2)}) async-start(f32[16,136,128]{2,1,0:T(8,128)} %trailing.1), calls=%async_computation | async-start | bytes 2228224 | tf_op jit(solution)/shard_map/all_to_all | solution.py:232
  18.7 34.8 %collective-permute-start.2 = (f32[128,2048]{1,0:T(8,128)}, f32[128,2048]{1,0:T(8,128)}, u32[]{:S(2)}, u32[]{:S(2)}) collective-permute-start(f32[128,2048]{1,0:T(8,128)} %get-tuple-element.40), channel_id=1, source_target_pairs={{0,32},{32,64},{64,96},{96,0},{1,33},{33,65},{65,97},{97,1},{2,34}... | collective-permute-start | bytes 3145736 | tf_op jit(solution)/shard_map/ppermute | solution.py:234
  19.1 34.8 %collective-permute-start.3 = (f32[128,2048]{1,0:T(8,128)}, f32[128,2048]{1,0:T(8,128)}, u32[]{:S(2)}, u32[]{:S(2)}) collective-permute-start(f32[128,2048]{1,0:T(8,128)} %get-tuple-element.39), channel_id=1, source_target_pairs={{0,96},{32,0},{64,32},{96,64},{1,97},{33,1},{65,33},{97,65},{2,98}... | collective-permute-start | bytes 3145736 | tf_op jit(solution)/shard_map/ppermute | solution.py:235
  36.4 1.0 copy-start.10
  36.4 2.0 %copy-start.11 = (f32[128,2048]{1,0:T(8,128)}, f32[128,2048]{1,0:T(8,128)S(1)}, u32[]{:S(2)}) copy-start(f32[128,2048]{1,0:T(8,128)S(1)} %collective-permute-done.1.rest_3_) | copy-start | bytes 3145732
  37.5 1.0 copy-start.5
  38.5 23.4 %copy-start = (bf16[1,256,2048]{2,1,0:T(8,128)(2,1)S(1)}, bf16[1,256,2048]{2,1,0:T(8,128)(2,1)}, u32[]{:S(2)}) copy-start(bf16[1,256,2048]{2,1,0:T(8,128)(2,1)} %param.7) | copy-start | bytes 3145732
  38.5 23.4 %copy-start.1 = (bf16[1,256,2048]{2,1,0:T(8,128)(2,1)S(1)}, bf16[1,256,2048]{2,1,0:T(8,128)(2,1)}, u32[]{:S(2)}) copy-start(bf16[1,256,2048]{2,1,0:T(8,128)(2,1)} %param.8) | copy-start | bytes 3145732
  38.5 23.4 %copy-start.7 = (s32[1,2]{1,0:T(1,128)S(1)}, s32[1,2]{1,0:T(1,128)}, u32[]{:S(2)}) copy-start(s32[1,2]{1,0:T(1,128)} %docs.7) | copy-start | bytes 28
  38.5 18.9 %all-to-all-start.1 = ((f32[16,128,128]{2,1,0:T(8,128)}), f32[16,128,128]{2,1,0:T(8,128)S(1)}, u32[]{:S(2)}, u32[]{:S(2)}) async-start(f32[16,128,128]{2,1,0:T(8,128)} %copy-done.5), calls=%async_computation.1 | async-start | bytes 2097152 | tf_op jit(solution)/shard_map/all_to_all | solution.py:265
  42.3 32.6 %collective-permute-start.4 = (f32[128,2048]{1,0:T(8,128)}, f32[128,2048]{1,0:T(8,128)}, u32[]{:S(2)}, u32[]{:S(2)}) collective-permute-start(f32[128,2048]{1,0:T(8,128)} %copy-done.10), channel_id=1, source_target_pairs={{0,32},{32,64},{64,96},{96,0},{1,33},{33,65},{65,97},{97,1},{2,34}... | collective-permute-start | bytes 3145736 | tf_op jit(solution)/shard_map/ppermute | solution.py:263
  42.6 32.3 %collective-permute-start.5 = (f32[128,2048]{1,0:T(8,128)}, f32[128,2048]{1,0:T(8,128)}, u32[]{:S(2)}, u32[]{:S(2)}) collective-permute-start(f32[128,2048]{1,0:T(8,128)} %copy-done.11), channel_id=1, source_target_pairs={{0,96},{32,0},{64,32},{96,64},{1,97},{33,1},{65,33},{97,65},{2,98}... | collective-permute-start | bytes 3145736 | tf_op jit(solution)/shard_map/ppermute | solution.py:264
  57.4 22.5 %all-to-all-start.2 = ((f32[16,136,128]{2,1,0:T(8,128)}), f32[16,136,128]{2,1,0:T(8,128)}, u32[]{:S(2)}, u32[]{:S(2)}) async-start(f32[16,136,128]{2,1,0:T(8,128)} %get-tuple-element.52), calls=%async_computation.2 | async-start | bytes 2228224 | tf_op jit(solution)/shard_map/all_to_all | solution.py:267
  61.9 1.2 copy-start.2
  68.4 1.0 copy-start.8
  69.4 0.7 copy-start.9
  74.9 20.7 %collective-permute-start.6 = (f32[512,256]{1,0:T(8,128)}, f32[512,256]{1,0:T(8,128)}, u32[]{:S(2)}, u32[]{:S(2)}) collective-permute-start(f32[512,256]{1,0:T(8,128)} %get-tuple-element.60), channel_id=1, source_target_pairs={{0,32},{32,64},{64,96},{96,0},{1,33},{33,65},{65,97},{97,1},{2,34}... | collective-permute-start | bytes 1572872 | tf_op jit(solution)/shard_map/ppermute | solution.py:292
  76.5 23.4 %collective-permute-start.7 = (f32[512,256]{1,0:T(8,128)}, f32[512,256]{1,0:T(8,128)}, u32[]{:S(2)}, u32[]{:S(2)}) collective-permute-start(f32[512,256]{1,0:T(8,128)} %get-tuple-element.61), channel_id=1, source_target_pairs={{0,96},{32,0},{64,32},{96,64},{1,97},{33,1},{65,33},{97,65},{2,98}... | collective-permute-start | bytes 1572872 | tf_op jit(solution)/shard_map/ppermute | solution.py:293
  78.2 23.3 %collective-permute-start.8 = (f32[512,256]{1,0:T(8,128)}, f32[512,256]{1,0:T(8,128)}, u32[]{:S(2)}, u32[]{:S(2)}) collective-permute-start(f32[512,256]{1,0:T(8,128)} %get-tuple-element.62), channel_id=1, source_target_pairs={{0,64},{32,96},{64,0},{96,32},{1,65},{33,97},{65,1},{97,33},{2,66}... | collective-permute-start | bytes 1572872 | tf_op jit(solution)/shard_map/ppermute | solution.py:291
  81.2 1.0 copy-start.4
  82.2 24.7 %all-to-all-start.3 = ((f32[16,128,128]{2,1,0:T(8,128)}), f32[16,128,128]{2,1,0:T(8,128)}, u32[]{:S(2)}, u32[]{:S(2)}) async-start(f32[16,128,128]{2,1,0:T(8,128)} %copy-done.4), calls=%async_computation.3 | async-start | bytes 2097152 | tf_op jit(solution)/shard_map/all_to_all | solution.py:302
  106.9 5.4 %collective-permute-start.9 = (f32[16,256,128]{2,1,0:T(8,128)}, f32[16,256,128]{2,1,0:T(8,128)}, u32[]{:S(2)}, u32[]{:S(2)}) collective-permute-start(f32[16,256,128]{2,1,0:T(8,128)} %product.3), channel_id=1, source_target_pairs={{0,16},{16,0},{1,17},{17,1},{2,18},{18,2},{3,19},{19,3},{4,20},{20... | collective-permute-start | bytes 6291464 | tf_op jit(solution)/shard_map/ppermute | solution.py:307
  116.2 38.5 %all-to-all-start.4 = ((f32[16,256,128]{2,1,0:T(8,128)}), f32[16,256,128]{2,1,0:T(8,128)}, u32[]{:S(2)}, u32[]{:S(2)}) async-start(f32[16,256,128]{2,1,0:T(8,128)} %add_multiply_fusion), calls=%async_computation.4 | async-start | bytes 4194304 | tf_op jit(solution)/shard_map/all_to_all | solution.py:308
  124.0 7.2 %copy-start.3 = (bf16[1,256,2048]{2,1,0:T(8,128)(2,1)S(1)}, bf16[1,256,2048]{2,1,0:T(8,128)(2,1)}, u32[]{:S(2)}) copy-start(bf16[1,256,2048]{2,1,0:T(8,128)(2,1)} %param.6) | copy-start | bytes 3145732
  124.0 7.2 %copy-start.6 = (bf16[256,2048]{1,0:T(8,128)(2,1)S(1)}, bf16[256,2048]{1,0:T(8,128)(2,1)}, u32[]{:S(2)}) copy-start(bf16[256,2048]{1,0:T(8,128)(2,1)} %get-tuple-element.45.g) | copy-start | bytes 3145732

commit v6 on v4

--- a/solution.py
+++ b/solution.py
@@ -291,6 +291,7 @@
     far = lax.ppermute(far, "y", ring(2))
     up = lax.ppermute(up, "y", ring(1))
     down = lax.ppermute(down, "y", ring(-1))
+    far_top, rev_scan = lax.optimization_barrier((far_top, rev_scan))
     gathered = pack(
         go, (low_top, low_bottom, high_top, high_bottom, far_top, far_bottom)
     )
@@ -298,7 +299,6 @@
     layer_out = jnp.dot(attended, weight, preferred_element_type=F32).astype(BF16)
 
     core = lax.axis_index("core")
-    gathered, rev_scan = lax.optimization_barrier((gathered, rev_scan))
     rev = lax.all_to_all(rev_scan, ctx, 0, 0, tiled=True)
     atts = (att_own, up, down, far)
     given = product(atts, gathered, 1 - core)

time: 159 us -> 157 us (0.987)
  starting transfers between devices: 42.1 us -> 46.7 us
  local copies, waits for them, and re-layouts: 15.2 us -> 11 us
  waiting for transfers between devices: 43 us -> 40.2 us
    ppermute x1, waiting for transfers between devices: 8.29 us -> 0.51 us  [body(): high_top = lax.ppermute(top, 'y', ring(-1))]
    ppermute x1, waiting for transfers between devices: 0.01 us -> 7.77 us  [body(): low_bottom = lax.ppermute(bottom, 'y', ring(1))]
    all_to_all x1, waiting for transfers between devices: 6.41 us -> 0.01 us  [body(): rev = lax.all_to_all(rev_scan, ctx, 0, 0, tiled=True)]
    unnamed x34 -> x32, local copies, waits for them, and re-layouts: 15.2 us -> 11 us
    all_to_all x1, starting transfers between devices: 4.44 us -> 7.84 us  [body(): spread = lax.all_to_all((kept + taken) * factor, ctx, 0, 0, tiled=True)]
    all_to_all x1, waiting for transfers between devices: 11.6 us -> 14.4 us  [body(): spread = lax.all_to_all((kept + taken) * factor, ctx, 0, 0, tiled=True)]
    ppermute x1, waiting for transfers between devices: 0.77 us -> 2.83 us  [body(): down = lax.ppermute(down, 'y', ring(-1))]
where the time goes in v6:
time: 157 us; the launch traced here: 155 us
  starting transfers between devices  46.7 us (30%)
  Pallas kernels  41.1 us (26%)
  waiting for transfers between devices  40.2 us (26%)
  local copies, waits for them, and re-layouts  11 us (7%)
  other arithmetic  8.35 us (5%)
  matrix products  7.14 us (5%)
    all_to_all x1, waiting for transfers between devices, body(): spread = lax.all_to_all((kept + taken) * factor, ctx, 0, 0, tiled=True)  14.4 us
    unnamed x32, local copies, waits for them, and re-layouts  11 us
    pallas_call x1, Pallas kernels, body(): pl.pallas_call(leading_kernel, grid=(HEADS // per,), in_specs=[SMEM, whol...  10.4 us
    pallas_call x1, Pallas kernels, body(): pl.pallas_call(grads_kernel, grid=(HEADS // per,), in_specs=[SMEM, block,...  9.05 us
    all_to_all x1, starting transfers between devices, body(): by_head = lax.all_to_all(trailing, ctx, 0, 0, tiled=True)  7.96 us
    all_to_all x1, starting transfers between devices, body(): rev = lax.all_to_all(rev_scan, ctx, 0, 0, tiled=True)  7.93 us
    all_to_all x1, starting transfers between devices, body(): spread = lax.all_to_all((kept + taken) * factor, ctx, 0, 0, tiled=True)  7.84 us
    ppermute x1, waiting for transfers between devices, body(): low_bottom = lax.ppermute(bottom, 'y', ring(1))  7.77 us
  transfers between devices with their start and end apart: 15, of which 8 were waited for; matrix products, arithmetic and copies ran while one was open for 5% of the time, Pallas kernels for 26%

profile of v6, /device:TPU:0, one launch (start us, length us, event | category | flops | bytes accessed | tf_op | source)
XLA Modules:
  0.0 155.4 jit_solution(17068624351531007824)
XLA Ops:
  0.6 2.8 %bitcast_convert_fusion = (f32[128,2048]{1,0:T(8,128)}, f32[128,2048]{1,0:T(8,128)}) fusion(bf16[1,256,2048]{2,1,0:T(8,128)(2,1)} %param.10), kind=kLoop, calls=%fused_computation.3 | loop fusion | flops 524288 | bytes 3145728 | tf_op jit(solution)/shard_map/convert_element_type | solution.py:210
  3.4 1.7 %collective-permute-start = (f32[128,2048]{1,0:T(8,128)}, f32[128,2048]{1,0:T(8,128)S(1)}, u32[]{:S(2)}, u32[]{:S(2)}) collective-permute-start(f32[128,2048]{1,0:T(8,128)} %get-tuple-element.39), channel_id=1, source_target_pairs={{0,32},{32,64},{64,96},{96,0},{1,33},{33,65},{65,97},{97,1},{2,34}... | collective-permute-start | bytes 3145736 | tf_op jit(solution)/shard_map/ppermute | solution.py:212
  5.1 1.6 %collective-permute-start.1 = (f32[128,2048]{1,0:T(8,128)}, f32[128,2048]{1,0:T(8,128)S(1)}, u32[]{:S(2)}, u32[]{:S(2)}) collective-permute-start(f32[128,2048]{1,0:T(8,128)} %get-tuple-element.40), channel_id=1, source_target_pairs={{0,96},{32,0},{64,32},{96,64},{1,97},{33,1},{65,33},{97,65},{2,98}... | collective-permute-start | bytes 3145736 | tf_op jit(solution)/shard_map/ppermute | solution.py:213
  6.6 4.1 %trailing.1 = f32[16,136,128]{2,1,0:T(8,128)} custom-call(s32[1,2]{1,0:T(1,128)} %docs.7, bf16[256,2048]{1,0:T(8,128)(2,1)} %bitcast.20, bf16[256,2048]{1,0:T(8,128)(2,1)} %bitcast.23), custom_call_target="tpu_custom_call" | custom-call | flops 1342177 | bytes 31457 | tf_op jit(solution)/shard_map/trailing/pallas_call | solution.py:222
  10.7 8.0 %all-to-all-start = ((f32[16,136,128]{2,1,0:T(8,128)}), f32[16,136,128]{2,1,0:T(8,128)S(1)}, u32[]{:S(2)}, u32[]{:S(2)}) async-start(f32[16,136,128]{2,1,0:T(8,128)} %trailing.1), calls=%async_computation | async-start | bytes 2228224 | tf_op jit(solution)/shard_map/all_to_all | solution.py:232
  18.7 0.4 collective-permute-start.2
  19.1 2.9 %collective-permute-start.3 = (f32[128,2048]{1,0:T(8,128)}, f32[128,2048]{1,0:T(8,128)}, u32[]{:S(2)}, u32[]{:S(2)}) collective-permute-start(f32[128,2048]{1,0:T(8,128)} %get-tuple-element.39), channel_id=1, source_target_pairs={{0,96},{32,0},{64,32},{96,64},{1,97},{33,1},{65,33},{97,65},{2,98}... | collective-permute-start | bytes 3145736 | tf_op jit(solution)/shard_map/ppermute | solution.py:235
  22.0 10.4 %leading.1 = (bf16[256,2048]{1,0:T(8,128)(2,1)}, f32[16,136,128]{2,1,0:T(8,128)}) custom-call(s32[1,2]{1,0:T(1,128)} %docs.7, bf16[256,2048]{1,0:T(8,128)(2,1)} %bitcast.29, bf16[2048,2048]{1,0:T(8,128)(2,1)} %weight.1, bf16[256,2048]{1,0:T(8,128)(2,1)} %bitcast.26), custom_call_target="tpu_custom_call" | custom-call | flops 21474836 | bytes 125829 | tf_op jit(solution)/shard_map/leading/pallas_call | solution.py:237
  32.4 4.1 %all-to-all-done.part = f32[16,136,128]{2,1,0:T(8,128)S(1)} async-done(((f32[16,136,128]{2,1,0:T(8,128)}), f32[16,136,128]{2,1,0:T(8,128)S(1)}, u32[]{:S(2)}, u32[]{:S(2)}) %all-to-all-start) | async-done | bytes 1114144 | tf_op jit(solution)/shard_map/all_to_all | solution.py:232
  36.4 0.0 collective-permute-done.rest_0_
  36.4 0.0 collective-permute-done.1.rest_3_
  36.5 0.0 copy-start.12
  36.5 1.0 copy-done.10
  37.4 0.1 scan.2
  37.5 0.0 copy-start.6
  37.6 1.0 copy-done.6
  38.5 0.0 copy-done.12
  38.5 3.8 %all-to-all-start.1 = ((f32[16,128,128]{2,1,0:T(8,128)}), f32[16,128,128]{2,1,0:T(8,128)S(1)}, u32[]{:S(2)}, u32[]{:S(2)}) async-start(f32[16,128,128]{2,1,0:T(8,128)} %copy-done.6), calls=%async_computation.1 | async-start | bytes 2097152 | tf_op jit(solution)/shard_map/all_to_all | solution.py:265
  42.3 0.3 collective-permute-start.4
  42.7 3.0 %collective-permute-start.5 = (f32[128,2048]{1,0:T(8,128)}, f32[128,2048]{1,0:T(8,128)}, u32[]{:S(2)}, u32[]{:S(2)}) collective-permute-start(f32[128,2048]{1,0:T(8,128)} %copy-done.12), channel_id=1, source_target_pairs={{0,96},{32,0},{64,32},{96,64},{1,97},{33,1},{65,33},{97,65},{2,98}... | collective-permute-start | bytes 3145736 | tf_op jit(solution)/shard_map/ppermute | solution.py:264
  45.6 7.8 %collective-permute-done.2.rest_1_ = f32[128,2048]{1,0:T(8,128)} collective-permute-done((f32[128,2048]{1,0:T(8,128)}, f32[128,2048]{1,0:T(8,128)}, u32[]{:S(2)}, u32[]{:S(2)}) %collective-permute-start.2) | collective-permute-done | bytes 1048608 | tf_op jit(solution)/shard_map/ppermute | solution.py:234
  53.4 0.5 collective-permute-done.3.rest_2_
  53.9 3.5 %all-to-all-done.1.state = f32[16,128,128]{2,1,0:T(8,128)S(1)} async-done(((f32[16,128,128]{2,1,0:T(8,128)}), f32[16,128,128]{2,1,0:T(8,128)S(1)}, u32[]{:S(2)}, u32[]{:S(2)}) %all-to-all-start.1) | async-done | bytes 1048608 | tf_op jit(solution)/shard_map/all_to_all | solution.py:265
  57.4 4.4 %all-to-all-start.2 = ((f32[16,136,128]{2,1,0:T(8,128)}), f32[16,136,128]{2,1,0:T(8,128)}, u32[]{:S(2)}, u32[]{:S(2)}) async-start(f32[16,136,128]{2,1,0:T(8,128)} %get-tuple-element.52), calls=%async_computation.2 | async-start | bytes 2228224 | tf_op jit(solution)/shard_map/all_to_all | solution.py:267
  61.9 0.0 copy-done
  61.9 0.0 copy-done.1
  61.9 0.0 copy-done.14
  61.9 0.0 copy-start.2
  61.9 1.2 copy-done.2
  63.1 5.3 %attended.1 = (bf16[256,2048]{1,0:T(8,128)(2,1)S(1)}, f32[512,256]{1,0:T(8,128)}, f32[512,256]{1,0:T(8,128)}, bf16[512,256]{1,0:T(8,128)(2,1)S(1)}, f32[512,256]{1,0:T(8,128)}) custom-call(s32[1]{0:T(128)} %bitcast.place, s32[1,2]{1,0:T(1,128)S(1)} %copy-done.14, bf16[256,2048]{1,0:T(8,128)(2,1)S(1)} %bitcast.27, bf16[256,2048]{1,0:T(8,128)(2,1)S(1)} %bitcast.21, ...), custom_call_target="tpu_custom_call" | custom-call | flops 5368709 | bytes 73400 | tf_op jit(solution)/shard_map/attended/pallas_call | solution.py:275
  68.5 1.0 copy-done.15
  69.4 5.5 %collective-permute-done.4.rest_4_ = f32[128,2048]{1,0:T(8,128)} collective-permute-done((f32[128,2048]{1,0:T(8,128)}, f32[128,2048]{1,0:T(8,128)}, u32[]{:S(2)}, u32[]{:S(2)}) %collective-permute-start.4) | collective-permute-done | bytes 1048608 | tf_op jit(solution)/shard_map/ppermute | solution.py:263
  74.9 0.0 collective-permute-done.5.rest_5_
  74.9 1.6 %collective-permute-start.6 = (f32[512,256]{1,0:T(8,128)}, f32[512,256]{1,0:T(8,128)}, u32[]{:S(2)}, u32[]{:S(2)}) collective-permute-start(f32[512,256]{1,0:T(8,128)} %get-tuple-element.60), channel_id=1, source_target_pairs={{0,32},{32,64},{64,96},{96,0},{1,33},{33,65},{65,97},{97,1},{2,34}... | collective-permute-start | bytes 1572872 | tf_op jit(solution)/shard_map/ppermute | solution.py:292
  76.5 1.7 %collective-permute-start.7 = (f32[512,256]{1,0:T(8,128)}, f32[512,256]{1,0:T(8,128)}, u32[]{:S(2)}, u32[]{:S(2)}) collective-permute-start(f32[512,256]{1,0:T(8,128)} %get-tuple-element.61), channel_id=1, source_target_pairs={{0,96},{32,0},{64,32},{96,64},{1,97},{33,1},{65,33},{97,65},{2,98}... | collective-permute-start | bytes 1572872 | tf_op jit(solution)/shard_map/ppermute | solution.py:293
  78.2 1.7 %collective-permute-start.8 = (f32[512,256]{1,0:T(8,128)}, f32[512,256]{1,0:T(8,128)}, u32[]{:S(2)}, u32[]{:S(2)}) collective-permute-start(f32[512,256]{1,0:T(8,128)} %get-tuple-element.62), channel_id=1, source_target_pairs={{0,64},{32,96},{64,0},{96,32},{1,65},{33,97},{65,1},{97,33},{2,66}... | collective-permute-start | bytes 1572872 | tf_op jit(solution)/shard_map/ppermute | solution.py:291
  79.9 0.0 all-to-all-done.2.part
  79.9 1.4 scan.3
  81.2 0.0 copy-start.5
  81.2 1.0 copy-done.5
  82.2 7.9 %all-to-all-start.3 = ((f32[16,128,128]{2,1,0:T(8,128)}), f32[16,128,128]{2,1,0:T(8,128)}, u32[]{:S(2)}, u32[]{:S(2)}) async-start(f32[16,128,128]{2,1,0:T(8,128)} %copy-done.5), calls=%async_computation.3 | async-start | bytes 2097152 | tf_op jit(solution)/shard_map/all_to_all | solution.py:302
  90.1 0.0 copy-start.4
  90.1 1.2 copy-done.4
  91.4 1.2 copy-done.11
  92.6 1.2 copy-done.13
  93.8 3.3 %pack.1.gathered = bf16[1024,2048]{1,0:T(8,128)(2,1)S(1)} custom-call(bf16[256,2048]{1,0:T(8,128)(2,1)S(1)} %bitcast.30, f32[128,2048]{1,0:T(8,128)S(1)} %copy-done.11, f32[128,2048]{1,0:T(8,128)} %collective-permute-done.2.rest_1_, f32[128,2048]{1,0:T(8,128)} %collective-permute-done.3.rest_2_, f32[128,2048]{1,0:T(8,128)S(1)} %copy-done.13, ...), custom_call_target="tpu_custom_call" | custom-call | flops 10485 | bytes 125829 | tf_op jit(solution)/shard_map/pack/pallas_call | solution.py:154
  97.1 0.0 copy-start.7
  97.1 0.0 collective-permute-done.6.att_low
  97.1 2.8 %collective-permute-done.7.att_high = f32[512,256]{1,0:T(8,128)} collective-permute-done((f32[512,256]{1,0:T(8,128)}, f32[512,256]{1,0:T(8,128)}, u32[]{:S(2)}, u32[]{:S(2)}) %collective-permute-start.7) | collective-permute-done | bytes 524320 | tf_op jit(solution)/shard_map/ppermute | solution.py:293
  99.9 1.6 %collective-permute-done.8.att_far = f32[512,256]{1,0:T(8,128)} collective-permute-done((f32[512,256]{1,0:T(8,128)}, f32[512,256]{1,0:T(8,128)}, u32[]{:S(2)}, u32[]{:S(2)}) %collective-permute-start.8) | collective-permute-done | bytes 524320 | tf_op jit(solution)/shard_map/ppermute | solution.py:291
  101.5 4.3 %product.3 = f32[16,256,128]{2,1,0:T(8,128)} custom-call(s32[1]{0:T(128)} %bitcast.12.side, bf16[512,256]{1,0:T(8,128)(2,1)S(1)} %get-tuple-element.59.att_own, f32[512,256]{1,0:T(8,128)} %collective-permute-done.6.att_low, f32[512,256]{1,0:T(8,128)} %collective-permute-done.7.att_high, f32[512,256]{1,0:T(8,128)} %collective-permute-done.8.att_far, ...), custom_call_target="tpu_custom_call" | custom-call | flops 16106127360 | bytes 1 | tf_op jit(solution)/shard_map/product/pallas_call | solution.py:190
  105.8 0.0 collective-permute-start.9
  105.8 0.0 all-to-all-done.3.rev
  105.8 2.2 %copy-done.8 = bf16[1024,2048]{1,0:T(8,128)(2,1)S(1)} copy-done((bf16[1024,2048]{1,0:T(8,128)(2,1)S(1)}, bf16[1024,2048]{1,0:T(8,128)(2,1)}, u32[]{:S(2)}) %copy-start.8) | copy-done | bytes 4194328
  108.0 3.3 %product.2 = f32[16,256,128]{2,1,0:T(8,128)S(1)} custom-call(s32[1]{0:T(128)} %bitcast.11.side, bf16[512,256]{1,0:T(8,128)(2,1)S(1)} %get-tuple-element.59.att_own, f32[512,256]{1,0:T(8,128)} %collective-permute-done.6.att_low, f32[512,256]{1,0:T(8,128)} %collective-permute-done.7.att_high, f32[512,256]{1,0:T(8,128)} %collective-permute-done.8.att_far, ...), custom_call_target="tpu_custom_call" | custom-call | flops 16106127360 | bytes 1 | tf_op jit(solution)/shard_map/product/pallas_call | solution.py:190
  111.3 0.0 collective-permute-done.9
  111.3 3.2 %add_multiply_fusion = f32[16,256,128]{2,1,0:T(8,128)} fusion(f32[16,256,128]{2,1,0:T(8,128)S(1)} %product.2, f32[16,256,128]{2,1,0:T(8,128)} %collective-permute-done.9), kind=kLoop, calls=%fused_computation.2 | loop fusion | flops 1048576 | bytes 6291456 | tf_op jit(solution)/shard_map/mul | solution.py:308
  114.5 7.8 %all-to-all-start.4 = ((f32[16,256,128]{2,1,0:T(8,128)}), f32[16,256,128]{2,1,0:T(8,128)}, u32[]{:S(2)}, u32[]{:S(2)}) async-start(f32[16,256,128]{2,1,0:T(8,128)} %add_multiply_fusion), calls=%async_computation.4 | async-start | bytes 4194304 | tf_op jit(solution)/shard_map/all_to_all | solution.py:308
  122.4 0.0 copy-start.3
  122.4 0.0 copy-start.9
  122.4 7.1 %fusion = bf16[1,256,2048]{2,1,0:T(8,128)(2,1)} fusion(bf16[256,2048]{1,0:T(8,128)(2,1)} %copy-done.15, bf16[2048,2048]{1,0:T(8,128)(2,1)} %weight.1), kind=kOutput, calls=%fused_computation.1 | convolution fusion | flops 2148007936 | bytes 10485760 | tf_op jit(solution)/shard_map/dot_general | solution.py:299
  129.5 9.0 %grads.1 = (bf16[256,2048]{1,0:T(8,128)(2,1)}, bf16[256,2048]{1,0:T(8,128)(2,1)}, bf16[256,2048]{1,0:T(8,128)(2,1)}) custom-call(s32[1,2]{1,0:T(1,128)S(1)} %copy-done.14, bf16[256,2048]{1,0:T(8,128)(2,1)S(1)} %bitcast.28, bf16[256,2048]{1,0:T(8,128)(2,1)S(1)} %bitcast.22, bf16[256,2048]{1,0:T(8,128)(2,1)S(1)} %bitcast.25, bf16[256,2048]{1,0:T(8,128)(2,1)S(1)} %copy-done.9, ...), custom_call_target="tpu_custom_call" | custom-call | flops 13421772 | bytes 94371 | tf_op jit(solution)/shard_map/grads/pallas_call | solution.py:311
  138.6 14.4 %all-to-all-done.4 = f32[16,256,128]{2,1,0:T(8,128)} async-done(((f32[16,256,128]{2,1,0:T(8,128)}), f32[16,256,128]{2,1,0:T(8,128)}, u32[]{:S(2)}, u32[]{:S(2)}) %all-to-all-start.4) | async-done | bytes 2097184 | tf_op jit(solution)/shard_map/all_to_all | solution.py:308
  153.0 2.4 %reduce_sum.9 = f32[256,128]{1,0:T(8,128)} reduce(f32[16,256,128]{2,1,0:T(8,128)} %all-to-all-done.4, f32[]{:T(128)} %constant.17.clone.1), dimensions={0}, to_apply=%region_0.0 | reduce | flops 491520 | bytes 2228228 | tf_op jit(solution)/shard_map/reduce_sum | solution.py:309
  (11 shorter events, 0.0 us)
Async XLA Ops:
  3.4 33.1 %collective-permute-start = (f32[128,2048]{1,0:T(8,128)}, f32[128,2048]{1,0:T(8,128)S(1)}, u32[]{:S(2)}, u32[]{:S(2)}) collective-permute-start(f32[128,2048]{1,0:T(8,128)} %get-tuple-element.39), channel_id=1, source_target_pairs={{0,32},{32,64},{64,96},{96,0},{1,33},{33,65},{65,97},{97,1},{2,34}... | collective-permute-start | bytes 3145736 | tf_op jit(solution)/shard_map/ppermute | solution.py:212
  5.1 31.4 %collective-permute-start.1 = (f32[128,2048]{1,0:T(8,128)}, f32[128,2048]{1,0:T(8,128)S(1)}, u32[]{:S(2)}, u32[]{:S(2)}) collective-permute-start(f32[128,2048]{1,0:T(8,128)} %get-tuple-element.40), channel_id=1, source_target_pairs={{0,96},{32,0},{64,32},{96,64},{1,97},{33,1},{65,33},{97,65},{2,98}... | collective-permute-start | bytes 3145736 | tf_op jit(solution)/shard_map/ppermute | solution.py:213
  10.7 25.7 %all-to-all-start = ((f32[16,136,128]{2,1,0:T(8,128)}), f32[16,136,128]{2,1,0:T(8,128)S(1)}, u32[]{:S(2)}, u32[]{:S(2)}) async-start(f32[16,136,128]{2,1,0:T(8,128)} %trailing.1), calls=%async_computation | async-start | bytes 2228224 | tf_op jit(solution)/shard_map/all_to_all | solution.py:232
  18.7 34.7 %collective-permute-start.2 = (f32[128,2048]{1,0:T(8,128)}, f32[128,2048]{1,0:T(8,128)}, u32[]{:S(2)}, u32[]{:S(2)}) collective-permute-start(f32[128,2048]{1,0:T(8,128)} %get-tuple-element.40), channel_id=1, source_target_pairs={{0,32},{32,64},{64,96},{96,0},{1,33},{33,65},{65,97},{97,1},{2,34}... | collective-permute-start | bytes 3145736 | tf_op jit(solution)/shard_map/ppermute | solution.py:234
  19.1 34.8 %collective-permute-start.3 = (f32[128,2048]{1,0:T(8,128)}, f32[128,2048]{1,0:T(8,128)}, u32[]{:S(2)}, u32[]{:S(2)}) collective-permute-start(f32[128,2048]{1,0:T(8,128)} %get-tuple-element.39), channel_id=1, source_target_pairs={{0,96},{32,0},{64,32},{96,64},{1,97},{33,1},{65,33},{97,65},{2,98}... | collective-permute-start | bytes 3145736 | tf_op jit(solution)/shard_map/ppermute | solution.py:235
  36.4 1.0 copy-start.10
  36.5 2.1 %copy-start.12 = (f32[128,2048]{1,0:T(8,128)}, f32[128,2048]{1,0:T(8,128)S(1)}, u32[]{:S(2)}) copy-start(f32[128,2048]{1,0:T(8,128)S(1)} %collective-permute-done.1.rest_3_) | copy-start | bytes 3145732
  37.5 1.0 copy-start.6
  38.5 23.3 %copy-start = (bf16[1,256,2048]{2,1,0:T(8,128)(2,1)S(1)}, bf16[1,256,2048]{2,1,0:T(8,128)(2,1)}, u32[]{:S(2)}) copy-start(bf16[1,256,2048]{2,1,0:T(8,128)(2,1)} %param.7) | copy-start | bytes 3145732
  38.5 23.4 %copy-start.1 = (bf16[1,256,2048]{2,1,0:T(8,128)(2,1)S(1)}, bf16[1,256,2048]{2,1,0:T(8,128)(2,1)}, u32[]{:S(2)}) copy-start(bf16[1,256,2048]{2,1,0:T(8,128)(2,1)} %param.8) | copy-start | bytes 3145732
  38.5 23.4 %copy-start.14 = (s32[1,2]{1,0:T(1,128)S(1)}, s32[1,2]{1,0:T(1,128)}, u32[]{:S(2)}) copy-start(s32[1,2]{1,0:T(1,128)} %docs.7) | copy-start | bytes 28
  38.5 18.9 %all-to-all-start.1 = ((f32[16,128,128]{2,1,0:T(8,128)}), f32[16,128,128]{2,1,0:T(8,128)S(1)}, u32[]{:S(2)}, u32[]{:S(2)}) async-start(f32[16,128,128]{2,1,0:T(8,128)} %copy-done.6), calls=%async_computation.1 | async-start | bytes 2097152 | tf_op jit(solution)/shard_map/all_to_all | solution.py:265
  42.3 32.6 %collective-permute-start.4 = (f32[128,2048]{1,0:T(8,128)}, f32[128,2048]{1,0:T(8,128)}, u32[]{:S(2)}, u32[]{:S(2)}) collective-permute-start(f32[128,2048]{1,0:T(8,128)} %copy-done.10), channel_id=1, source_target_pairs={{0,32},{32,64},{64,96},{96,0},{1,33},{33,65},{65,97},{97,1},{2,34}... | collective-permute-start | bytes 3145736 | tf_op jit(solution)/shard_map/ppermute | solution.py:263
  42.7 32.2 %collective-permute-start.5 = (f32[128,2048]{1,0:T(8,128)}, f32[128,2048]{1,0:T(8,128)}, u32[]{:S(2)}, u32[]{:S(2)}) collective-permute-start(f32[128,2048]{1,0:T(8,128)} %copy-done.12), channel_id=1, source_target_pairs={{0,96},{32,0},{64,32},{96,64},{1,97},{33,1},{65,33},{97,65},{2,98}... | collective-permute-start | bytes 3145736 | tf_op jit(solution)/shard_map/ppermute | solution.py:264
  57.4 22.4 %all-to-all-start.2 = ((f32[16,136,128]{2,1,0:T(8,128)}), f32[16,136,128]{2,1,0:T(8,128)}, u32[]{:S(2)}, u32[]{:S(2)}) async-start(f32[16,136,128]{2,1,0:T(8,128)} %get-tuple-element.52), calls=%async_computation.2 | async-start | bytes 2228224 | tf_op jit(solution)/shard_map/all_to_all | solution.py:267
  61.9 1.2 copy-start.2
  68.5 1.0 copy-start.15
  74.9 22.2 %collective-permute-start.6 = (f32[512,256]{1,0:T(8,128)}, f32[512,256]{1,0:T(8,128)}, u32[]{:S(2)}, u32[]{:S(2)}) collective-permute-start(f32[512,256]{1,0:T(8,128)} %get-tuple-element.60), channel_id=1, source_target_pairs={{0,32},{32,64},{64,96},{96,0},{1,33},{33,65},{65,97},{97,1},{2,34}... | collective-permute-start | bytes 1572872 | tf_op jit(solution)/shard_map/ppermute | solution.py:292
  76.5 23.4 %collective-permute-start.7 = (f32[512,256]{1,0:T(8,128)}, f32[512,256]{1,0:T(8,128)}, u32[]{:S(2)}, u32[]{:S(2)}) collective-permute-start(f32[512,256]{1,0:T(8,128)} %get-tuple-element.61), channel_id=1, source_target_pairs={{0,96},{32,0},{64,32},{96,64},{1,97},{33,1},{65,33},{97,65},{2,98}... | collective-permute-start | bytes 1572872 | tf_op jit(solution)/shard_map/ppermute | solution.py:293
  78.2 23.3 %collective-permute-start.8 = (f32[512,256]{1,0:T(8,128)}, f32[512,256]{1,0:T(8,128)}, u32[]{:S(2)}, u32[]{:S(2)}) collective-permute-start(f32[512,256]{1,0:T(8,128)} %get-tuple-element.62), channel_id=1, source_target_pairs={{0,64},{32,96},{64,0},{96,32},{1,65},{33,97},{65,1},{97,33},{2,66}... | collective-permute-start | bytes 1572872 | tf_op jit(solution)/shard_map/ppermute | solution.py:291
  81.2 1.0 copy-start.5
  82.2 23.6 %all-to-all-start.3 = ((f32[16,128,128]{2,1,0:T(8,128)}), f32[16,128,128]{2,1,0:T(8,128)}, u32[]{:S(2)}, u32[]{:S(2)}) async-start(f32[16,128,128]{2,1,0:T(8,128)} %copy-done.5), calls=%async_computation.3 | async-start | bytes 2097152 | tf_op jit(solution)/shard_map/all_to_all | solution.py:302
  90.1 1.2 copy-start.4
  91.4 1.2 copy-start.11
  92.6 1.2 copy-start.13
  97.1 8.7 %copy-start.7 = (bf16[1024,2048]{1,0:T(8,128)(2,1)}, bf16[1024,2048]{1,0:T(8,128)(2,1)S(1)}, u32[]{:S(2)}) copy-start(bf16[1024,2048]{1,0:T(8,128)(2,1)S(1)} %pack.1.gathered) | copy-start | bytes 12582916
  105.8 5.5 %collective-permute-start.9 = (f32[16,256,128]{2,1,0:T(8,128)}, f32[16,256,128]{2,1,0:T(8,128)}, u32[]{:S(2)}, u32[]{:S(2)}) collective-permute-start(f32[16,256,128]{2,1,0:T(8,128)} %product.3), channel_id=1, source_target_pairs={{0,16},{16,0},{1,17},{17,1},{2,18},{18,2},{3,19},{19,3},{4,20},{20... | collective-permute-start | bytes 6291464 | tf_op jit(solution)/shard_map/ppermute | solution.py:307
  105.8 2.2 %copy-start.8 = (bf16[1024,2048]{1,0:T(8,128)(2,1)S(1)}, bf16[1024,2048]{1,0:T(8,128)(2,1)}, u32[]{:S(2)}) copy-start(bf16[1024,2048]{1,0:T(8,128)(2,1)} %copy-done.7) | copy-start | bytes 12582916
  114.5 38.5 %all-to-all-start.4 = ((f32[16,256,128]{2,1,0:T(8,128)}), f32[16,256,128]{2,1,0:T(8,128)}, u32[]{:S(2)}, u32[]{:S(2)}) async-start(f32[16,256,128]{2,1,0:T(8,128)} %add_multiply_fusion), calls=%async_computation.4 | async-start | bytes 4194304 | tf_op jit(solution)/shard_map/all_to_all | solution.py:308
  122.4 7.2 %copy-start.3 = (bf16[1,256,2048]{2,1,0:T(8,128)(2,1)S(1)}, bf16[1,256,2048]{2,1,0:T(8,128)(2,1)}, u32[]{:S(2)}) copy-start(bf16[1,256,2048]{2,1,0:T(8,128)(2,1)} %param.6) | copy-start | bytes 3145732
  122.4 7.2 %copy-start.9 = (bf16[256,2048]{1,0:T(8,128)(2,1)S(1)}, bf16[256,2048]{1,0:T(8,128)(2,1)}, u32[]{:S(2)}) copy-start(bf16[256,2048]{1,0:T(8,128)(2,1)} %get-tuple-element.45.g) | copy-start | bytes 3145732
